TPU v7x, 32 devices: a whole 2x2x4 slice. The times are simulated.
32 devices in a mesh: groups: 2 (over x), lon: 16 (over z, y, core).
Axes of the slice: x: 2, y: 2, z: 4, core: 2. Of those that a mesh axis runs over, the one named last changes fastest.
Arguments:
- latlon_fields: bfloat16 [32, 32, 2048], P('groups', 'lon'), parts along dimension 0, may hold values from -6 to 6
- remap_table: int32 [2, 32, 2048], P(None, None, 'lon'), may hold values from 0 to 2047, as said below
- kernel_first: bfloat16 [3, 3, 64, 16], replicated, may hold values from -0.5 to 0.5
- kernel_second: bfloat16 [3, 3, 64, 64], replicated, may hold values from -0.25 to 0.25
- kernel_down: bfloat16 [3, 3, 128, 64], replicated, may hold values from -0.25 to 0.25
- kernel_coarse: bfloat16 [3, 3, 128, 128], replicated, may hold values from -0.1875 to 0.1875
- kernel_up: bfloat16 [3, 3, 64, 128], replicated, may hold values from -0.375 to 0.375
- kernel_merge: bfloat16 [3, 3, 64, 128], replicated, may hold values from -0.1875 to 0.1875
- projection: bfloat16 [8, 64], replicated, may hold values from -0.75 to 0.75
Outputs:
- forecast: float32 [16, 32, 2048], P('groups', None, 'lon'), parts along dimension 0
There are 2 independent parts, one for each index of `groups`. A program takes and returns all parts, laid end to end along the dimension named above; an argument that names none is the same for every part. Nothing has to cross between parts.
Inputs may be any that keep to these rules, and one draw needn't show every extreme that they name: remap_table[0] is a lat-lon row below 32; remap_table[1] is a lat-lon column, and for a grid cell in column w it lies in the same block of 128 columns as w, that is between (w // 128) * 128 and (w // 128) * 128 + 127.
All inputs are finite; a program needn't handle non-finite values.
Results may differ from a plain program's by a relative error of at most 0.00084.
Values may be sent and summed in bfloat16 or wider, within the bound.
No kernel may reach another device: no remote copies, remote signals or barrier semaphores. Data moves between devices by JAX's collectives and lax.ppermute only.
A program may use at most 128 MiB of HBM per device.

v0:
```python
import functools

import jax
import jax.numpy as jnp
from jax import lax
from jax.experimental import pallas as pl
from jax.experimental.pallas import tpu as pltpu
from jax.sharding import PartitionSpec as P

F32 = jnp.float32
BF16 = jnp.bfloat16
HALO = 8
FINE_COLUMN = (1, 2, 3, 0)


def from_behind(block, axis, distance):
    devices = range(lax.axis_size(axis))
    route = [((i - distance) % len(devices), i) for i in devices]
    return lax.ppermute(block, axis, route)


def tap(kernel_ref, row, col):
    if 0 <= row < 3 and 0 <= col < 3:
        return kernel_ref[row, col].astype(F32)
    return jnp.zeros(kernel_ref.shape[2:], F32)


def arrange_kernel(first, second, down, coarse, up, merge, projection, w1, w2, wd, wc, wu, wm, wp):
    channels = second.shape[3]
    inputs = first.shape[2]
    for half in range(2):
        for side in range(2):
            for p in range(2):
                for q in range(2):
                    t = 1 + p if half == 0 else (3, 0)[p]
                    u = 1 + q if side == 0 else (3, 0)[q]
                    at = (((half * 2 + side) * 2 + p) * 2 + q) * inputs
                    pieces = [tap(first, t - a, u - b) for a in range(2) for b in range(2)]
                    w1[at : at + inputs, :] = jnp.concatenate(pieces, axis=1).astype(BF16)
    for t in range(4):
        for code, u in enumerate(FINE_COLUMN):
            at = t * 4 * channels + code * channels
            for p in range(2):
                pair = jnp.concatenate([tap(second, t - p, u), tap(second, t - p, u - 1)], axis=0)
                w2[at : at + channels, p * 128 : (p + 1) * 128] = pair.T.astype(BF16)
            for q in range(2):
                pair = jnp.concatenate([tap(merge, t, u - q), tap(merge, t - 1, u - q)], axis=0).T.astype(BF16)
                wm[at : at + channels, q * 128 : (q + 1) * 128] = pair[:channels]
                wm[16 * channels + at : 16 * channels + at + channels, q * 128 : (q + 1) * 128] = pair[channels:]
            if t < 3:
                wd[at : at + channels, :] = tap(down, t, u).T.astype(BF16)
    wide = coarse.shape[3]
    for a in range(3):
        for b in range(3):
            at = (a * 3 + b) * wide
            wc[at : at + wide, :] = tap(coarse, a, b).T.astype(BF16)
    lifts = ((1, 3), (0, 2))
    for di in range(2):
        for dj in range(2):
            at = (di * 2 + dj) * wide
            for p in range(2):
                pair = jnp.concatenate([tap(up, lifts[p][di], lifts[q][dj]) for q in range(2)], axis=0)
                wu[at : at + wide, p * 128 : (p + 1) * 128] = pair.T.astype(BF16)
    rows = projection[...].astype(F32)
    nothing = jnp.zeros_like(rows)
    upper = jnp.concatenate([rows, nothing], axis=1)
    lower = jnp.concatenate([nothing, rows], axis=1)
    wp[...] = jnp.concatenate([upper, lower], axis=0).astype(BF16)


def arrange(first, second, down, coarse, up, merge, projection):
    channels, wide = second.shape[3], coarse.shape[3]
    shapes = (
        (16 * first.shape[3], 4 * channels),
        (16 * channels, 4 * channels),
        (12 * channels, wide),
        (9 * wide, wide),
        (4 * wide, 4 * channels),
        (32 * channels, 4 * channels),
        (2 * projection.shape[0], 2 * channels),
    )
    return pl.pallas_call(
        arrange_kernel,
        out_shape=[jax.ShapeDtypeStruct(s, BF16) for s in shapes],
        compiler_params=pltpu.CompilerParams(vmem_limit_bytes=32 * 2**20),
        name="arrange_weights",
    )(jnp.swapaxes(first, 2, 3), second, down, coarse, up, merge, projection)


def remap_kernel(block, table, cells, to_left, to_right, skip, source, picked):
    devices, depth, columns = block.shape
    channels = depth // 2
    grid_rows = table.shape[1]
    half = columns // 2
    lane = lax.broadcasted_iota(jnp.int32, (8, columns), 1)
    spread = (lane % half) * 2 + lane // half

    def load(s, carry):
        source[pl.ds(pl.multiple_of(s * depth, depth), depth), :] = block[s].astype(F32)
        return carry

    lax.fori_loop(0, devices, load, 0)

    def one_row(h, carry):
        rows = jnp.broadcast_to(table[0, pl.ds(h, 1), :], (8, columns))
        cols = jnp.broadcast_to(table[1, pl.ds(h, 1), :], (8, columns))
        rows = jnp.take_along_axis(rows, spread, axis=1)
        cols = jnp.take_along_axis(cols, spread, axis=1) % columns
        parts = [jnp.zeros((8, columns), F32) for _ in range(channels // 8)]
        for r in range(2 * devices):
            here = rows == r
            for n in range(channels // 8):
                at = r * channels + n * 8
                value = jnp.take_along_axis(source[at : at + 8, :], cols, axis=1)
                parts[n] = jnp.where(here, value, parts[n])
        for n in range(channels // 8):
            picked[pl.ds(pl.multiple_of(h * channels + n * 8, 8), 8), :] = parts[n]
        skip[pl.ds(pl.multiple_of(h * 8, 8), 8), :] = parts[0]
        return carry

    lax.fori_loop(0, grid_rows, one_row, 0)
    for i in range(grid_rows // 2):
        turned = picked[i * 2 * channels : (i + 1) * 2 * channels, :].T
        pieces = []
        for p in range(2):
            for q in range(2):
                pieces.append(turned[q * half : (q + 1) * half, p * channels : (p + 1) * channels])
        paired = jnp.concatenate(pieces + pieces, axis=1)
        cells[i * half : (i + 1) * half, :] = paired.astype(BF16)
        to_left[i * HALO : (i + 1) * HALO, :] = paired[:HALO]
        to_right[i * HALO : (i + 1) * HALO, :] = paired[half - HALO :]


def remap(block, table):
    devices, depth, columns = block.shape
    grid_rows = table.shape[1]
    channels = depth // 2
    half = columns // 2
    lanes = 8 * channels
    return pl.pallas_call(
        remap_kernel,
        out_shape=[
            jax.ShapeDtypeStruct((grid_rows // 2 * half, lanes), BF16),
            jax.ShapeDtypeStruct((grid_rows // 2 * HALO, lanes), F32),
            jax.ShapeDtypeStruct((grid_rows // 2 * HALO, lanes), F32),
            jax.ShapeDtypeStruct((grid_rows * 8, columns), F32),
        ],
        scratch_shapes=[
            pltpu.VMEM((devices * depth, columns), F32),
            pltpu.VMEM((grid_rows * channels, columns), F32),
        ],
        compiler_params=pltpu.CompilerParams(vmem_limit_bytes=16 * 2**20),
        name="remap",
    )(block, table)


def silu(values):
    h = 0.5 * values
    return (h + h * jnp.tanh(h)).astype(BF16).astype(F32)


def neighbours(values):
    count = values.shape[0]
    return pltpu.roll(values, 1, 0), pltpu.roll(values, count - 1, 0)


def network_kernel(cells, left, right, across, skip, w1, w2, wd, wc, wu, wm, wp, out, x0, y0, y1, y2, yc, yo, yu):
    half = cells.shape[0] // (left.shape[0] // HALO)
    blocks = left.shape[0] // HALO
    step = half + 2 * HALO
    polar = across.shape[0] // step
    top = 0
    bottom = blocks + 1
    pole = blocks + 2
    end = pole + polar + 1
    group = 4

    def at(row, count=1):
        return slice(row * step, (row + count) * step)

    def chunks(polar_rows):
        found = [(1 + i, group) for i in range(0, blocks, group)]
        if polar_rows:
            found.append((pole + 1, polar_rows))
        return found

    def lane_mask(rows, width):
        return lax.broadcasted_iota(jnp.int32, (rows, 128), 1) // width % 2 == 0

    x0[...] = jnp.zeros_like(x0)
    for i in range(blocks):
        base = (1 + i) * step
        x0[base : base + HALO, :] = left[i * HALO : (i + 1) * HALO, :]
        x0[base + HALO : base + HALO + half, :] = cells[i * half : (i + 1) * half, :].astype(F32)
        x0[base + HALO + half : base + step, :] = right[i * HALO : (i + 1) * HALO, :]
    x0[at(pole + 1, polar), :] = across[...]
    x0[at(top), :] = pltpu.roll(x0[at(pole + 1), :], 32, 1)
    x0[at(pole), :] = pltpu.roll(x0[at(1), :], 32, 1)
    for row in range(0, end + 1):
        x = x0[at(row), :]
        before, after = neighbours(x)
        side = jnp.where(lane_mask(step, 16), after, before)
        y0[at(row), :] = jnp.where(lane_mask(step, 64), x, side)

    def store_fine(y, row, count, values):
        before, after = neighbours(values)
        mask = lane_mask(count * step, 64)
        for p in range(2):
            lanes = slice(p * 128, (p + 1) * 128)
            y[at(row, count), p * 256 : p * 256 + 128] = values[:, lanes].astype(BF16)
            y[at(row, count), p * 256 + 128 : p * 256 + 256] = jnp.where(
                mask, after[:, lanes], before[:, lanes]
            ).astype(BF16)

    def edges_fine(y, polar_rows):
        y[at(top), 256:512] = y[at(pole + 1), 0:256]
        y[at(pole), 256:512] = y[at(1), 0:256]
        y[at(bottom), 0:256] = jnp.zeros((step, 256), BF16)
        y[at(pole + 1 + polar_rows), 0:256] = jnp.zeros((step, 256), BF16)

    def patch(y, row, count):
        return [
            y[at(row - 1, count), 256:512],
            y[at(row, count), :],
            y[at(row + 1, count), 0:256],
        ]

    def product(pieces, weights):
        return jnp.dot(jnp.concatenate(pieces, axis=1), weights[...], preferred_element_type=F32)

    for row, count in chunks(polar):
        mask = lane_mask(count * step, 32)
        vertical = jnp.where(mask, y0[at(row + 1, count), :], y0[at(row - 1, count), :])
        pieces = [y0[at(row, count), :].astype(BF16), vertical.astype(BF16)]
        store_fine(y1, row, count, silu(product(pieces, w1)))
    edges_fine(y1, polar)

    for row, count in chunks(polar - 1):
        store_fine(y2, row, count, silu(product(patch(y1, row, count), w2)))
    edges_fine(y2, polar - 1)

    for row, count in chunks(polar - 1):
        pieces = [y2[at(row - 1, count), 256:512], y2[at(row, count), :]]
        values = silu(product(pieces, wd))
        before, after = neighbours(values)
        yc[at(row, count), 0:128] = before.astype(BF16)
        yc[at(row, count), 128:256] = values.astype(BF16)
        yc[at(row, count), 256:384] = after.astype(BF16)
    yc[at(top), :] = yc[at(pole + 1), :]
    yc[at(pole), :] = yc[at(1), :]
    yc[at(bottom), :] = jnp.zeros((step, 384), BF16)

    for row, count in chunks(polar - 2):
        pieces = [yc[at(row + a, count), :] for a in (-1, 0, 1)]
        values = silu(product(pieces, wc))
        yo[at(row, count), 0:128] = values.astype(BF16)
        yo[at(row, count), 128:256] = neighbours(values)[1].astype(BF16)
    yo[at(bottom), :] = jnp.zeros((step, 256), BF16)
    yo[at(pole + 2), :] = jnp.zeros((step, 256), BF16)

    for row, count in chunks(polar - 2):
        pieces = [yo[at(row, count), :], yo[at(row + 1, count), :]]
        store_fine(yu, row, count, silu(product(pieces, wu)))
    edges_fine(yu, polar - 2)

    lane = lax.broadcasted_iota(jnp.int32, (2 * 8, 2 * half), 1)
    weave = (lane % 2) * half + lane // 2
    for row, count in chunks(0):
        merged = silu(product(patch(y2, row, count) + patch(yu, row, count), wm))
        columns = []
        for i in range(count):
            own = merged[i * step + HALO : i * step + HALO + half, :]
            columns += [own[:, 0:128], own[:, 128:256]]
        columns = jnp.concatenate(columns, axis=0).astype(BF16)
        update = lax.dot_general(wp[...], columns, (((1,), (1,)), ((), ())), preferred_element_type=F32)
        for i in range(count):
            r = row - 1 + i
            total = update[:, i * 2 * half : (i + 1) * 2 * half] + skip[r * 16 : (r + 1) * 16, :]
            total = jnp.take_along_axis(total, weave, axis=1)
            for p in range(2):
                out[:, 2 * r + p, :] = total[p * 8 : (p + 1) * 8, :]


def network(cells, left, right, across, skip, weights):
    blocks = left.shape[0] // HALO
    half = cells.shape[0] // blocks
    step = half + 2 * HALO
    rows = (blocks + 2 + across.shape[0] // step + 2) * step
    vmem = pltpu.VMEM
    return pl.pallas_call(
        network_kernel,
        out_shape=jax.ShapeDtypeStruct((weights[-1].shape[0] // 2, 2 * blocks, 2 * half), F32),
        scratch_shapes=[
            vmem((rows, 128), F32),
            vmem((rows, 128), F32),
            vmem((rows, 512), BF16),
            vmem((rows, 512), BF16),
            vmem((rows, 384), BF16),
            vmem((rows, 256), BF16),
            vmem((rows, 512), BF16),
        ],
        compiler_params=pltpu.CompilerParams(vmem_limit_bytes=40 * 2**20),
        name="network",
    )(cells, left, right, across, skip, *weights)


def shards(
    latlon_fields,
    remap_table,
    kernel_first,
    kernel_second,
    kernel_down,
    kernel_coarse,
    kernel_up,
    kernel_merge,
    projection,
):
    columns = remap_table.shape[2]
    count = lax.axis_size("lon")
    channels, rows, _ = latlon_fields.shape
    parcels = latlon_fields.reshape(channels, rows, count, columns).transpose(2, 1, 0, 3)
    parcels = parcels.reshape(count, rows * channels, columns)
    block = lax.all_to_all(parcels, "lon", split_axis=0, concat_axis=0, tiled=True)
    weights = arrange(
        kernel_first, kernel_second, kernel_down, kernel_coarse, kernel_up, kernel_merge, projection
    )
    cells, to_left, to_right, skip = remap(block, remap_table)
    left = from_behind(to_right, "lon", 1)
    right = from_behind(to_left, "lon", -1)
    polar = 3
    half = columns // 2
    own = cells[: polar * half].reshape(polar, half, -1).astype(F32)
    edge = jnp.concatenate(
        [left[: polar * HALO].reshape(polar, HALO, -1), own, right[: polar * HALO].reshape(polar, HALO, -1)], axis=1
    )
    across = from_behind(edge.reshape(-1, edge.shape[2]), "lon", count // 2)
    return network(cells, left, right, across, skip, weights)


def solution(mesh):
    return jax.shard_map(
        shards,
        mesh=mesh,
        in_specs=(
            P("groups", "lon", None),
            P(None, None, "lon"),
            P(),
            P(),
            P(),
            P(),
            P(),
            P(),
            P(),
        ),
        out_specs=P("groups", None, "lon"),
        check_vma=False,
    )
```

profile of v0, /device:TPU:0, one launch (start us, length us, event | category | flops | bytes accessed | tf_op | source)
XLA Modules:
  0.0 45.6 jit_solution(10924715808886400338)
XLA Ops:
  0.0 1.0 %reshape.18 = bf16[16,2,16,128]{3,2,1,0:T(8,128)(2,1)S(1)} reshape(bf16[16,2,2048]{2,1,0:T(2,128)(2,1)} %param.9) | data formatting | bytes 262144 | tf_op jit(solution)/shard_map/reshape | solution.py:321
  1.0 0.1 copy.10
  1.1 0.0 copy-start.5
  1.1 15.1 %all_to_all.5.block = bf16[16,32,128]{2,1,0:T(8,128)(2,1)S(1)} all-to-all(bf16[16,32,128]{2,1,0:T(8,128)(2,1)S(1)} %bitcast.12), channel_id=1, replica_groups=mesh['groups'=2,'lon'=16] {'lon'}, dimensions={0} | all-to-all | bytes 262144 | tf_op jit(solution)/shard_map/all_to_all | solution.py:323
  16.2 0.0 copy-done.5
  16.2 8.1 %remap.1 = (bf16[1024,128]{1,0:T(8,128)(2,1)S(1)}, f32[128,128]{1,0:T(8,128)S(1)}, f32[128,128]{1,0:T(8,128)S(1)}, f32[256,128]{1,0:T(8,128)S(1)}) custom-call(bf16[16,32,128]{2,1,0:T(8,128)(2,1)S(1)} %all_to_all.5.block, s32[2,32,128]{2,1,0:T(8,128)S(1)} %copy-done.5), custom_call_target="tpu_custom_call" | custom-call | tf_op jit(solution)/shard_map/remap/pallas_call | solution.py:140
  24.3 0.1 collective-permute-start
  24.4 0.0 copy-start.7
  24.4 0.0 copy-start.4
  24.4 4.5 %collective-permute-start.1 = (f32[128,128]{1,0:T(8,128)S(1)}, f32[128,128]{1,0:T(8,128)S(1)}, u32[]{:S(2)}, u32[]{:S(2)}) collective-permute-start(f32[128,128]{1,0:T(8,128)S(1)} %get-tuple-element.18), channel_id=1, source_target_pairs={{1,0},{2,1},{3,2},{4,3},{5,4},{6,5},{7,6},{8,7},{9,8},{10,9},{11,1... | collective-permute-start | bytes 196616 | tf_op jit(solution)/shard_map/ppermute | solution.py:19
  28.9 1.9 %collective-permute-done.left = f32[128,128]{1,0:T(8,128)S(1)} collective-permute-done((f32[128,128]{1,0:T(8,128)S(1)}, f32[128,128]{1,0:T(8,128)S(1)}, u32[]{:S(2)}, u32[]{:S(2)}) %collective-permute-start) | collective-permute-done | bytes 65568 | tf_op jit(solution)/shard_map/ppermute | solution.py:19
  30.7 0.7 %collective-permute-done.1.right = f32[128,128]{1,0:T(8,128)S(1)} collective-permute-done((f32[128,128]{1,0:T(8,128)S(1)}, f32[128,128]{1,0:T(8,128)S(1)}, u32[]{:S(2)}, u32[]{:S(2)}) %collective-permute-start.1) | collective-permute-done | bytes 65568 | tf_op jit(solution)/shard_map/ppermute | solution.py:19
  31.4 0.0 copy-start.1
  31.4 0.0 copy-start.2
  31.4 0.1 collective-permute-start.2
  31.5 0.0 copy-start.6
  31.5 0.2 copy.11.down
  31.8 0.0 copy-done.3
  31.8 0.6 %copy-done = bf16[3,3,128,128]{3,2,1,0:T(8,128)(2,1)S(1)} copy-done((bf16[3,3,128,128]{3,2,1,0:T(8,128)(2,1)S(1)}, bf16[3,3,128,128]{3,2,1,0:T(8,128)(2,1)}, u32[]{:S(2)}) %copy-start) | copy-done | bytes 294936
  32.4 0.0 copy-done.1
  32.4 0.1 copy-done.2
  32.5 0.8 %arrange_weights.1 = (bf16[256,256]{1,0:T(8,128)(2,1)S(1)}, bf16[1024,256]{1,0:T(8,128)(2,1)S(1)}, bf16[768,128]{1,0:T(8,128)(2,1)S(1)}, bf16[1152,128]{1,0:T(8,...) custom-call(bf16[3,3,16,64]{3,2,1,0:T(8,128)(2,1)S(1)} %bitcast.11, ...), custom_call_target="tpu_custom_call" | custom-call | tf_op jit(solution)/shard_map/arrange_weights/pallas_call | solution.py:82
  33.3 4.0 %collective-permute-done.2.across = f32[240,128]{1,0:T(8,128)S(1)} collective-permute-done((f32[240,128]{1,0:T(8,128)S(1)}, f32[240,128]{1,0:T(8,128)S(1)}, u32[]{:S(2)}, u32[]{:S(2)}) %collective-permute-start.2) | collective-permute-done | bytes 122912 | tf_op jit(solution)/shard_map/ppermute | solution.py:19
  37.3 8.4 %network.1 = f32[8,32,128]{2,1,0:T(8,128)} custom-call(bf16[1024,128]{1,0:T(8,128)(2,1)S(1)} %get-tuple-element.16.cells, f32[128,128]{1,0:T(8,128)S(1)} %collective-permute-done.left, f32[128,128]{1,0:T(8,128)S(1)} %collective-permute-done.1.right, f32[240,128]{1,0:T(8,128)S(1)} %collective-permute-done.2.across, f32[256,128]{1,0:T(8,128)S(1)} %get-tuple-element.19.skip, ...), custom_call_target="tpu_custom_call" | custom-call | tf_op jit(solution)/shard_map/network/pallas_call | solution.py:290
  (10 shorter events, 0.0 us)
Async XLA Ops:
  1.1 15.1 %copy-start.5 = (s32[2,32,128]{2,1,0:T(8,128)S(1)}, s32[2,32,128]{2,1,0:T(8,128)}, u32[]{:S(2)}) copy-start(s32[2,32,128]{2,1,0:T(8,128)} %table.1) | copy-start | bytes 98308
  24.3 6.4 %collective-permute-start = (f32[128,128]{1,0:T(8,128)S(1)}, f32[128,128]{1,0:T(8,128)S(1)}, u32[]{:S(2)}, u32[]{:S(2)}) collective-permute-start(f32[128,128]{1,0:T(8,128)S(1)} %get-tuple-element.17), channel_id=1, source_target_pairs={{15,0},{0,1},{1,2},{2,3},{3,4},{4,5},{5,6},{6,7},{7,8},{8,9},{9,10... | collective-permute-start | bytes 196616 | tf_op jit(solution)/shard_map/ppermute | solution.py:19
  24.4 7.2 %copy-start.7 = (bf16[3,3,128,64]{2,3,1,0:T(8,128)(2,1)S(1)}, bf16[3,3,128,64]{2,3,1,0:T(8,128)(2,1)}, u32[]{:S(2)}) copy-start(bf16[3,3,128,64]{2,3,1,0:T(8,128)(2,1)} %param.13) | copy-start | bytes 442372
  24.4 7.4 %copy-start.4 = (bf16[3,3,64,16]{2,3,1,0:T(8,128)(2,1)S(1)}, bf16[3,3,64,16]{2,3,1,0:T(8,128)(2,1)}, u32[]{:S(2)}) copy-start(bf16[3,3,64,16]{2,3,1,0:T(8,128)(2,1)} %param.11) | copy-start | bytes 55300
  24.4 7.0 %collective-permute-start.1 = (f32[128,128]{1,0:T(8,128)S(1)}, f32[128,128]{1,0:T(8,128)S(1)}, u32[]{:S(2)}, u32[]{:S(2)}) collective-permute-start(f32[128,128]{1,0:T(8,128)S(1)} %get-tuple-element.18), channel_id=1, source_target_pairs={{1,0},{2,1},{3,2},{4,3},{5,4},{6,5},{7,6},{8,7},{9,8},{10,9},{11,1... | collective-permute-start | bytes 196616 | tf_op jit(solution)/shard_map/ppermute | solution.py:19
  30.7 1.0 %copy-start.3 = (bf16[3,3,64,128]{3,2,1,0:T(8,128)(2,1)S(1)}, bf16[3,3,64,128]{3,2,1,0:T(8,128)(2,1)}, u32[]{:S(2)}) copy-start(bf16[3,3,64,128]{3,2,1,0:T(8,128)(2,1)} %merge.1) | copy-start | bytes 442372
  31.4 1.0 %copy-start = (bf16[3,3,128,128]{3,2,1,0:T(8,128)(2,1)S(1)}, bf16[3,3,128,128]{3,2,1,0:T(8,128)(2,1)}, u32[]{:S(2)}) copy-start(bf16[3,3,128,128]{3,2,1,0:T(8,128)(2,1)} %coarse.1) | copy-start | bytes 884740
  31.4 1.0 %copy-start.1 = (bf16[3,3,64,64]{3,2,1,0:T(8,128)(2,1)S(1)}, bf16[3,3,64,64]{3,2,1,0:T(8,128)(2,1)}, u32[]{:S(2)}) copy-start(bf16[3,3,64,64]{3,2,1,0:T(8,128)(2,1)} %second.1) | copy-start | bytes 221188
  31.4 1.1 %copy-start.2 = (bf16[3,3,64,128]{3,2,1,0:T(8,128)(2,1)S(1)}, bf16[3,3,64,128]{3,2,1,0:T(8,128)(2,1)}, u32[]{:S(2)}) copy-start(bf16[3,3,64,128]{3,2,1,0:T(8,128)(2,1)} %up.1) | copy-start | bytes 442372
  31.4 5.8 %collective-permute-start.2 = (f32[240,128]{1,0:T(8,128)S(1)}, f32[240,128]{1,0:T(8,128)S(1)}, u32[]{:S(2)}, u32[]{:S(2)}) collective-permute-start(f32[240,128]{1,0:T(8,128)S(1)} %bitcast.14), channel_id=1, source_target_pairs={{8,0},{9,1},{10,2},{11,3},{12,4},{13,5},{14,6},{15,7},{0,8},{1,9},... | collective-permute-start | bytes 368648 | tf_op jit(solution)/shard_map/ppermute | solution.py:19
  31.5 1.0 %copy-start.6 = (bf16[8,64]{1,0:T(8,128)(2,1)S(1)}, bf16[8,64]{1,0:T(8,128)(2,1)}, u32[]{:S(2)}) copy-start(bf16[8,64]{1,0:T(8,128)(2,1)} %projection.1) | copy-start | bytes 3076
where the time goes:
time: 45.9 us; the launch traced here: 45.6 us
  Pallas kernels  17.2 us (37%)
  blocking collectives  15.1 us (33%)
  waiting for transfers between devices  6.56 us (14%)
  starting transfers between devices  4.59 us (10%)
  local copies, waits for them, and re-layouts  2.02 us (4%)
    all_to_all x1, blocking collectives, shards(): lax.all_to_all(parcels, 'lon', split_axis=0, concat_axis=0, tiled=True)  15.1 us
    pallas_call x1, Pallas kernels, network(): pl.pallas_call(network_kernel, out_shape=jax.ShapeDtypeStruct((weights[-1...  8.36 us
    pallas_call x1, Pallas kernels, remap(): pl.pallas_call(remap_kernel, out_shape=[jax.ShapeDtypeStruct((grid_rows /...  8.1 us
    ppermute x3, waiting for transfers between devices, from_behind(): return lax.ppermute(block, axis, route)  6.56 us
    ppermute x3, starting transfers between devices, from_behind(): return lax.ppermute(block, axis, route)  4.59 us
    reshape x2, local copies, waits for them, and re-layouts, shards(): latlon_fields.reshape(channels, rows, count, columns).transpose(2, 1, 0, 3)  1.05 us
    unnamed x17, local copies, waits for them, and re-layouts  0.97 us
  transfers between devices with their start and end apart: 3, of which 3 were waited for; matrix products, arithmetic and copies ran while one was open for 1% of the time, Pallas kernels for 2%

commit v1 on v0

v1 whole, which is shorter than its diff:
```python
import jax
import jax.numpy as jnp
from jax import lax
from jax.experimental import pallas as pl
from jax.experimental.pallas import tpu as pltpu
from jax.sharding import PartitionSpec as P

F32 = jnp.float32
BF16 = jnp.bfloat16
HALO = 4
GAP = 8
POLAR = 3
TOP = 2


def from_behind(block, axis, distance):
    devices = range(lax.axis_size(axis))
    route = [((i - distance) % len(devices), i) for i in devices]
    return lax.ppermute(block, axis, route)


def tap(kernel_ref, row, col):
    if 0 <= row < 3 and 0 <= col < 3:
        return kernel_ref[row, col].astype(F32)
    return jnp.zeros(kernel_ref.shape[2:], F32)


def arrange_kernel(first, second, down, coarse, up, merge, projection, w1, w2, wd, wc, wu, wm, wp):
    channels = second.shape[3]
    inputs = first.shape[2]
    for half in range(2):
        for side in range(2):
            for p in range(2):
                for q in range(2):
                    t = 1 + p if half == 0 else (3, 0)[p]
                    u = 1 + q if side == 0 else (3, 0)[q]
                    at = (((half * 2 + side) * 2 + p) * 2 + q) * inputs
                    pieces = [tap(first, t - a, u - b) for a in range(2) for b in range(2)]
                    w1[at : at + inputs, :] = jnp.concatenate(pieces, axis=1).astype(BF16)
    for t in range(4):
        for code in range(4):
            at = (t * 4 + code) * channels
            source = (0, 1, -2, -1)[code]
            for p in range(2):
                pair = [tap(second, t - p, source - target + 1) for target in (-1, 0)]
                w2[at : at + channels, p * 128 : (p + 1) * 128] = jnp.concatenate(pair, axis=0).T.astype(BF16)
            source = code - 1
            for p in range(2):
                pair = [tap(merge, t - p, source - target + 1) for target in (0, 1)]
                pair = jnp.concatenate(pair, axis=0).T.astype(BF16)
                wm[at : at + channels, p * 128 : (p + 1) * 128] = pair[:channels]
                wm[16 * channels + at : 16 * channels + at + channels, p * 128 : (p + 1) * 128] = pair[channels:]
            if t < 3:
                wd[at : at + channels, :] = tap(down, t, code).astype(BF16)
    wide = coarse.shape[3]
    for a in range(3):
        for b in range(3):
            at = (a * 3 + b) * wide
            wc[at : at + wide, :] = tap(coarse, a, b).T.astype(BF16)
    row_taps = ((1, 3), (0, 2))
    col_taps = ((0, 2), (3, 1))
    for di in range(2):
        for dj in range(2):
            at = (di * 2 + dj) * wide
            for p in range(2):
                pair = jnp.concatenate([tap(up, row_taps[p][di], col_taps[q][dj]) for q in range(2)], axis=0)
                wu[at : at + wide, p * 128 : (p + 1) * 128] = pair.T.astype(BF16)
    rows = projection[...].astype(F32)
    blank = jnp.zeros_like(rows)
    lines = [jnp.concatenate([rows if m == n else blank for m in range(4)], axis=1) for n in range(4)]
    wp[...] = jnp.concatenate(lines, axis=0).astype(BF16)


def arrange(first, second, down, coarse, up, merge, projection):
    channels, wide = second.shape[3], coarse.shape[3]
    shapes = (
        (16 * first.shape[3], 4 * channels),
        (16 * channels, 4 * channels),
        (12 * channels, wide),
        (9 * wide, wide),
        (4 * wide, 4 * channels),
        (32 * channels, 4 * channels),
        (4 * projection.shape[0], 4 * channels),
    )
    return pl.pallas_call(
        arrange_kernel,
        out_shape=[jax.ShapeDtypeStruct(s, BF16) for s in shapes],
        compiler_params=pltpu.CompilerParams(vmem_limit_bytes=16 * 2**20),
        name="arrange_weights",
    )(jnp.swapaxes(first, 2, 3), second, jnp.swapaxes(down, 2, 3), coarse, up, merge, projection)


def locate_kernel(table, onehot, source):
    _, grid_rows, columns = table.shape
    half = columns // 2
    code = table[0] * columns + lax.rem(table[1], columns)
    lane = lax.broadcasted_iota(jnp.int32, (grid_rows, columns), 1)
    odd = [jnp.take_along_axis(code, lax.rem(lane, half) * 2 + q, axis=1) for q in range(2)]
    left = lax.broadcasted_iota(jnp.int32, (1, columns), 1) < half
    place = lax.broadcasted_iota(jnp.int32, (2 * columns, columns), 0)
    for pair in range(grid_rows // 4):
        for p in range(2):
            for q in range(2):
                n = p * 2 + q
                above, below = 4 * pair + p, 4 * pair + 2 + p
                line = jnp.where(left, odd[q][above : above + 1, :], odd[q][below : below + 1, :])
                source[4 * pair + n : 4 * pair + n + 1, :] = lax.div(line, 2 * columns)
                here = place == lax.rem(line, 2 * columns)
                onehot[pair * 2 * columns : (pair + 1) * 2 * columns, n * columns : (n + 1) * columns] = jnp.where(
                    here, 1.0, 0.0
                ).astype(BF16)


def locate(table):
    _, grid_rows, columns = table.shape
    return pl.pallas_call(
        locate_kernel,
        out_shape=[
            jax.ShapeDtypeStruct((grid_rows // 4 * 2 * columns, 4 * columns), BF16),
            jax.ShapeDtypeStruct((grid_rows, columns), jnp.int32),
        ],
        compiler_params=pltpu.CompilerParams(vmem_limit_bytes=16 * 2**20),
        name="locate",
    )(table)


def remap(block, onehot, source, pairs):
    devices, depth, columns = block.shape
    channels = depth // 2
    half = columns // 2
    count = len(pairs)

    def kernel(block, onehot, source, cells, to_left, to_right, skip):
        upper = block[:, 0:channels, :].reshape(devices * channels, columns)
        lower = block[:, channels:depth, :].reshape(devices * channels, columns)
        fields = jnp.concatenate([upper, lower], axis=1)
        for at, pair in enumerate(pairs):
            chosen = onehot[pair * 2 * columns : (pair + 1) * 2 * columns, :]
            found = jnp.dot(fields, chosen, preferred_element_type=F32)
            lines = []
            for n in range(4):
                own = jnp.broadcast_to(source[4 * pair + n : 4 * pair + n + 1, :], (channels, columns))
                total = jnp.zeros((channels, columns), F32)
                for s in range(devices):
                    value = found[s * channels : (s + 1) * channels, n * columns : (n + 1) * columns]
                    total = jnp.where(own == s, value, total)
                lines.append(total)
                skip[(at * 4 + n) * 8 : (at * 4 + n + 1) * 8, :] = total[:8]
            turned = jnp.concatenate(lines + lines, axis=0).T
            cells[at * columns : (at + 1) * columns, :] = turned.astype(BF16)
            for i in range(2):
                row = (at * 2 + i) * HALO
                to_left[row : row + HALO, :] = turned[i * half : i * half + HALO]
                to_right[row : row + HALO, :] = turned[(i + 1) * half - HALO : (i + 1) * half]

    return pl.pallas_call(
        kernel,
        out_shape=[
            jax.ShapeDtypeStruct((count * columns, columns), BF16),
            jax.ShapeDtypeStruct((count * 2 * HALO, columns), F32),
            jax.ShapeDtypeStruct((count * 2 * HALO, columns), F32),
            jax.ShapeDtypeStruct((count * 32, columns), F32),
        ],
        compiler_params=pltpu.CompilerParams(vmem_limit_bytes=16 * 2**20),
        name="remap",
    )(block, onehot, source)


def silu(values):
    h = 0.5 * values
    return (h + h * jnp.tanh(h)).astype(BF16).astype(F32)


def ring(values, step, shift):
    rows = [pltpu.roll(values[at : at + step], shift % step, 0) for at in range(0, values.shape[0], step)]
    return rows[0] if len(rows) == 1 else jnp.concatenate(rows, axis=0)


def network_kernel(
    cells_top, cells_rest, left, right, across, skip_top, skip_rest,
    w1, w2, wd, wc, wu, wm, wp, out, x0, y0, y1, y2, yc, yo, yu,
):
    half = out.shape[2] // 2
    blocks = out.shape[1] // 2
    step = half + 2 * HALO + GAP
    polar = POLAR
    top = 0
    bottom = blocks + 1
    pole = blocks + 2
    end = pole + polar + 1
    group = 4

    def at(row, count=1):
        return slice(row * step, (row + count) * step)

    def chunks(polar_rows):
        return [(1 + i, group) for i in range(0, blocks, group)] + [(pole + 1, polar_rows)]

    def lane_mask(rows, width):
        return lax.rem(lax.div(lax.broadcasted_iota(jnp.int32, (rows, 128), 1), width), 2) == 0

    x0[...] = jnp.zeros_like(x0)
    rows_of_top = cells_top.shape[0] // half
    for i in range(blocks + polar):
        base = (1 + i if i < blocks else pole + 1 + i - blocks) * step
        if i >= blocks:
            own = across[(i - blocks) * half : (i - blocks + 1) * half, :]
        elif i < rows_of_top:
            own = cells_top[i * half : (i + 1) * half, :]
        else:
            own = cells_rest[(i - rows_of_top) * half : (i - rows_of_top + 1) * half, :]
        x0[base : base + half, :] = own.astype(F32)
        x0[base + half : base + half + HALO, :] = right[i * HALO : (i + 1) * HALO, :]
        x0[base + step - HALO : base + step, :] = left[i * HALO : (i + 1) * HALO, :]
    x0[at(top), :] = pltpu.roll(x0[at(pole + 1), :], 32, 1)
    x0[at(pole), :] = pltpu.roll(x0[at(1), :], 32, 1)
    for row in range(0, end + 1):
        x = x0[at(row), :]
        side = jnp.where(lane_mask(step, 16), ring(x, step, -1), ring(x, step, 1))
        y0[at(row), :] = jnp.where(lane_mask(step, 64), x, side)

    def store_fine(y, row, count, values, shift):
        moved = ring(values, step, shift).astype(BF16)
        values = values.astype(BF16)
        for p in range(2):
            lanes = slice(p * 128, (p + 1) * 128)
            y[at(row, count), p * 256 : p * 256 + 128] = values[:, lanes]
            y[at(row, count), p * 256 + 128 : p * 256 + 256] = moved[:, lanes]

    def edges_fine(y, polar_rows):
        y[at(top), 256:512] = y[at(pole + 1), 0:256]
        y[at(pole), 256:512] = y[at(1), 0:256]
        y[at(bottom), 0:256] = jnp.zeros((step, 256), BF16)
        y[at(pole + 1 + polar_rows), 0:256] = jnp.zeros((step, 256), BF16)

    def product(pieces, weights):
        return jnp.dot(jnp.concatenate(pieces, axis=1), weights[...], preferred_element_type=F32)

    for row, count in chunks(polar):
        mask = lane_mask(count * step, 32)
        vertical = jnp.where(mask, y0[at(row + 1, count), :], y0[at(row - 1, count), :])
        pieces = [y0[at(row, count), :].astype(BF16), vertical.astype(BF16)]
        store_fine(y1, row, count, silu(product(pieces, w1)), 1)
    edges_fine(y1, polar)

    for row, count in chunks(polar - 1):
        pieces = [y1[at(row - 1, count), 256:512], y1[at(row, count), :], y1[at(row + 1, count), 0:256]]
        store_fine(y2, row, count, silu(product(pieces, w2)), -1)
    edges_fine(y2, polar - 1)

    for row, count in chunks(polar - 1):
        pieces = [y2[at(row - 1, count), 256:512], y2[at(row, count), :]]
        values = silu(product(pieces, wd))
        yc[at(row, count), 0:128] = ring(values, step, 1).astype(BF16)
        yc[at(row, count), 128:256] = values.astype(BF16)
        yc[at(row, count), 256:384] = ring(values, step, -1).astype(BF16)
    yc[at(top), :] = yc[at(pole + 1), :]
    yc[at(pole), :] = yc[at(1), :]
    yc[at(bottom), :] = jnp.zeros((step, 384), BF16)

    for row, count in chunks(polar - 2):
        pieces = [yc[at(row + a, count), :] for a in (-1, 0, 1)]
        values = silu(product(pieces, wc))
        yo[at(row, count), 0:128] = ring(values, step, 1).astype(BF16)
        yo[at(row, count), 128:256] = values.astype(BF16)
    yo[at(bottom), :] = jnp.zeros((step, 256), BF16)
    yo[at(pole + 2), :] = jnp.zeros((step, 256), BF16)

    for row, count in chunks(polar - 2):
        pieces = [yo[at(row, count), :], yo[at(row + 1, count), :]]
        store_fine(yu, row, count, silu(product(pieces, wu)), -1)
    edges_fine(yu, polar - 2)

    lane = lax.broadcasted_iota(jnp.int32, (8, 2 * half), 1)
    even = lax.rem(lane, 2) == 0
    for row in range(1, 1 + blocks, group):

        def own(y, offset, lanes):
            rows = [y[(row + offset + i) * step : (row + offset + i) * step + half, lanes] for i in range(group)]
            return jnp.concatenate(rows, axis=0)

        pieces = []
        for y in (y2, yu):
            pieces += [own(y, -1, slice(256, 512)), own(y, 0, slice(0, 512)), own(y, 1, slice(0, 256))]
        merged = silu(product(pieces, wm)).astype(BF16)
        update = lax.dot_general(wp[...], merged, (((1,), (1,)), ((), ())), preferred_element_type=F32)
        for n in range(group // 2):
            pair = (row - 1) // 2 + n
            skip, place = (skip_top, pair) if pair < TOP else (skip_rest, pair - TOP)
            total = update[:, n * 2 * half : (n + 1) * 2 * half] + skip[place * 32 : (place + 1) * 32, :]
            for i in range(2):
                spread = lax.div(lane, 2) + i * half
                for p in range(2):
                    evens = jnp.take_along_axis(total[p * 16 : p * 16 + 8], spread, axis=1)
                    odds = jnp.take_along_axis(total[p * 16 + 8 : p * 16 + 16], spread, axis=1)
                    out[:, 4 * pair + 2 * i + p, :] = jnp.where(even, evens, odds)


def network(out_shape, cells_top, cells_rest, left, right, across, skip_top, skip_rest, weights):
    step = out_shape[2] // 2 + 2 * HALO + GAP
    rows = (out_shape[1] // 2 + 2 + POLAR + 2) * step
    vmem = pltpu.VMEM
    return pl.pallas_call(
        network_kernel,
        out_shape=jax.ShapeDtypeStruct(out_shape, F32),
        scratch_shapes=[
            vmem((rows, 128), F32),
            vmem((rows, 128), F32),
            vmem((rows, 512), BF16),
            vmem((rows, 512), BF16),
            vmem((rows, 384), BF16),
            vmem((rows, 256), BF16),
            vmem((rows, 512), BF16),
        ],
        compiler_params=pltpu.CompilerParams(vmem_limit_bytes=40 * 2**20),
        name="network",
    )(cells_top, cells_rest, left, right, across, skip_top, skip_rest, *weights)


def shards(
    latlon_fields,
    remap_table,
    kernel_first,
    kernel_second,
    kernel_down,
    kernel_coarse,
    kernel_up,
    kernel_merge,
    projection,
):
    _, grid_rows, columns = remap_table.shape
    count = lax.axis_size("lon")
    channels, rows, _ = latlon_fields.shape
    half = columns // 2
    parcels = latlon_fields.reshape(channels, rows, count, columns).transpose(2, 1, 0, 3)
    parcels = parcels.reshape(count, rows * channels, columns)
    block = lax.all_to_all(parcels, "lon", split_axis=0, concat_axis=0, tiled=True)
    weights = arrange(
        kernel_first, kernel_second, kernel_down, kernel_coarse, kernel_up, kernel_merge, projection
    )
    onehot, source = locate(remap_table)
    cells_top, left_top, right_top, skip_top = remap(block, onehot, source, range(TOP))
    across = from_behind(cells_top[: POLAR * half], "lon", count // 2)
    cells_rest, left_rest, right_rest, skip_rest = remap(block, onehot, source, range(TOP, grid_rows // 4))
    polar = across.reshape(POLAR, half, -1).astype(F32)
    to_left = jnp.concatenate([left_top, left_rest, polar[:, :HALO].reshape(POLAR * HALO, -1)], axis=0)
    to_right = jnp.concatenate([right_top, right_rest, polar[:, half - HALO :].reshape(POLAR * HALO, -1)], axis=0)
    left = from_behind(to_right, "lon", 1)
    right = from_behind(to_left, "lon", -1)
    out_shape = (projection.shape[0], grid_rows, columns)
    return network(out_shape, cells_top, cells_rest, left, right, across, skip_top, skip_rest, weights)


def solution(mesh):
    return jax.shard_map(
        shards,
        mesh=mesh,
        in_specs=(
            P("groups", "lon", None),
            P(None, None, "lon"),
            P(),
            P(),
            P(),
            P(),
            P(),
            P(),
            P(),
        ),
        out_specs=P("groups", None, "lon"),
        check_vma=False,
    )
```

time: 45.9 us -> 39.8 us (0.87)
  blocking collectives: 15.1 us -> 0 us
  starting transfers between devices: 4.59 us -> 12.2 us
  Pallas kernels: 17.2 us -> 9.9 us
  local copies, waits for them, and re-layouts: 2.02 us -> 6.5 us
  waiting for transfers between devices: 6.56 us -> 9.01 us
  other arithmetic: 0.02 us -> 1.49 us
    all_to_all x1 -> x0, blocking collectives: 15.1 us -> none  [shards(): lax.all_to_all(parcels, 'lon', split_axis=0, concat_axis=0, tiled=True)]
    all_to_all x0 -> x1, starting transfers between devices: none -> 7.39 us  [shards(): lax.all_to_all(parcels, 'lon', split_axis=0, concat_axis=0, tiled=True)]
    pallas_call x2 -> x4, Pallas kernels: 16.5 us -> 9.27 us  [the longest x1 7.36 us: network(): pl.pallas_call(network_kernel, out_shape=jax.ShapeDtypeStruct(out_shape,...]
    all_to_all x0 -> x1, waiting for transfers between devices: none -> 6.32 us  [shards(): lax.all_to_all(parcels, 'lon', split_axis=0, concat_axis=0, tiled=True)]
    ppermute x3, waiting for transfers between devices: 6.56 us -> 2.69 us  [from_behind(): return lax.ppermute(block, axis, route)]
    unnamed x17 -> x24, local copies, waits for them, and re-layouts: 0.97 us -> 4.77 us
    concatenate x1 -> x2, other arithmetic: 0.01 us -> 1.49 us  [the longest x1 0.74 us: shards(): jnp.concatenate([right_top, right_rest, polar[:, half - HALO:].reshape(PO...]
    reshape x2, local copies, waits for them, and re-layouts: 1.05 us -> 1.7 us  [shards(): latlon_fields.reshape(channels, rows, count, columns).transpose(2, 1, 0, 3)]
  transfers between devices with their start and end apart: 3 -> 4, of which waited for: 3 -> 2; matrix products, arithmetic and copies ran while one was open for 1% -> 2% of each run, Pallas kernels for 2% -> 5%
where the time goes in v1:
time: 39.8 us; the launch traced here: 39.3 us
  starting transfers between devices  12.2 us (31%)
  Pallas kernels  9.9 us (25%)
  waiting for transfers between devices  9.01 us (23%)
  local copies, waits for them, and re-layouts  6.5 us (16%)
  other arithmetic  1.49 us (4%)
    all_to_all x1, starting transfers between devices, shards(): lax.all_to_all(parcels, 'lon', split_axis=0, concat_axis=0, tiled=True)  7.39 us
    pallas_call x1, Pallas kernels, network(): pl.pallas_call(network_kernel, out_shape=jax.ShapeDtypeStruct(out_shape,...  7.36 us
    all_to_all x1, waiting for transfers between devices, shards(): lax.all_to_all(parcels, 'lon', split_axis=0, concat_axis=0, tiled=True)  6.32 us
    ppermute x3, starting transfers between devices, from_behind(): return lax.ppermute(block, axis, route)  4.86 us
    unnamed x24, local copies, waits for them, and re-layouts  4.77 us
    ppermute x3, waiting for transfers between devices, from_behind(): return lax.ppermute(block, axis, route)  2.69 us
    reshape x2, local copies, waits for them, and re-layouts, shards(): latlon_fields.reshape(channels, rows, count, columns).transpose(2, 1, 0, 3)  1.7 us
    pallas_call x2, Pallas kernels, remap(): pl.pallas_call(kernel, out_shape=[jax.ShapeDtypeStruct((count * columns,...  1.06 us
  transfers between devices with their start and end apart: 4, of which 2 were waited for; matrix products, arithmetic and copies ran while one was open for 2% of the time, Pallas kernels for 5%

profile of v1, /device:TPU:0, one launch (start us, length us, event | category | flops | bytes accessed | tf_op | source)
XLA Modules:
  0.0 39.3 jit_solution(10166167587650935332)
XLA Ops:
  0.0 1.0 %reshape.15 = bf16[16,2,16,128]{3,2,1,0:T(8,128)(2,1)S(1)} reshape(bf16[16,2,2048]{2,1,0:T(2,128)(2,1)} %param.9) | data formatting | bytes 262144 | tf_op jit(solution)/shard_map/reshape | solution.py:335
  1.0 0.7 %copy.10 = bf16[16,2,16,128]{3,0,1,2:T(8,128)(2,1)} copy(bf16[16,2,16,128]{3,2,1,0:T(8,128)(2,1)S(1)} %reshape.15) | data formatting | bytes 262144 | tf_op jit(solution)/shard_map/reshape | solution.py:335
  1.7 7.4 %all-to-all-start = ((bf16[16,32,128]{2,1,0:T(8,128)(2,1)}), bf16[16,32,128]{2,1,0:T(8,128)(2,1)S(1)}, u32[]{:S(2)}, u32[]{:S(2)}) async-start(bf16[16,32,128]{2,1,0:T(8,128)(2,1)} %bitcast.1), calls=%async_computation | async-start | bytes 262144 | tf_op jit(solution)/shard_map/all_to_all | solution.py:337
  9.1 0.0 copy-start.8
  9.1 0.7 %copy-done.8 = s32[2,32,128]{2,1,0:T(8,128)S(1)} copy-done((s32[2,32,128]{2,1,0:T(8,128)S(1)}, s32[2,32,128]{2,1,0:T(8,128)}, u32[]{:S(2)}) %copy-start.8) | copy-done | bytes 32792
  9.9 0.8 %locate.1 = (bf16[2048,512]{1,0:T(8,128)(2,1)S(1)}, s32[32,128]{1,0:T(8,128)S(1)}) custom-call(s32[2,32,128]{2,1,0:T(8,128)S(1)} %copy-done.8), custom_call_target="tpu_custom_call" | custom-call | tf_op jit(solution)/shard_map/locate/pallas_call | solution.py:116
  10.7 6.3 %all-to-all-done.block = bf16[16,32,128]{2,1,0:T(8,128)(2,1)S(1)} async-done(((bf16[16,32,128]{2,1,0:T(8,128)(2,1)}), bf16[16,32,128]{2,1,0:T(8,128)(2,1)S(1)}, u32[]{:S(2)}, u32[]{:S(2)}) %all-to-all-start) | async-done | bytes 131104 | tf_op jit(solution)/shard_map/all_to_all | solution.py:337
  17.0 0.0 copy-start.4
  17.1 0.4 %remap.2 = (bf16[256,128]{1,0:T(8,128)(2,1)S(1)}, f32[16,128]{1,0:T(8,128)S(1)}, f32[16,128]{1,0:T(8,128)S(1)}, f32[64,128]{1,0:T(8,128)S(1)}) custom-call(bf16[16,32,128]{2,1,0:T(8,128)(2,1)S(1)} %all-to-all-done.block, bf16[2048,512]{1,0:T(8,128)(2,1)S(1)} %get-tuple-element.22.onehot, s32[32,128]{1,0:T(8,128)S(1)} %get-tuple-element.23.source), custom_call_target="tpu_custom_call" | custom-call | tf_op jit(solution)/shard_map/remap/pallas_call | solution.py:156
  17.5 0.6 %copy-done.6 = f32[64,128]{1,0:T(8,128)} copy-done((f32[64,128]{1,0:T(8,128)}, f32[64,128]{1,0:T(8,128)S(1)}, u32[]{:S(2)}) %copy-start.6) | copy-done | bytes 32792
  18.1 0.4 %collective-permute-start = (bf16[192,128]{1,0:T(8,128)(2,1)S(1)}, bf16[192,128]{1,0:T(8,128)(2,1)S(1)}, u32[]{:S(2)}, u32[]{:S(2)}) collective-permute-start(bf16[192,128]{1,0:T(8,128)(2,1)S(1)} %slice.9), channel_id=1, source_target_pairs={{8,0},{9,1},{10,2},{11,3},{12,4},{13,5},{14,6},{15,7},{0,8},{1,9},... | collective-permute-start | bytes 147464 | tf_op jit(solution)/shard_map/ppermute | solution.py:19
  18.5 0.7 %remap.3 = (bf16[768,128]{1,0:T(8,128)(2,1)S(1)}, f32[48,128]{1,0:T(8,128)S(1)}, f32[48,128]{1,0:T(8,128)S(1)}, f32[192,128]{1,0:T(8,128)S(1)}) custom-call(bf16[16,32,128]{2,1,0:T(8,128)(2,1)S(1)} %all-to-all-done.block, bf16[2048,512]{1,0:T(8,128)(2,1)S(1)} %get-tuple-element.22.onehot, s32[32,128]{1,0:T(8,128)S(1)} %get-tuple-element.23.source), custom_call_target="tpu_custom_call" | custom-call | tf_op jit(solution)/shard_map/remap/pallas_call | solution.py:156
  19.2 0.6 %copy-done.9 = f32[48,128]{1,0:T(8,128)} copy-done((f32[48,128]{1,0:T(8,128)}, f32[48,128]{1,0:T(8,128)S(1)}, u32[]{:S(2)}) %copy-start.9) | copy-done | bytes 24600
  19.8 0.6 %copy-done.10 = f32[48,128]{1,0:T(8,128)} copy-done((f32[48,128]{1,0:T(8,128)}, f32[48,128]{1,0:T(8,128)S(1)}, u32[]{:S(2)}) %copy-start.10) | copy-done | bytes 24600
  20.4 2.7 %collective-permute-done.across = bf16[192,128]{1,0:T(8,128)(2,1)S(1)} collective-permute-done((bf16[192,128]{1,0:T(8,128)(2,1)S(1)}, bf16[192,128]{1,0:T(8,128)(2,1)S(1)}, u32[]{:S(2)}, u32[]{:S(2)}) %collective-permute-start) | collective-permute-done | bytes 49184 | tf_op jit(solution)/shard_map/ppermute | solution.py:19
  23.1 0.7 %pad_maximum_fusion = f32[76,128]{1,0:T(8,128)S(1)} fusion(f32[12,128]{1,0:T(8,128)S(1)} %reshape.17, f32[48,128]{1,0:T(8,128)} %copy-done.10, f32[16,128]{1,0:T(8,128)S(1)} %get-tuple-element.26), kind=kLoop, calls=%fused_computation | loop fusion | flops 19456 | bytes 77824 | tf_op jit(solution)/shard_map/concatenate | solution.py:347
  23.8 0.7 %pad_maximum_fusion.1 = f32[76,128]{1,0:T(8,128)S(1)} fusion(f32[12,128]{1,0:T(8,128)S(1)} %reshape.18, f32[48,128]{1,0:T(8,128)} %copy-done.9, f32[16,128]{1,0:T(8,128)S(1)} %get-tuple-element.28), kind=kLoop, calls=%fused_computation.1 | loop fusion | flops 19456 | bytes 77824 | tf_op jit(solution)/shard_map/concatenate | solution.py:346
  24.6 4.4 %collective-permute-start.2 = (f32[76,128]{1,0:T(8,128)S(1)}, f32[76,128]{1,0:T(8,128)S(1)}, u32[]{:S(2)}, u32[]{:S(2)}) collective-permute-start(f32[76,128]{1,0:T(8,128)S(1)} %pad_maximum_fusion.1), channel_id=1, source_target_pairs={{1,0},{2,1},{3,2},{4,3},{5,4},{6,5},{7,6},{8,7},{9,8},{10,9},{11,1... | collective-permute-start | bytes 116744 | tf_op jit(solution)/shard_map/ppermute | solution.py:19
  29.0 0.0 copy-start.5
  29.1 0.8 %copy-done.5 = bf16[3,3,64,16]{2,3,1,0:T(8,128)(2,1)S(1)} copy-done((bf16[3,3,64,16]{2,3,1,0:T(8,128)(2,1)S(1)}, bf16[3,3,64,16]{2,3,1,0:T(8,128)(2,1)}, u32[]{:S(2)}) %copy-start.5) | copy-done | bytes 18456
  29.8 0.7 %copy-done.11 = bf16[8,64]{1,0:T(8,128)(2,1)S(1)} copy-done((bf16[8,64]{1,0:T(8,128)(2,1)S(1)}, bf16[8,64]{1,0:T(8,128)(2,1)}, u32[]{:S(2)}) %copy-start.11) | copy-done | bytes 1048
  30.5 0.6 %arrange_weights.1 = (bf16[256,256]{1,0:T(8,128)(2,1)S(1)}, bf16[1024,256]{1,0:T(8,128)(2,1)S(1)}, bf16[768,128]{1,0:T(8,128)(2,1)S(1)}, bf16[1152,128]{1,0:T(8,...) custom-call(bf16[3,3,16,64]{3,2,1,0:T(8,128)(2,1)S(1)} %bitcast.9, ...), custom_call_target="tpu_custom_call" | custom-call | tf_op jit(solution)/shard_map/arrange_weights/pallas_call | solution.py:85
  31.2 0.7 %copy-done.7 = f32[64,128]{1,0:T(8,128)S(1)} copy-done((f32[64,128]{1,0:T(8,128)S(1)}, f32[64,128]{1,0:T(8,128)}, u32[]{:S(2)}) %copy-start.7) | copy-done | bytes 32792
  31.9 7.4 %network.1 = f32[8,32,128]{2,1,0:T(8,128)} custom-call(bf16[256,128]{1,0:T(8,128)(2,1)S(1)} %get-tuple-element.24.cells_top, bf16[768,128]{1,0:T(8,128)(2,1)S(1)} %get-tuple-element.25.cells_rest, f32[76,128]{1,0:T(8,128)S(1)} %collective-permute-done.1.left, f32[76,128]{1,0:T(8,128)S(1)} %collective-permute-done.2.right, ...), custom_call_target="tpu_custom_call" | custom-call | tf_op jit(solution)/shard_map/network/pallas_call | solution.py:303
  (21 shorter events, 0.1 us)
Async XLA Ops:
  1.7 15.3 %all-to-all-start = ((bf16[16,32,128]{2,1,0:T(8,128)(2,1)}), bf16[16,32,128]{2,1,0:T(8,128)(2,1)S(1)}, u32[]{:S(2)}, u32[]{:S(2)}) async-start(bf16[16,32,128]{2,1,0:T(8,128)(2,1)} %bitcast.1), calls=%async_computation | async-start | bytes 262144 | tf_op jit(solution)/shard_map/all_to_all | solution.py:337
  9.1 0.8 %copy-start.8 = (s32[2,32,128]{2,1,0:T(8,128)S(1)}, s32[2,32,128]{2,1,0:T(8,128)}, u32[]{:S(2)}) copy-start(s32[2,32,128]{2,1,0:T(8,128)} %table.1) | copy-start | bytes 98308
  17.0 12.0 %copy-start = (bf16[3,3,128,128]{3,2,1,0:T(8,128)(2,1)S(1)}, bf16[3,3,128,128]{3,2,1,0:T(8,128)(2,1)}, u32[]{:S(2)}) copy-start(bf16[3,3,128,128]{3,2,1,0:T(8,128)(2,1)} %coarse.1) | copy-start | bytes 884740
  17.0 12.0 %copy-start.1 = (bf16[3,3,64,64]{3,2,1,0:T(8,128)(2,1)S(1)}, bf16[3,3,64,64]{3,2,1,0:T(8,128)(2,1)}, u32[]{:S(2)}) copy-start(bf16[3,3,64,64]{3,2,1,0:T(8,128)(2,1)} %second.1) | copy-start | bytes 221188
  17.0 12.0 %copy-start.2 = (bf16[3,3,128,64]{2,3,1,0:T(8,128)(2,1)S(1)}, bf16[3,3,128,64]{2,3,1,0:T(8,128)(2,1)}, u32[]{:S(2)}) copy-start(bf16[3,3,128,64]{2,3,1,0:T(8,128)(2,1)} %param.13) | copy-start | bytes 442372
  17.0 12.0 %copy-start.3 = (bf16[3,3,64,128]{3,2,1,0:T(8,128)(2,1)S(1)}, bf16[3,3,64,128]{3,2,1,0:T(8,128)(2,1)}, u32[]{:S(2)}) copy-start(bf16[3,3,64,128]{3,2,1,0:T(8,128)(2,1)} %up.1) | copy-start | bytes 442372
  17.0 12.0 %copy-start.4 = (bf16[3,3,64,128]{3,2,1,0:T(8,128)(2,1)S(1)}, bf16[3,3,64,128]{3,2,1,0:T(8,128)(2,1)}, u32[]{:S(2)}) copy-start(bf16[3,3,64,128]{3,2,1,0:T(8,128)(2,1)} %merge.1) | copy-start | bytes 442372
  17.5 0.6 %copy-start.6 = (f32[64,128]{1,0:T(8,128)}, f32[64,128]{1,0:T(8,128)S(1)}, u32[]{:S(2)}) copy-start(f32[64,128]{1,0:T(8,128)S(1)} %get-tuple-element.30.skip_top) | copy-start | bytes 98308
  18.1 5.0 %collective-permute-start = (bf16[192,128]{1,0:T(8,128)(2,1)S(1)}, bf16[192,128]{1,0:T(8,128)(2,1)S(1)}, u32[]{:S(2)}, u32[]{:S(2)}) collective-permute-start(bf16[192,128]{1,0:T(8,128)(2,1)S(1)} %slice.9), channel_id=1, source_target_pairs={{8,0},{9,1},{10,2},{11,3},{12,4},{13,5},{14,6},{15,7},{0,8},{1,9},... | collective-permute-start | bytes 147464 | tf_op jit(solution)/shard_map/ppermute | solution.py:19
  19.2 0.6 %copy-start.9 = (f32[48,128]{1,0:T(8,128)}, f32[48,128]{1,0:T(8,128)S(1)}, u32[]{:S(2)}) copy-start(f32[48,128]{1,0:T(8,128)S(1)} %get-tuple-element.29) | copy-start | bytes 73732
  19.8 0.6 %copy-start.10 = (f32[48,128]{1,0:T(8,128)}, f32[48,128]{1,0:T(8,128)S(1)}, u32[]{:S(2)}) copy-start(f32[48,128]{1,0:T(8,128)S(1)} %get-tuple-element.27) | copy-start | bytes 73732
  23.8 7.3 %collective-permute-start.1 = (f32[76,128]{1,0:T(8,128)S(1)}, f32[76,128]{1,0:T(8,128)S(1)}, u32[]{:S(2)}, u32[]{:S(2)}) collective-permute-start(f32[76,128]{1,0:T(8,128)S(1)} %pad_maximum_fusion), channel_id=1, source_target_pairs={{15,0},{0,1},{1,2},{2,3},{3,4},{4,5},{5,6},{6,7},{7,8},{8,9},{9,10... | collective-permute-start | bytes 116744 | tf_op jit(solution)/shard_map/ppermute | solution.py:19
  24.6 6.6 %collective-permute-start.2 = (f32[76,128]{1,0:T(8,128)S(1)}, f32[76,128]{1,0:T(8,128)S(1)}, u32[]{:S(2)}, u32[]{:S(2)}) collective-permute-start(f32[76,128]{1,0:T(8,128)S(1)} %pad_maximum_fusion.1), channel_id=1, source_target_pairs={{1,0},{2,1},{3,2},{4,3},{5,4},{6,5},{7,6},{8,7},{9,8},{10,9},{11,1... | collective-permute-start | bytes 116744 | tf_op jit(solution)/shard_map/ppermute | solution.py:19
  29.0 0.8 %copy-start.5 = (bf16[3,3,64,16]{2,3,1,0:T(8,128)(2,1)S(1)}, bf16[3,3,64,16]{2,3,1,0:T(8,128)(2,1)}, u32[]{:S(2)}) copy-start(bf16[3,3,64,16]{2,3,1,0:T(8,128)(2,1)} %param.11) | copy-start | bytes 55300
  29.8 0.7 %copy-start.11 = (bf16[8,64]{1,0:T(8,128)(2,1)S(1)}, bf16[8,64]{1,0:T(8,128)(2,1)}, u32[]{:S(2)}) copy-start(bf16[8,64]{1,0:T(8,128)(2,1)} %projection.1) | copy-start | bytes 3076
  31.2 0.8 %copy-start.7 = (f32[64,128]{1,0:T(8,128)S(1)}, f32[64,128]{1,0:T(8,128)}, u32[]{:S(2)}) copy-start(f32[64,128]{1,0:T(8,128)} %copy-done.6) | copy-start | bytes 98308

commit v2 on v1

--- a/solution.py
+++ b/solution.py
@@ -10,7 +10,7 @@
 HALO = 4
 GAP = 8
 POLAR = 3
-TOP = 2
+PLACES = 16
 
 
 def from_behind(block, axis, distance):
@@ -19,13 +19,53 @@
     return lax.ppermute(block, axis, route)
 
 
+def pack_kernel(fields_hbm, table_hbm, parcels, fields, table, sems):
+    channels, rows, _ = fields.shape
+    devices, depth, columns = parcels.shape
+    depth = rows * channels
+    copies = [
+        pltpu.make_async_copy(fields_hbm, fields, sems.at[0]),
+        pltpu.make_async_copy(table_hbm, table, sems.at[1]),
+    ]
+    for copy in copies:
+        copy.start()
+    copies[1].wait()
+    lines = [table[0, : 2 * POLAR, :], lax.rem(table[1, : 2 * POLAR, :], columns)]
+    lines.append(jnp.zeros((PLACES - 4 * POLAR, columns), jnp.int32))
+    lines = jnp.concatenate(lines, axis=0).astype(F32).astype(BF16)
+    for target in range(devices):
+        parcels[target, 2 * depth :, :] = lines
+    copies[0].wait()
+    values = fields[...].astype(F32)
+    for row in range(rows):
+        line = values[:, row, :].astype(BF16)
+        for target in range(devices):
+            piece = line[:, target * columns : (target + 1) * columns]
+            opposite = (target + devices // 2) % devices
+            parcels[target, row * channels : (row + 1) * channels, :] = piece
+            parcels[opposite, depth + row * channels : depth + (row + 1) * channels, :] = piece
+
+
+def pack(fields, table, devices):
+    channels, rows, _ = fields.shape
+    args = (fields, table)
+    return pl.pallas_call(
+        pack_kernel,
+        in_specs=[pl.BlockSpec(memory_space=pltpu.HBM)] * 2,
+        out_shape=jax.ShapeDtypeStruct((devices, 2 * rows * channels + PLACES, table.shape[2]), BF16),
+        scratch_shapes=[pltpu.VMEM(a.shape, a.dtype) for a in args] + [pltpu.SemaphoreType.DMA((2,))],
+        compiler_params=pltpu.CompilerParams(vmem_limit_bytes=16 * 2**20),
+        name="pack",
+    )(*[pltpu.with_memory_space_constraint(a, pltpu.HBM) for a in args])
+
+
 def tap(kernel_ref, row, col):
     if 0 <= row < 3 and 0 <= col < 3:
         return kernel_ref[row, col].astype(F32)
     return jnp.zeros(kernel_ref.shape[2:], F32)
 
 
-def arrange_kernel(first, second, down, coarse, up, merge, projection, w1, w2, wd, wc, wu, wm, wp):
+def arrange(first, second, down, coarse, up, merge, projection, w1, w2, wd, wc, wu, wm, wp):
     channels = second.shape[3]
     inputs = first.shape[2]
     for half in range(2):
@@ -71,29 +111,10 @@
     wp[...] = jnp.concatenate(lines, axis=0).astype(BF16)
 
 
-def arrange(first, second, down, coarse, up, merge, projection):
-    channels, wide = second.shape[3], coarse.shape[3]
-    shapes = (
-        (16 * first.shape[3], 4 * channels),
-        (16 * channels, 4 * channels),
-        (12 * channels, wide),
-        (9 * wide, wide),
-        (4 * wide, 4 * channels),
-        (32 * channels, 4 * channels),
-        (4 * projection.shape[0], 4 * channels),
-    )
-    return pl.pallas_call(
-        arrange_kernel,
-        out_shape=[jax.ShapeDtypeStruct(s, BF16) for s in shapes],
-        compiler_params=pltpu.CompilerParams(vmem_limit_bytes=16 * 2**20),
-        name="arrange_weights",
-    )(jnp.swapaxes(first, 2, 3), second, jnp.swapaxes(down, 2, 3), coarse, up, merge, projection)
-
-
-def locate_kernel(table, onehot, source):
-    _, grid_rows, columns = table.shape
+def locate(rows, cols, onehot, source):
+    grid_rows, columns = rows.shape
     half = columns // 2
-    code = table[0] * columns + lax.rem(table[1], columns)
+    code = rows * columns + cols
     lane = lax.broadcasted_iota(jnp.int32, (grid_rows, columns), 1)
     odd = [jnp.take_along_axis(code, lax.rem(lane, half) * 2 + q, axis=1) for q in range(2)]
     left = lax.broadcasted_iota(jnp.int32, (1, columns), 1) < half
@@ -111,55 +132,108 @@
                 ).astype(BF16)
 
 
-def locate(table):
-    _, grid_rows, columns = table.shape
+def prepare_kernel(*refs):
+    args, outs, scratch, sems = refs[:8], refs[8:17], refs[17:25], refs[25]
+    copies = [
+        pltpu.make_async_copy(source, target, sems.at[n]) for n, (source, target) in enumerate(zip(args, scratch))
+    ]
+    for copy in copies:
+        copy.start()
+    copies[0].wait()
+    table = scratch[0]
+    locate(table[0], lax.rem(table[1], table.shape[2]), *outs[:2])
+    for copy in copies[1:]:
+        copy.wait()
+    arrange(*scratch[1:], *outs[2:])
+
+
+def prepare(table, first, second, down, coarse, up, merge, projection):
+    channels, wide = second.shape[3], coarse.shape[3]
+    columns = table.shape[2]
+    pairs = table.shape[1] // 4
+    shapes = (
+        (16 * first.shape[3], 4 * channels),
+        (16 * channels, 4 * channels),
+        (12 * channels, wide),
+        (9 * wide, wide),
+        (4 * wide, 4 * channels),
+        (32 * channels, 4 * channels),
+        (4 * projection.shape[0], 4 * channels),
+    )
+    args = (table, jnp.swapaxes(first, 2, 3), second, jnp.swapaxes(down, 2, 3), coarse, up, merge, projection)
     return pl.pallas_call(
-        locate_kernel,
+        prepare_kernel,
+        in_specs=[pl.BlockSpec(memory_space=pltpu.HBM)] * 8,
         out_shape=[
-            jax.ShapeDtypeStruct((grid_rows // 4 * 2 * columns, 4 * columns), BF16),
-            jax.ShapeDtypeStruct((grid_rows, columns), jnp.int32),
-        ],
+            jax.ShapeDtypeStruct((pairs * 2 * columns, 4 * columns), BF16),
+            jax.ShapeDtypeStruct((pairs * 4, columns), jnp.int32),
+        ]
+        + [jax.ShapeDtypeStruct(s, BF16) for s in shapes],
+        scratch_shapes=[pltpu.VMEM(a.shape, a.dtype) for a in args] + [pltpu.SemaphoreType.DMA((8,))],
         compiler_params=pltpu.CompilerParams(vmem_limit_bytes=16 * 2**20),
-        name="locate",
-    )(table)
-
-
-def remap(block, onehot, source, pairs):
+        name="prepare",
+    )(*[pltpu.with_memory_space_constraint(a, pltpu.HBM) for a in args])
+
+
+def remap_kernel(block, onehot, source, cells, to_left, to_right, skip, polar_onehot, polar_source):
     devices, depth, columns = block.shape
+    depth = (depth - PLACES) // 2
     channels = depth // 2
+    opposite = lax.rem(lax.axis_index("lon") + devices // 2, devices)
+    places = block[opposite, 2 * depth :, :].astype(F32).astype(jnp.int32)
+    blank = jnp.zeros((polar_source.shape[0] - 2 * POLAR, columns), jnp.int32)
+    rows = jnp.concatenate([places[: 2 * POLAR], blank], axis=0)
+    cols = jnp.concatenate([places[2 * POLAR : 4 * POLAR], blank], axis=0)
+    locate(rows, cols, polar_onehot, polar_source)
     half = columns // 2
-    count = len(pairs)
-
-    def kernel(block, onehot, source, cells, to_left, to_right, skip):
-        upper = block[:, 0:channels, :].reshape(devices * channels, columns)
-        lower = block[:, channels:depth, :].reshape(devices * channels, columns)
-        fields = jnp.concatenate([upper, lower], axis=1)
-        for at, pair in enumerate(pairs):
-            chosen = onehot[pair * 2 * columns : (pair + 1) * 2 * columns, :]
-            found = jnp.dot(fields, chosen, preferred_element_type=F32)
-            lines = []
-            for n in range(4):
-                own = jnp.broadcast_to(source[4 * pair + n : 4 * pair + n + 1, :], (channels, columns))
-                total = jnp.zeros((channels, columns), F32)
-                for s in range(devices):
-                    value = found[s * channels : (s + 1) * channels, n * columns : (n + 1) * columns]
-                    total = jnp.where(own == s, value, total)
-                lines.append(total)
-                skip[(at * 4 + n) * 8 : (at * 4 + n + 1) * 8, :] = total[:8]
-            turned = jnp.concatenate(lines + lines, axis=0).T
-            cells[at * columns : (at + 1) * columns, :] = turned.astype(BF16)
-            for i in range(2):
-                row = (at * 2 + i) * HALO
-                to_left[row : row + HALO, :] = turned[i * half : i * half + HALO]
-                to_right[row : row + HALO, :] = turned[(i + 1) * half - HALO : (i + 1) * half]
-
+    fields = []
+    for side in range(2):
+        at = side * depth
+        upper = block[:, at : at + channels, :].reshape(devices * channels, columns)
+        lower = block[:, at + channels : at + depth, :].reshape(devices * channels, columns)
+        fields.append(jnp.concatenate([upper, lower], axis=1))
+    pairs = cells.shape[0] // columns
+    own_pairs = skip.shape[0] // 32
+    for pair in range(pairs):
+        own = pair < own_pairs
+        at = pair if own else pair - own_pairs
+        chosen = (onehot if own else polar_onehot)[at * 2 * columns : (at + 1) * 2 * columns, :]
+        found = jnp.dot(fields[0 if own else 1], chosen, preferred_element_type=F32)
+        lines = []
+        for n in range(4):
+            line = (source if own else polar_source)[4 * at + n : 4 * at + n + 1, :]
+            line = jnp.broadcast_to(line, (channels, columns))
+            total = jnp.zeros((channels, columns), F32)
+            for s in range(devices):
+                value = found[s * channels : (s + 1) * channels, n * columns : (n + 1) * columns]
+                total = jnp.where(line == s, value, total)
+            lines.append(total)
+            if own:
+                skip[(pair * 4 + n) * 8 : (pair * 4 + n + 1) * 8, :] = total[:8]
+        turned = jnp.concatenate(lines + lines, axis=0).T
+        cells[pair * columns : (pair + 1) * columns, :] = turned.astype(BF16)
+        for i in range(2):
+            row = (pair * 2 + i) * HALO
+            to_left[row : row + HALO, :] = turned[i * half : i * half + HALO]
+            to_right[row : row + HALO, :] = turned[(i + 1) * half - HALO : (i + 1) * half]
+
+
+def remap(block, onehot, source):
+    columns = block.shape[2]
+    own_rows = source.shape[0]
+    polar_rows = 4 * ((POLAR + 1) // 2)
+    count = (own_rows + polar_rows) // 4
     return pl.pallas_call(
-        kernel,
+        remap_kernel,
         out_shape=[
             jax.ShapeDtypeStruct((count * columns, columns), BF16),
             jax.ShapeDtypeStruct((count * 2 * HALO, columns), F32),
             jax.ShapeDtypeStruct((count * 2 * HALO, columns), F32),
-            jax.ShapeDtypeStruct((count * 32, columns), F32),
+            jax.ShapeDtypeStruct((own_rows * 8, columns), F32),
+        ],
+        scratch_shapes=[
+            pltpu.VMEM((polar_rows // 4 * 2 * columns, 4 * columns), BF16),
+            pltpu.VMEM((polar_rows, columns), jnp.int32),
         ],
         compiler_params=pltpu.CompilerParams(vmem_limit_bytes=16 * 2**20),
         name="remap",
@@ -177,8 +251,7 @@
 
 
 def network_kernel(
-    cells_top, cells_rest, left, right, across, skip_top, skip_rest,
-    w1, w2, wd, wc, wu, wm, wp, out, x0, y0, y1, y2, yc, yo, yu,
+    cells, left, right, skip, w1, w2, wd, wc, wu, wm, wp, out, x0, y0, y1, y2, yc, yo, yu
 ):
     half = out.shape[2] // 2
     blocks = out.shape[1] // 2
@@ -200,16 +273,9 @@
         return lax.rem(lax.div(lax.broadcasted_iota(jnp.int32, (rows, 128), 1), width), 2) == 0
 
     x0[...] = jnp.zeros_like(x0)
-    rows_of_top = cells_top.shape[0] // half
     for i in range(blocks + polar):
         base = (1 + i if i < blocks else pole + 1 + i - blocks) * step
-        if i >= blocks:
-            own = across[(i - blocks) * half : (i - blocks + 1) * half, :]
-        elif i < rows_of_top:
-            own = cells_top[i * half : (i + 1) * half, :]
-        else:
-            own = cells_rest[(i - rows_of_top) * half : (i - rows_of_top + 1) * half, :]
-        x0[base : base + half, :] = own.astype(F32)
+        x0[base : base + half, :] = cells[i * half : (i + 1) * half, :].astype(F32)
         x0[base + half : base + half + HALO, :] = right[i * HALO : (i + 1) * HALO, :]
         x0[base + step - HALO : base + step, :] = left[i * HALO : (i + 1) * HALO, :]
     x0[at(top), :] = pltpu.roll(x0[at(pole + 1), :], 32, 1)
@@ -286,8 +352,7 @@
         update = lax.dot_general(wp[...], merged, (((1,), (1,)), ((), ())), preferred_element_type=F32)
         for n in range(group // 2):
             pair = (row - 1) // 2 + n
-            skip, place = (skip_top, pair) if pair < TOP else (skip_rest, pair - TOP)
-            total = update[:, n * 2 * half : (n + 1) * 2 * half] + skip[place * 32 : (place + 1) * 32, :]
+            total = update[:, n * 2 * half : (n + 1) * 2 * half] + skip[pair * 32 : (pair + 1) * 32, :]
             for i in range(2):
                 spread = lax.div(lane, 2) + i * half
                 for p in range(2):
@@ -296,7 +361,7 @@
                     out[:, 4 * pair + 2 * i + p, :] = jnp.where(even, evens, odds)
 
 
-def network(out_shape, cells_top, cells_rest, left, right, across, skip_top, skip_rest, weights):
+def network(out_shape, cells, left, right, skip, weights):
     step = out_shape[2] // 2 + 2 * HALO + GAP
     rows = (out_shape[1] // 2 + 2 + POLAR + 2) * step
     vmem = pltpu.VMEM
@@ -312,9 +377,9 @@
             vmem((rows, 256), BF16),
             vmem((rows, 512), BF16),
         ],
-        compiler_params=pltpu.CompilerParams(vmem_limit_bytes=40 * 2**20),
+        compiler_params=pltpu.CompilerParams(vmem_limit_bytes=24 * 2**20),
         name="network",
-    )(cells_top, cells_rest, left, right, across, skip_top, skip_rest, *weights)
+    )(cells, left, right, skip, *weights)
 
 
 def shards(
@@ -330,25 +395,15 @@
 ):
     _, grid_rows, columns = remap_table.shape
     count = lax.axis_size("lon")
-    channels, rows, _ = latlon_fields.shape
-    half = columns // 2
-    parcels = latlon_fields.reshape(channels, rows, count, columns).transpose(2, 1, 0, 3)
-    parcels = parcels.reshape(count, rows * channels, columns)
+    parcels = pack(latlon_fields, remap_table, count)
     block = lax.all_to_all(parcels, "lon", split_axis=0, concat_axis=0, tiled=True)
-    weights = arrange(
-        kernel_first, kernel_second, kernel_down, kernel_coarse, kernel_up, kernel_merge, projection
+    onehot, source, *weights = prepare(
+        remap_table, kernel_first, kernel_second, kernel_down, kernel_coarse, kernel_up, kernel_merge, projection
     )
-    onehot, source = locate(remap_table)
-    cells_top, left_top, right_top, skip_top = remap(block, onehot, source, range(TOP))
-    across = from_behind(cells_top[: POLAR * half], "lon", count // 2)
-    cells_rest, left_rest, right_rest, skip_rest = remap(block, onehot, source, range(TOP, grid_rows // 4))
-    polar = across.reshape(POLAR, half, -1).astype(F32)
-    to_left = jnp.concatenate([left_top, left_rest, polar[:, :HALO].reshape(POLAR * HALO, -1)], axis=0)
-    to_right = jnp.concatenate([right_top, right_rest, polar[:, half - HALO :].reshape(POLAR * HALO, -1)], axis=0)
+    cells, to_left, to_right, skip = remap(block, onehot, source)
     left = from_behind(to_right, "lon", 1)
     right = from_behind(to_left, "lon", -1)
-    out_shape = (projection.shape[0], grid_rows, columns)
-    return network(out_shape, cells_top, cells_rest, left, right, across, skip_top, skip_rest, weights)
+    return network((projection.shape[0], grid_rows, columns), cells, left, right, skip, weights)
 
 
 def solution(mesh):

time: 39.8 us -> 35.3 us (0.89)
  local copies, waits for them, and re-layouts: 6.5 us -> 3.53 us
  Pallas kernels: 9.9 us -> 12.7 us
  waiting for transfers between devices: 9.01 us -> 6.83 us
  other arithmetic: 1.49 us -> 0 us
    pallas_call x4 -> x3, Pallas kernels: 2.55 us -> 5.37 us  [the longest x1 2.42 us: prepare(): pl.pallas_call(prepare_kernel, in_specs=[pl.BlockSpec(memory_space=pltpu....]
    reshape x4 -> x0, local copies, waits for them, and re-layouts: 1.72 us -> none  [the longest x2 1.7 us: shards(): latlon_fields.reshape(channels, rows, count, columns).transpose(2, 1, 0, 3)]
    concatenate x2 -> x0, other arithmetic: 1.49 us -> none  [the longest x1 0.74 us: shards(): jnp.concatenate([right_top, right_rest, polar[:, half - HALO:].reshape(PO...]
    unnamed x24 -> x20, local copies, waits for them, and re-layouts: 4.77 us -> 3.53 us
    all_to_all x1, waiting for transfers between devices: 6.32 us -> 5.15 us  [shards(): lax.all_to_all(parcels, 'lon', split_axis=0, concat_axis=0, tiled=True)]
    ppermute x3 -> x2, waiting for transfers between devices: 2.69 us -> 1.68 us  [from_behind(): return lax.ppermute(block, axis, route)]
    ppermute x3 -> x2, starting transfers between devices: 4.86 us -> 4.49 us  [from_behind(): return lax.ppermute(block, axis, route)]
  transfers between devices with their start and end apart: 4 -> 3, of which waited for: 2 -> 2; matrix products, arithmetic and copies ran while one was open for 2% -> 0% of each run, Pallas kernels for 5% -> 7%
where the time goes in v2:
time: 35.3 us; the launch traced here: 35.1 us
  Pallas kernels  12.7 us (36%)
  starting transfers between devices  11.9 us (34%)
  waiting for transfers between devices  6.83 us (19%)
  local copies, waits for them, and re-layouts  3.53 us (10%)
    all_to_all x1, starting transfers between devices, shards(): lax.all_to_all(parcels, 'lon', split_axis=0, concat_axis=0, tiled=True)  7.4 us
    pallas_call x1, Pallas kernels, network(): pl.pallas_call(network_kernel, out_shape=jax.ShapeDtypeStruct(out_shape,...  7.36 us
    all_to_all x1, waiting for transfers between devices, shards(): lax.all_to_all(parcels, 'lon', split_axis=0, concat_axis=0, tiled=True)  5.15 us
    ppermute x2, starting transfers between devices, from_behind(): return lax.ppermute(block, axis, route)  4.49 us
    unnamed x20, local copies, waits for them, and re-layouts  3.53 us
    pallas_call x1, Pallas kernels, prepare(): pl.pallas_call(prepare_kernel, in_specs=[pl.BlockSpec(memory_space=pltpu....  2.42 us
    pallas_call x1, Pallas kernels, pack(): pl.pallas_call(pack_kernel, in_specs=[pl.BlockSpec(memory_space=pltpu.HBM...  1.99 us
    ppermute x2, waiting for transfers between devices, from_behind(): return lax.ppermute(block, axis, route)  1.68 us
  transfers between devices with their start and end apart: 3, of which 2 were waited for; matrix products, arithmetic and copies ran while one was open for 0% of the time, Pallas kernels for 7%

profile of v2, /device:TPU:0, one launch (start us, length us, event | category | flops | bytes accessed | tf_op | source)
XLA Modules:
  0.0 35.1 jit_solution(4010502816002743176)
XLA Ops:
  0.0 2.0 %pack.1 = bf16[16,80,128]{2,1,0:T(8,128)(2,1)} custom-call(bf16[16,2,2048]{2,1,0:T(2,128)(2,1)} %fields_hbm.1, s32[2,32,128]{2,1,0:T(8,128)} %refs_0_.1), custom_call_target="tpu_custom_call" | custom-call | tf_op jit(solution)/shard_map/pack/pallas_call | solution.py:52
  2.0 7.4 %all-to-all-start = ((bf16[16,80,128]{2,1,0:T(8,128)(2,1)}), bf16[16,80,128]{2,1,0:T(8,128)(2,1)S(1)}, u32[]{:S(2)}, u32[]{:S(2)}) async-start(bf16[16,80,128]{2,1,0:T(8,128)(2,1)} %pack.1), calls=%async_computation | async-start | bytes 655360 | tf_op jit(solution)/shard_map/all_to_all | solution.py:399
  9.4 2.4 %prepare.1 = (bf16[2048,512]{1,0:T(8,128)(2,1)S(1)}, s32[32,128]{1,0:T(8,128)S(1)}, bf16[256,256]{1,0:T(8,128)(2,1)S(1)}, bf16[1024,256]{1,0:T(8,128)(2,1)S(1)},...) custom-call(s32[2,32,128]{2,1,0:T(8,128)} %refs_0_.1, ...), custom_call_target="tpu_custom_call" | custom-call | tf_op jit(solution)/shard_map/prepare/pallas_call | solution.py:164
  11.8 0.0 copy-start
  11.8 0.8 %copy-done = bf16[1024,256]{1,0:T(8,128)(2,1)} copy-done((bf16[1024,256]{1,0:T(8,128)(2,1)}, bf16[1024,256]{1,0:T(8,128)(2,1)S(1)}, u32[]{:S(2)}) %copy-start) | copy-done | bytes 524312
  12.6 0.0 copy-start.2
  12.6 0.7 %copy-done.2 = bf16[1152,128]{1,0:T(8,128)(2,1)} copy-done((bf16[1152,128]{1,0:T(8,128)(2,1)}, bf16[1152,128]{1,0:T(8,128)(2,1)S(1)}, u32[]{:S(2)}) %copy-start.2) | copy-done | bytes 294936
  13.3 0.0 copy-start.4
  13.3 0.7 %copy-done.4 = bf16[512,256]{1,0:T(8,128)(2,1)} copy-done((bf16[512,256]{1,0:T(8,128)(2,1)}, bf16[512,256]{1,0:T(8,128)(2,1)S(1)}, u32[]{:S(2)}) %copy-start.4) | copy-done | bytes 262168
  14.0 0.7 %copy-done.6 = bf16[768,128]{1,0:T(8,128)(2,1)} copy-done((bf16[768,128]{1,0:T(8,128)(2,1)}, bf16[768,128]{1,0:T(8,128)(2,1)S(1)}, u32[]{:S(2)}) %copy-start.6) | copy-done | bytes 196632
  14.7 0.7 %copy-done.8 = bf16[256,256]{1,0:T(8,128)(2,1)} copy-done((bf16[256,256]{1,0:T(8,128)(2,1)}, bf16[256,256]{1,0:T(8,128)(2,1)S(1)}, u32[]{:S(2)}) %copy-start.8) | copy-done | bytes 131096
  15.4 5.1 %all-to-all-done.block = bf16[16,80,128]{2,1,0:T(8,128)(2,1)S(1)} async-done(((bf16[16,80,128]{2,1,0:T(8,128)(2,1)}), bf16[16,80,128]{2,1,0:T(8,128)(2,1)S(1)}, u32[]{:S(2)}, u32[]{:S(2)}) %all-to-all-start) | async-done | bytes 327712 | tf_op jit(solution)/shard_map/all_to_all | solution.py:399
  20.5 0.0 copy-start.9
  20.5 1.0 %remap.1 = (bf16[1280,128]{1,0:T(8,128)(2,1)S(1)}, f32[80,128]{1,0:T(8,128)S(1)}, f32[80,128]{1,0:T(8,128)S(1)}, f32[256,128]{1,0:T(8,128)S(1)}) custom-call(bf16[16,80,128]{2,1,0:T(8,128)(2,1)S(1)} %all-to-all-done.block, bf16[2048,512]{1,0:T(8,128)(2,1)S(1)} %get-tuple-element.18.onehot, s32[32,128]{1,0:T(8,128)S(1)} %get-tuple-element.19.source), custom_call_target="tpu_custom_call" | custom-call | tf_op jit(solution)/shard_map/remap/pallas_call | solution.py:226
  21.5 0.2 collective-permute-start
  21.6 4.3 %collective-permute-start.1 = (f32[80,128]{1,0:T(8,128)S(1)}, f32[80,128]{1,0:T(8,128)S(1)}, u32[]{:S(2)}, u32[]{:S(2)}) collective-permute-start(f32[80,128]{1,0:T(8,128)S(1)} %get-tuple-element.22), channel_id=1, source_target_pairs={{1,0},{2,1},{3,2},{4,3},{5,4},{6,5},{7,6},{8,7},{9,8},{10,9},{11,1... | collective-permute-start | bytes 122888 | tf_op jit(solution)/shard_map/ppermute | solution.py:19
  26.0 1.7 %collective-permute-done.left = f32[80,128]{1,0:T(8,128)S(1)} collective-permute-done((f32[80,128]{1,0:T(8,128)S(1)}, f32[80,128]{1,0:T(8,128)S(1)}, u32[]{:S(2)}, u32[]{:S(2)}) %collective-permute-start) | collective-permute-done | bytes 40992 | tf_op jit(solution)/shard_map/ppermute | solution.py:19
  27.7 0.0 collective-permute-done.1.right
  27.7 0.0 copy-done.1
  27.7 0.0 copy-done.3
  27.7 0.0 copy-done.5
  27.7 0.0 copy-done.7
  27.7 0.0 copy-done.9
  27.7 7.4 %network.1 = f32[8,32,128]{2,1,0:T(8,128)} custom-call(bf16[1280,128]{1,0:T(8,128)(2,1)S(1)} %get-tuple-element.20.cells, f32[80,128]{1,0:T(8,128)S(1)} %collective-permute-done.left, f32[80,128]{1,0:T(8,128)S(1)} %collective-permute-done.1.right, f32[256,128]{1,0:T(8,128)S(1)} %get-tuple-element.23.skip, bf16[256,256]{1,0:T(8,128)(2,1)S(1)} %copy-done.9, ...), custom_call_target="tpu_custom_call" | custom-call | tf_op jit(solution)/shard_map/network/pallas_call | solution.py:368
  (6 shorter events, 0.0 us)
Async XLA Ops:
  2.0 18.5 %all-to-all-start = ((bf16[16,80,128]{2,1,0:T(8,128)(2,1)}), bf16[16,80,128]{2,1,0:T(8,128)(2,1)S(1)}, u32[]{:S(2)}, u32[]{:S(2)}) async-start(bf16[16,80,128]{2,1,0:T(8,128)(2,1)} %pack.1), calls=%async_computation | async-start | bytes 655360 | tf_op jit(solution)/shard_map/all_to_all | solution.py:399
  11.8 0.8 %copy-start = (bf16[1024,256]{1,0:T(8,128)(2,1)}, bf16[1024,256]{1,0:T(8,128)(2,1)S(1)}, u32[]{:S(2)}) copy-start(bf16[1024,256]{1,0:T(8,128)(2,1)S(1)} %get-tuple-element.25.w2) | copy-start | bytes 1572868
  12.6 0.7 %copy-start.2 = (bf16[1152,128]{1,0:T(8,128)(2,1)}, bf16[1152,128]{1,0:T(8,128)(2,1)S(1)}, u32[]{:S(2)}) copy-start(bf16[1152,128]{1,0:T(8,128)(2,1)S(1)} %get-tuple-element.27.wc) | copy-start | bytes 884740
  13.3 0.7 %copy-start.4 = (bf16[512,256]{1,0:T(8,128)(2,1)}, bf16[512,256]{1,0:T(8,128)(2,1)S(1)}, u32[]{:S(2)}) copy-start(bf16[512,256]{1,0:T(8,128)(2,1)S(1)} %get-tuple-element.28.wu) | copy-start | bytes 786436
  14.0 0.7 %copy-start.6 = (bf16[768,128]{1,0:T(8,128)(2,1)}, bf16[768,128]{1,0:T(8,128)(2,1)S(1)}, u32[]{:S(2)}) copy-start(bf16[768,128]{1,0:T(8,128)(2,1)S(1)} %get-tuple-element.26.wd) | copy-start | bytes 589828
  14.7 0.7 %copy-start.8 = (bf16[256,256]{1,0:T(8,128)(2,1)}, bf16[256,256]{1,0:T(8,128)(2,1)S(1)}, u32[]{:S(2)}) copy-start(bf16[256,256]{1,0:T(8,128)(2,1)S(1)} %get-tuple-element.24.w1) | copy-start | bytes 393220
  20.5 7.2 %copy-start.1 = (bf16[1024,256]{1,0:T(8,128)(2,1)S(1)}, bf16[1024,256]{1,0:T(8,128)(2,1)}, u32[]{:S(2)}) copy-start(bf16[1024,256]{1,0:T(8,128)(2,1)} %copy-done) | copy-start | bytes 1572868
  20.5 7.2 %copy-start.3 = (bf16[1152,128]{1,0:T(8,128)(2,1)S(1)}, bf16[1152,128]{1,0:T(8,128)(2,1)}, u32[]{:S(2)}) copy-start(bf16[1152,128]{1,0:T(8,128)(2,1)} %copy-done.2) | copy-start | bytes 884740
  20.5 7.2 %copy-start.5 = (bf16[512,256]{1,0:T(8,128)(2,1)S(1)}, bf16[512,256]{1,0:T(8,128)(2,1)}, u32[]{:S(2)}) copy-start(bf16[512,256]{1,0:T(8,128)(2,1)} %copy-done.4) | copy-start | bytes 786436
  20.5 7.2 %copy-start.7 = (bf16[768,128]{1,0:T(8,128)(2,1)S(1)}, bf16[768,128]{1,0:T(8,128)(2,1)}, u32[]{:S(2)}) copy-start(bf16[768,128]{1,0:T(8,128)(2,1)} %copy-done.6) | copy-start | bytes 589828
  20.5 7.2 %copy-start.9 = (bf16[256,256]{1,0:T(8,128)(2,1)S(1)}, bf16[256,256]{1,0:T(8,128)(2,1)}, u32[]{:S(2)}) copy-start(bf16[256,256]{1,0:T(8,128)(2,1)} %copy-done.8) | copy-start | bytes 393220
  21.5 6.2 %collective-permute-start = (f32[80,128]{1,0:T(8,128)S(1)}, f32[80,128]{1,0:T(8,128)S(1)}, u32[]{:S(2)}, u32[]{:S(2)}) collective-permute-start(f32[80,128]{1,0:T(8,128)S(1)} %get-tuple-element.21), channel_id=1, source_target_pairs={{15,0},{0,1},{1,2},{2,3},{3,4},{4,5},{5,6},{6,7},{7,8},{8,9},{9,10... | collective-permute-start | bytes 122888 | tf_op jit(solution)/shard_map/ppermute | solution.py:19
  21.6 6.0 %collective-permute-start.1 = (f32[80,128]{1,0:T(8,128)S(1)}, f32[80,128]{1,0:T(8,128)S(1)}, u32[]{:S(2)}, u32[]{:S(2)}) collective-permute-start(f32[80,128]{1,0:T(8,128)S(1)} %get-tuple-element.22), channel_id=1, source_target_pairs={{1,0},{2,1},{3,2},{4,3},{5,4},{6,5},{7,6},{8,7},{9,8},{10,9},{11,1... | collective-permute-start | bytes 122888 | tf_op jit(solution)/shard_map/ppermute | solution.py:19

commit v3 on v2

--- a/solution.py
+++ b/solution.py
@@ -8,15 +8,14 @@
 F32 = jnp.float32
 BF16 = jnp.bfloat16
 HALO = 4
-GAP = 8
 POLAR = 3
 PLACES = 16
 
 
-def from_behind(block, axis, distance):
-    devices = range(lax.axis_size(axis))
-    route = [((i - distance) % len(devices), i) for i in devices]
-    return lax.ppermute(block, axis, route)
+def swap(block, axis, first):
+    devices = lax.axis_size(axis)
+    pairs = [((first + i) % devices, (first + i + 1) % devices) for i in range(0, devices, 2)]
+    return lax.ppermute(block, axis, pairs + [(b, a) for a, b in pairs])
 
 
 def pack_kernel(fields_hbm, table_hbm, parcels, fields, table, sems):
@@ -175,7 +174,8 @@
     )(*[pltpu.with_memory_space_constraint(a, pltpu.HBM) for a in args])
 
 
-def remap_kernel(block, onehot, source, cells, to_left, to_right, skip, polar_onehot, polar_source):
+def remap_kernel(block, onehot, source, cells, inner, outer, skip, polar_onehot, polar_source):
+    even = lax.rem(lax.axis_index("lon"), 2) == 0
     devices, depth, columns = block.shape
     depth = (depth - PLACES) // 2
     channels = depth // 2
@@ -214,8 +214,10 @@
         cells[pair * columns : (pair + 1) * columns, :] = turned.astype(BF16)
         for i in range(2):
             row = (pair * 2 + i) * HALO
-            to_left[row : row + HALO, :] = turned[i * half : i * half + HALO]
-            to_right[row : row + HALO, :] = turned[(i + 1) * half - HALO : (i + 1) * half]
+            begin = turned[i * half : i * half + HALO]
+            finish = turned[(i + 1) * half - HALO : (i + 1) * half]
+            inner[row : row + HALO, :] = jnp.where(even, finish, begin)
+            outer[row : row + HALO, :] = jnp.where(even, begin, finish)
 
 
 def remap(block, onehot, source):
@@ -250,48 +252,43 @@
     return rows[0] if len(rows) == 1 else jnp.concatenate(rows, axis=0)
 
 
-def network_kernel(
-    cells, left, right, skip, w1, w2, wd, wc, wu, wm, wp, out, x0, y0, y1, y2, yc, yo, yu
-):
-    half = out.shape[2] // 2
-    blocks = out.shape[1] // 2
-    step = half + 2 * HALO + GAP
-    polar = POLAR
-    top = 0
-    bottom = blocks + 1
-    pole = blocks + 2
-    end = pole + polar + 1
-    group = 4
-
-    def at(row, count=1):
-        return slice(row * step, (row + count) * step)
-
-    def chunks(polar_rows):
-        return [(1 + i, group) for i in range(0, blocks, group)] + [(pole + 1, polar_rows)]
-
-    def lane_mask(rows, width):
-        return lax.rem(lax.div(lax.broadcasted_iota(jnp.int32, (rows, 128), 1), width), 2) == 0
-
-    x0[...] = jnp.zeros_like(x0)
-    for i in range(blocks + polar):
-        base = (1 + i if i < blocks else pole + 1 + i - blocks) * step
-        x0[base : base + half, :] = cells[i * half : (i + 1) * half, :].astype(F32)
-        x0[base + half : base + half + HALO, :] = right[i * HALO : (i + 1) * HALO, :]
-        x0[base + step - HALO : base + step, :] = left[i * HALO : (i + 1) * HALO, :]
+class Rows:
+    def __init__(self, step, blocks):
+        self.step, self.blocks = step, blocks
+        self.top, self.bottom, self.pole = 0, blocks + 1, blocks + 2
+        self.count = blocks + 2 + POLAR + 2
+
+    def __call__(self, row, count=1):
+        return slice(row * self.step, (row + count) * self.step)
+
+    def of(self, i):
+        return 1 + i if i < self.blocks else self.pole + 1 + i - self.blocks
+
+    def mask(self, count, width):
+        lane = lax.broadcasted_iota(jnp.int32, (count * self.step, 128), 1)
+        return lax.rem(lax.div(lane, width), 2) == 0
+
+
+def product(pieces, weights):
+    return jnp.dot(jnp.concatenate(pieces, axis=1), weights[...], preferred_element_type=F32)
+
+
+def layers(at, chunks, moved, x0, y0, y1, y2, yc, yo, yu, w1, w2, wd, wc, wu):
+    step, top, bottom, pole = at.step, at.top, at.bottom, at.pole
     x0[at(top), :] = pltpu.roll(x0[at(pole + 1), :], 32, 1)
     x0[at(pole), :] = pltpu.roll(x0[at(1), :], 32, 1)
-    for row in range(0, end + 1):
+    for row in range(at.count):
         x = x0[at(row), :]
-        side = jnp.where(lane_mask(step, 16), ring(x, step, -1), ring(x, step, 1))
-        y0[at(row), :] = jnp.where(lane_mask(step, 64), x, side)
-
-    def store_fine(y, row, count, values, shift):
-        moved = ring(values, step, shift).astype(BF16)
+        side = jnp.where(at.mask(1, 16), moved("x0", row, 1, x, -1), moved("x0", row, 1, x, 1))
+        y0[at(row), :] = jnp.where(at.mask(1, 64), x, side)
+
+    def store_fine(y, name, row, count, values, shift):
+        shifted = moved(name, row, count, values, shift).astype(BF16)
         values = values.astype(BF16)
         for p in range(2):
             lanes = slice(p * 128, (p + 1) * 128)
             y[at(row, count), p * 256 : p * 256 + 128] = values[:, lanes]
-            y[at(row, count), p * 256 + 128 : p * 256 + 256] = moved[:, lanes]
+            y[at(row, count), p * 256 + 128 : p * 256 + 256] = shifted[:, lanes]
 
     def edges_fine(y, polar_rows):
         y[at(top), 256:512] = y[at(pole + 1), 0:256]
@@ -299,87 +296,200 @@
         y[at(bottom), 0:256] = jnp.zeros((step, 256), BF16)
         y[at(pole + 1 + polar_rows), 0:256] = jnp.zeros((step, 256), BF16)
 
-    def product(pieces, weights):
-        return jnp.dot(jnp.concatenate(pieces, axis=1), weights[...], preferred_element_type=F32)
-
-    for row, count in chunks(polar):
-        mask = lane_mask(count * step, 32)
-        vertical = jnp.where(mask, y0[at(row + 1, count), :], y0[at(row - 1, count), :])
+    for row, count in chunks(POLAR):
+        vertical = jnp.where(at.mask(count, 32), y0[at(row + 1, count), :], y0[at(row - 1, count), :])
         pieces = [y0[at(row, count), :].astype(BF16), vertical.astype(BF16)]
-        store_fine(y1, row, count, silu(product(pieces, w1)), 1)
-    edges_fine(y1, polar)
-
-    for row, count in chunks(polar - 1):
+        store_fine(y1, "y1", row, count, silu(product(pieces, w1)), 1)
+    edges_fine(y1, POLAR)
+
+    for row, count in chunks(POLAR - 1):
         pieces = [y1[at(row - 1, count), 256:512], y1[at(row, count), :], y1[at(row + 1, count), 0:256]]
-        store_fine(y2, row, count, silu(product(pieces, w2)), -1)
-    edges_fine(y2, polar - 1)
-
-    for row, count in chunks(polar - 1):
-        pieces = [y2[at(row - 1, count), 256:512], y2[at(row, count), :]]
-        values = silu(product(pieces, wd))
-        yc[at(row, count), 0:128] = ring(values, step, 1).astype(BF16)
+        store_fine(y2, "y2", row, count, silu(product(pieces, w2)), -1)
+    edges_fine(y2, POLAR - 1)
+
+    for row, count in chunks(POLAR - 1):
+        values = silu(product([y2[at(row - 1, count), 256:512], y2[at(row, count), :]], wd))
+        yc[at(row, count), 0:128] = moved("yc", row, count, values, 1).astype(BF16)
         yc[at(row, count), 128:256] = values.astype(BF16)
-        yc[at(row, count), 256:384] = ring(values, step, -1).astype(BF16)
+        yc[at(row, count), 256:384] = moved("yc", row, count, values, -1).astype(BF16)
     yc[at(top), :] = yc[at(pole + 1), :]
     yc[at(pole), :] = yc[at(1), :]
     yc[at(bottom), :] = jnp.zeros((step, 384), BF16)
 
-    for row, count in chunks(polar - 2):
-        pieces = [yc[at(row + a, count), :] for a in (-1, 0, 1)]
-        values = silu(product(pieces, wc))
-        yo[at(row, count), 0:128] = ring(values, step, 1).astype(BF16)
+    for row, count in chunks(POLAR - 2):
+        values = silu(product([yc[at(row + a, count), :] for a in (-1, 0, 1)], wc))
+        yo[at(row, count), 0:128] = moved("yo", row, count, values, 1).astype(BF16)
         yo[at(row, count), 128:256] = values.astype(BF16)
     yo[at(bottom), :] = jnp.zeros((step, 256), BF16)
     yo[at(pole + 2), :] = jnp.zeros((step, 256), BF16)
 
-    for row, count in chunks(polar - 2):
-        pieces = [yo[at(row, count), :], yo[at(row + 1, count), :]]
-        store_fine(yu, row, count, silu(product(pieces, wu)), -1)
-    edges_fine(yu, polar - 2)
-
+    for row, count in chunks(POLAR - 2):
+        values = silu(product([yo[at(row, count), :], yo[at(row + 1, count), :]], wu))
+        store_fine(yu, "yu", row, count, values, -1)
+    edges_fine(yu, POLAR - 2)
+
+
+def merge(at, row, count, y2, yu, wm, wp):
+    pieces = []
+    for y in (y2, yu):
+        pieces += [y[at(row - 1, count), 256:512], y[at(row, count), :], y[at(row + 1, count), 0:256]]
+    merged = silu(product(pieces, wm)).astype(BF16)
+    return lax.dot_general(wp[...], merged, (((1,), (1,)), ((), ())), preferred_element_type=F32)
+
+
+SHARED = (("y1", 256, (1,)), ("y2", 256, (-1,)), ("yc", 128, (1, -1)), ("yo", 128, (1,)), ("yu", 256, (-1,)))
+SHARED_KEYS = [(name, lanes, shift) for name, lanes, shifts in SHARED for shift in shifts]
+
+
+def inside_kernel(cells, skip, w1, w2, wd, wc, wu, wm, wp, update, rest, *refs):
+    shared, scratch = refs[: len(SHARED_KEYS)], refs[len(SHARED_KEYS) :]
+    half = update.shape[1] // 2
+    blocks = update.shape[0] // 16
+    at = Rows(half, blocks)
+    group = 4
+
+    def chunks(polar_rows):
+        return [(1 + i, group) for i in range(0, blocks, group)] + [(at.pole + 1, polar_rows)]
+
+    def moved(name, row, count, values, shift):
+        for (key, _, way), ref in zip(SHARED_KEYS, shared):
+            if key == name and way == shift:
+                column = half - HALO - 1 if shift == 1 else HALO
+                for i in range(count):
+                    ref[row + i : row + i + 1, :] = values[i * half + column : i * half + column + 1, :]
+        return ring(values, half, shift)
+
+    x0 = scratch[0]
+    for row in (at.top, at.bottom, at.pole, at.count - 1):
+        x0[at(row), :] = jnp.zeros((half, 128), F32)
+    for i in range(blocks + POLAR):
+        x0[at(at.of(i)), :] = cells[i * half : (i + 1) * half, :].astype(F32)
+    layers(at, chunks, moved, *scratch, w1, w2, wd, wc, wu)
+
+    y2, yu = scratch[3], scratch[6]
     lane = lax.broadcasted_iota(jnp.int32, (8, 2 * half), 1)
     even = lax.rem(lane, 2) == 0
+
+    def weave(values, i, p):
+        spread = lax.div(lane, 2) + i * half
+        evens = jnp.take_along_axis(values[p * 16 : p * 16 + 8], spread, axis=1)
+        odds = jnp.take_along_axis(values[p * 16 + 8 : p * 16 + 16], spread, axis=1)
+        return jnp.where(even, evens, odds)
+
     for row in range(1, 1 + blocks, group):
-
-        def own(y, offset, lanes):
-            rows = [y[(row + offset + i) * step : (row + offset + i) * step + half, lanes] for i in range(group)]
-            return jnp.concatenate(rows, axis=0)
-
-        pieces = []
-        for y in (y2, yu):
-            pieces += [own(y, -1, slice(256, 512)), own(y, 0, slice(0, 512)), own(y, 1, slice(0, 256))]
-        merged = silu(product(pieces, wm)).astype(BF16)
-        update = lax.dot_general(wp[...], merged, (((1,), (1,)), ((), ())), preferred_element_type=F32)
+        found = merge(at, row, group, y2, yu, wm, wp)
         for n in range(group // 2):
             pair = (row - 1) // 2 + n
-            total = update[:, n * 2 * half : (n + 1) * 2 * half] + skip[pair * 32 : (pair + 1) * 32, :]
+            own = found[:, n * 2 * half : (n + 1) * 2 * half]
+            base = skip[pair * 32 : (pair + 1) * 32, :]
             for i in range(2):
-                spread = lax.div(lane, 2) + i * half
                 for p in range(2):
-                    evens = jnp.take_along_axis(total[p * 16 : p * 16 + 8], spread, axis=1)
-                    odds = jnp.take_along_axis(total[p * 16 + 8 : p * 16 + 16], spread, axis=1)
-                    out[:, 4 * pair + 2 * i + p, :] = jnp.where(even, evens, odds)
-
-
-def network(out_shape, cells, left, right, skip, weights):
-    step = out_shape[2] // 2 + 2 * HALO + GAP
-    rows = (out_shape[1] // 2 + 2 + POLAR + 2) * step
-    vmem = pltpu.VMEM
+                    line = (4 * pair + 2 * i + p) * 8
+                    update[line : line + 8, :] = weave(own, i, p)
+                    rest[line : line + 8, :] = weave(base, i, p)
+
+
+def edges_kernel(cells, inner, outer, w1, w2, wd, wc, wu, wm, wp, update, rest, *refs):
+    shared, out, scratch = refs[: len(SHARED_KEYS)], refs[len(SHARED_KEYS)], refs[len(SHARED_KEYS) + 1 :]
+    even = lax.rem(lax.axis_index("lon"), 2) == 0
+    half = out.shape[2] // 2
+    blocks = out.shape[1] // 2
+    step = 4 * HALO
+    at = Rows(step, blocks)
+    place = lax.broadcasted_iota(jnp.int32, (step, 128), 0)
+    x0 = scratch[0]
+    beside = {}
+    for row in (at.top, at.bottom, at.pole, at.count - 1):
+        x0[at(row), :] = jnp.zeros((step, 128), F32)
+    for i in range(blocks + POLAR):
+        row = at.of(i)
+        begin = cells[i * half : i * half + 16, :].astype(F32)
+        finish = cells[(i + 1) * half - 16 : (i + 1) * half, :].astype(F32)
+        near = inner[i * HALO : (i + 1) * HALO, :]
+        far = outer[i * HALO : (i + 1) * HALO, :]
+        base = row * step
+        x0[base : base + HALO, :] = jnp.where(even, far, near)
+        x0[base + HALO : base + 2 * HALO, :] = begin[:HALO]
+        x0[base + 2 * HALO : base + 3 * HALO, :] = finish[16 - HALO :]
+        x0[base + 3 * HALO : base + 4 * HALO, :] = jnp.where(even, near, far)
+        beside[row] = {-1: begin[HALO : HALO + 1], 1: finish[15 - HALO : 16 - HALO]}
+    beside[at.top] = {way: pltpu.roll(line, 32, 1) for way, line in beside[at.pole + 1].items()}
+    beside[at.pole] = {way: pltpu.roll(line, 32, 1) for way, line in beside[1].items()}
+
+    def moved(name, row, count, values, shift):
+        lines = []
+        target = 2 * HALO if shift == 1 else 2 * HALO - 1
+        for i in range(count):
+            line = pltpu.roll(values[i * step : (i + 1) * step], shift % step, 0)
+            if name == "x0":
+                own = beside[row + i][shift] if row + i in beside else None
+            else:
+                ref = next(r for (key, _, way), r in zip(SHARED_KEYS, shared) if (key, way) == (name, shift))
+                own = ref[row + i : row + i + 1, :]
+            if own is not None:
+                parts = []
+                for lanes in range(0, values.shape[1], 128):
+                    fix = jnp.broadcast_to(own[:, lanes : lanes + 128], (step, 128))
+                    parts.append(jnp.where(place == target, fix, line[:, lanes : lanes + 128]))
+                line = parts[0] if len(parts) == 1 else jnp.concatenate(parts, axis=1)
+            lines.append(line)
+        return lines[0] if count == 1 else jnp.concatenate(lines, axis=0)
+
+    def chunks(polar_rows):
+        return [(1, at.pole + polar_rows)]
+
+    layers(at, chunks, moved, *scratch, w1, w2, wd, wc, wu)
+    found = merge(at, 1, blocks, scratch[3], scratch[6], wm, wp)
+
+    columns = 2 * half
+    lane = lax.broadcasted_iota(jnp.int32, (8, columns), 1)
+    first = lane < 2 * HALO
+    edge = first | (lane >= columns - 2 * HALO)
+    column = jnp.where(first, HALO + lax.div(lane, 2), 3 * HALO - lax.div(columns + 1 - lane, 2))
+    column = jnp.where(edge, column, 0)
+    odd = lax.rem(lane, 2) == 1
+    per = columns // step
+    for i in range(blocks):
+        spread = column + (i % per) * step
+        lanes = slice(i // per * columns, (i // per + 1) * columns)
+        for p in range(2):
+            evens = jnp.take_along_axis(found[p * 16 : p * 16 + 8, lanes], spread, axis=1)
+            odds = jnp.take_along_axis(found[p * 16 + 8 : p * 16 + 16, lanes], spread, axis=1)
+            h = 2 * i + p
+            line = slice(h * 8, (h + 1) * 8)
+            value = jnp.where(edge, jnp.where(odd, odds, evens), update[line, :])
+            out[:, h, :] = value + rest[line, :]
+
+
+def buffers(step, blocks):
+    rows = Rows(step, blocks).count * step
+    shapes = ((128, F32), (128, F32), (512, BF16), (512, BF16), (384, BF16), (256, BF16), (512, BF16))
+    return [pltpu.VMEM((rows, lanes), dtype) for lanes, dtype in shapes]
+
+
+def inside(cells, skip, weights):
+    columns = skip.shape[1]
+    blocks = skip.shape[0] // 16
+    rows = Rows(columns // 2, blocks).count
     return pl.pallas_call(
-        network_kernel,
+        inside_kernel,
+        out_shape=[jax.ShapeDtypeStruct((blocks * 16, columns), F32)] * 2
+        + [jax.ShapeDtypeStruct((rows, lanes), F32) for _, lanes, _ in SHARED_KEYS],
+        scratch_shapes=buffers(columns // 2, blocks),
+        compiler_params=pltpu.CompilerParams(vmem_limit_bytes=20 * 2**20),
+        cost_estimate=pl.CostEstimate(flops=4 * 10**9, bytes_accessed=4 * 10**6, transcendentals=0),
+        name="inside",
+    )(cells, skip, *weights)
+
+
+def edges(out_shape, cells, inner, outer, weights, found):
+    return pl.pallas_call(
+        edges_kernel,
         out_shape=jax.ShapeDtypeStruct(out_shape, F32),
-        scratch_shapes=[
-            vmem((rows, 128), F32),
-            vmem((rows, 128), F32),
-            vmem((rows, 512), BF16),
-            vmem((rows, 512), BF16),
-            vmem((rows, 384), BF16),
-            vmem((rows, 256), BF16),
-            vmem((rows, 512), BF16),
-        ],
-        compiler_params=pltpu.CompilerParams(vmem_limit_bytes=24 * 2**20),
-        name="network",
-    )(cells, left, right, skip, *weights)
+        scratch_shapes=buffers(4 * HALO, out_shape[1] // 2),
+        compiler_params=pltpu.CompilerParams(vmem_limit_bytes=20 * 2**20),
+        name="edges",
+    )(cells, inner, outer, *weights, *found)
 
 
 def shards(
@@ -400,10 +510,11 @@
     onehot, source, *weights = prepare(
         remap_table, kernel_first, kernel_second, kernel_down, kernel_coarse, kernel_up, kernel_merge, projection
     )
-    cells, to_left, to_right, skip = remap(block, onehot, source)
-    left = from_behind(to_right, "lon", 1)
-    right = from_behind(to_left, "lon", -1)
-    return network((projection.shape[0], grid_rows, columns), cells, left, right, skip, weights)
+    cells, inner, outer, skip = remap(block, onehot, source)
+    outer = swap(outer, "lon", 1)
+    inner = swap(inner, "lon", 0)
+    found = inside(cells, skip, weights)
+    return edges((projection.shape[0], grid_rows, columns), cells, inner, outer, weights, found)
 
 
 def solution(mesh):

time: 35.3 us -> 33.4 us (0.946)
  starting transfers between devices: 11.9 us -> 9.44 us
  Pallas kernels: 12.7 us -> 14.9 us
  waiting for transfers between devices: 6.83 us -> 5.14 us
    ppermute x2, starting transfers between devices: 4.49 us -> 2.04 us  [swap(): return lax.ppermute(block, axis, pairs + [(b, a) for a, b in pairs])]
    pallas_call x1 -> x2, Pallas kernels: 7.36 us -> 9.56 us  [the longest x1 6.1 us: inside(): pl.pallas_call(inside_kernel, out_shape=[jax.ShapeDtypeStruct((blocks * 1...]
    ppermute x2, waiting for transfers between devices: 1.68 us -> 0.01 us  [swap(): return lax.ppermute(block, axis, pairs + [(b, a) for a, b in pairs])]
  transfers between devices with their start and end apart: 3 -> 3, of which waited for: 2 -> 1; matrix products, arithmetic and copies ran while one was open for 0% -> 0% of each run, Pallas kernels for 7% -> 26%
where the time goes in v3:
time: 33.4 us; the launch traced here: 33.2 us
  Pallas kernels  14.9 us (45%)
  starting transfers between devices  9.44 us (28%)
  waiting for transfers between devices  5.14 us (15%)
  local copies, waits for them, and re-layouts  3.55 us (11%)
    all_to_all x1, starting transfers between devices, shards(): lax.all_to_all(parcels, 'lon', split_axis=0, concat_axis=0, tiled=True)  7.4 us
    pallas_call x1, Pallas kernels, inside(): pl.pallas_call(inside_kernel, out_shape=[jax.ShapeDtypeStruct((blocks * 1...  6.1 us
    all_to_all x1, waiting for transfers between devices, shards(): lax.all_to_all(parcels, 'lon', split_axis=0, concat_axis=0, tiled=True)  5.13 us
    unnamed x20, local copies, waits for them, and re-layouts  3.55 us
    pallas_call x1, Pallas kernels, edges(): pl.pallas_call(edges_kernel, out_shape=jax.ShapeDtypeStruct(out_shape, F3...  3.46 us
    pallas_call x1, Pallas kernels, prepare(): pl.pallas_call(prepare_kernel, in_specs=[pl.BlockSpec(memory_space=pltpu....  2.42 us
    ppermute x2, starting transfers between devices, swap(): return lax.ppermute(block, axis, pairs + [(b, a) for a, b in pairs])  2.04 us
    pallas_call x1, Pallas kernels, pack(): pl.pallas_call(pack_kernel, in_specs=[pl.BlockSpec(memory_space=pltpu.HBM...  2 us
  transfers between devices with their start and end apart: 3, of which 1 were waited for; matrix products, arithmetic and copies ran while one was open for 0% of the time, Pallas kernels for 26%

profile of v3, /device:TPU:0, one launch (start us, length us, event | category | flops | bytes accessed | tf_op | source)
XLA Modules:
  0.0 33.2 jit_solution(12592820258438352938)
XLA Ops:
  0.0 2.0 %pack.1 = bf16[16,80,128]{2,1,0:T(8,128)(2,1)} custom-call(bf16[16,2,2048]{2,1,0:T(2,128)(2,1)} %fields_hbm.1, s32[2,32,128]{2,1,0:T(8,128)} %refs_0_.1), custom_call_target="tpu_custom_call" | custom-call | tf_op jit(solution)/shard_map/pack/pallas_call | solution.py:51
  2.0 7.4 %all-to-all-start = ((bf16[16,80,128]{2,1,0:T(8,128)(2,1)}), bf16[16,80,128]{2,1,0:T(8,128)(2,1)S(1)}, u32[]{:S(2)}, u32[]{:S(2)}) async-start(bf16[16,80,128]{2,1,0:T(8,128)(2,1)} %pack.1), calls=%async_computation | async-start | bytes 655360 | tf_op jit(solution)/shard_map/all_to_all | solution.py:509
  9.4 2.4 %prepare.1 = (bf16[2048,512]{1,0:T(8,128)(2,1)S(1)}, s32[32,128]{1,0:T(8,128)S(1)}, bf16[256,256]{1,0:T(8,128)(2,1)S(1)}, bf16[1024,256]{1,0:T(8,128)(2,1)S(1)},...) custom-call(s32[2,32,128]{2,1,0:T(8,128)} %refs_0_.1, ...), custom_call_target="tpu_custom_call" | custom-call | tf_op jit(solution)/shard_map/prepare/pallas_call | solution.py:163
  11.8 0.0 copy-start
  11.8 0.8 %copy-done = bf16[1024,256]{1,0:T(8,128)(2,1)} copy-done((bf16[1024,256]{1,0:T(8,128)(2,1)}, bf16[1024,256]{1,0:T(8,128)(2,1)S(1)}, u32[]{:S(2)}) %copy-start) | copy-done | bytes 524312
  12.6 0.0 copy-start.2
  12.6 0.7 %copy-done.2 = bf16[1152,128]{1,0:T(8,128)(2,1)} copy-done((bf16[1152,128]{1,0:T(8,128)(2,1)}, bf16[1152,128]{1,0:T(8,128)(2,1)S(1)}, u32[]{:S(2)}) %copy-start.2) | copy-done | bytes 294936
  13.3 0.7 %copy-done.4 = bf16[512,256]{1,0:T(8,128)(2,1)} copy-done((bf16[512,256]{1,0:T(8,128)(2,1)}, bf16[512,256]{1,0:T(8,128)(2,1)S(1)}, u32[]{:S(2)}) %copy-start.4) | copy-done | bytes 262168
  14.0 0.7 %copy-done.6 = bf16[768,128]{1,0:T(8,128)(2,1)} copy-done((bf16[768,128]{1,0:T(8,128)(2,1)}, bf16[768,128]{1,0:T(8,128)(2,1)S(1)}, u32[]{:S(2)}) %copy-start.6) | copy-done | bytes 196632
  14.7 0.7 %copy-done.8 = bf16[256,256]{1,0:T(8,128)(2,1)} copy-done((bf16[256,256]{1,0:T(8,128)(2,1)}, bf16[256,256]{1,0:T(8,128)(2,1)S(1)}, u32[]{:S(2)}) %copy-start.8) | copy-done | bytes 131096
  15.4 5.1 %all-to-all-done.block = bf16[16,80,128]{2,1,0:T(8,128)(2,1)S(1)} async-done(((bf16[16,80,128]{2,1,0:T(8,128)(2,1)}), bf16[16,80,128]{2,1,0:T(8,128)(2,1)S(1)}, u32[]{:S(2)}, u32[]{:S(2)}) %all-to-all-start) | async-done | bytes 327712 | tf_op jit(solution)/shard_map/all_to_all | solution.py:509
  20.5 0.0 copy-start.9
  20.5 1.0 %remap.1 = (bf16[1280,128]{1,0:T(8,128)(2,1)S(1)}, f32[80,128]{1,0:T(8,128)S(1)}, f32[80,128]{1,0:T(8,128)S(1)}, f32[256,128]{1,0:T(8,128)S(1)}) custom-call(bf16[16,80,128]{2,1,0:T(8,128)(2,1)S(1)} %all-to-all-done.block, bf16[2048,512]{1,0:T(8,128)(2,1)S(1)} %get-tuple-element.26.onehot, s32[32,128]{1,0:T(8,128)S(1)} %get-tuple-element.27.source), custom_call_target="tpu_custom_call" | custom-call | tf_op jit(solution)/shard_map/remap/pallas_call | solution.py:228
  21.5 0.2 collective-permute-start
  21.7 1.9 %collective-permute-start.1 = (f32[80,128]{1,0:T(8,128)S(1)}, f32[80,128]{1,0:T(8,128)S(1)}, u32[]{:S(2)}, u32[]{:S(2)}) collective-permute-start(f32[80,128]{1,0:T(8,128)S(1)} %get-tuple-element.30), channel_id=1, source_target_pairs={{1,2},{3,4},{5,6},{7,8},{9,10},{11,12},{13,14},{15,0},{2,1},{4,3},... | collective-permute-start | bytes 122888 | tf_op jit(solution)/shard_map/ppermute | solution.py:18
  23.5 0.0 copy-done.1
  23.5 0.0 copy-done.3
  23.5 0.0 copy-done.5
  23.5 0.0 copy-done.7
  23.5 0.0 copy-done.9
  23.6 6.1 %inside.1 = (f32[256,128]{1,0:T(8,128)S(1)}, f32[256,128]{1,0:T(8,128)S(1)}, f32[23,256]{1,0:T(8,128)S(1)}, f32[23,256]{1,0:T(8,128)S(1)}, f32[23,128]{1,0:T(8,1...) custom-call(bf16[1280,128]{1,0:T(8,128)(2,1)S(1)} %get-tuple-element.28.cells, ...), custom_call_target="tpu_custom_call" | custom-call | flops 4000000000 | bytes 4000000 | tf_op jit(solution)/shard_map/inside/pallas_call | solution.py:474
  29.7 0.0 collective-permute-done.inner
  29.7 0.0 collective-permute-done.1.outer
  29.7 3.5 %edges.1 = f32[8,32,128]{2,1,0:T(8,128)} custom-call(bf16[1280,128]{1,0:T(8,128)(2,1)S(1)} %get-tuple-element.28.cells, f32[80,128]{1,0:T(8,128)S(1)} %collective-permute-done.inner, f32[80,128]{1,0:T(8,128)S(1)} %collective-permute-done.1.outer, bf16[256,256]{1,0:T(8,128)(2,1)S(1)} %copy-done.9, bf16[1024,256]{1,0:T(8,128)(2,1)S(1)} %copy-done.1, ...), custom_call_target="tpu_custom_call" | custom-call | tf_op jit(solution)/shard_map/edges/pallas_call | solution.py:486
  (7 shorter events, 0.0 us)
Async XLA Ops:
  2.0 18.5 %all-to-all-start = ((bf16[16,80,128]{2,1,0:T(8,128)(2,1)}), bf16[16,80,128]{2,1,0:T(8,128)(2,1)S(1)}, u32[]{:S(2)}, u32[]{:S(2)}) async-start(bf16[16,80,128]{2,1,0:T(8,128)(2,1)} %pack.1), calls=%async_computation | async-start | bytes 655360 | tf_op jit(solution)/shard_map/all_to_all | solution.py:509
  11.8 0.8 %copy-start = (bf16[1024,256]{1,0:T(8,128)(2,1)}, bf16[1024,256]{1,0:T(8,128)(2,1)S(1)}, u32[]{:S(2)}) copy-start(bf16[1024,256]{1,0:T(8,128)(2,1)S(1)} %get-tuple-element.32.w2) | copy-start | bytes 1572868
  12.6 0.7 %copy-start.2 = (bf16[1152,128]{1,0:T(8,128)(2,1)}, bf16[1152,128]{1,0:T(8,128)(2,1)S(1)}, u32[]{:S(2)}) copy-start(bf16[1152,128]{1,0:T(8,128)(2,1)S(1)} %get-tuple-element.34.wc) | copy-start | bytes 884740
  13.3 0.7 %copy-start.4 = (bf16[512,256]{1,0:T(8,128)(2,1)}, bf16[512,256]{1,0:T(8,128)(2,1)S(1)}, u32[]{:S(2)}) copy-start(bf16[512,256]{1,0:T(8,128)(2,1)S(1)} %get-tuple-element.35.wu) | copy-start | bytes 786436
  14.0 0.7 %copy-start.6 = (bf16[768,128]{1,0:T(8,128)(2,1)}, bf16[768,128]{1,0:T(8,128)(2,1)S(1)}, u32[]{:S(2)}) copy-start(bf16[768,128]{1,0:T(8,128)(2,1)S(1)} %get-tuple-element.33.wd) | copy-start | bytes 589828
  14.7 0.7 %copy-start.8 = (bf16[256,256]{1,0:T(8,128)(2,1)}, bf16[256,256]{1,0:T(8,128)(2,1)S(1)}, u32[]{:S(2)}) copy-start(bf16[256,256]{1,0:T(8,128)(2,1)S(1)} %get-tuple-element.31.w1) | copy-start | bytes 393220
  20.5 3.0 %copy-start.1 = (bf16[1024,256]{1,0:T(8,128)(2,1)S(1)}, bf16[1024,256]{1,0:T(8,128)(2,1)}, u32[]{:S(2)}) copy-start(bf16[1024,256]{1,0:T(8,128)(2,1)} %copy-done) | copy-start | bytes 1572868
  20.5 3.0 %copy-start.3 = (bf16[1152,128]{1,0:T(8,128)(2,1)S(1)}, bf16[1152,128]{1,0:T(8,128)(2,1)}, u32[]{:S(2)}) copy-start(bf16[1152,128]{1,0:T(8,128)(2,1)} %copy-done.2) | copy-start | bytes 884740
  20.5 3.0 %copy-start.5 = (bf16[512,256]{1,0:T(8,128)(2,1)S(1)}, bf16[512,256]{1,0:T(8,128)(2,1)}, u32[]{:S(2)}) copy-start(bf16[512,256]{1,0:T(8,128)(2,1)} %copy-done.4) | copy-start | bytes 786436
  20.5 3.0 %copy-start.7 = (bf16[768,128]{1,0:T(8,128)(2,1)S(1)}, bf16[768,128]{1,0:T(8,128)(2,1)}, u32[]{:S(2)}) copy-start(bf16[768,128]{1,0:T(8,128)(2,1)} %copy-done.6) | copy-start | bytes 589828
  20.5 3.0 %copy-start.9 = (bf16[256,256]{1,0:T(8,128)(2,1)S(1)}, bf16[256,256]{1,0:T(8,128)(2,1)}, u32[]{:S(2)}) copy-start(bf16[256,256]{1,0:T(8,128)(2,1)} %copy-done.8) | copy-start | bytes 393220
  21.5 8.2 %collective-permute-start = (f32[80,128]{1,0:T(8,128)S(1)}, f32[80,128]{1,0:T(8,128)S(1)}, u32[]{:S(2)}, u32[]{:S(2)}) collective-permute-start(f32[80,128]{1,0:T(8,128)S(1)} %get-tuple-element.29), channel_id=1, source_target_pairs={{0,1},{2,3},{4,5},{6,7},{8,9},{10,11},{12,13},{14,15},{1,0},{3,2},... | collective-permute-start | bytes 122888 | tf_op jit(solution)/shard_map/ppermute | solution.py:18
  21.7 8.0 %collective-permute-start.1 = (f32[80,128]{1,0:T(8,128)S(1)}, f32[80,128]{1,0:T(8,128)S(1)}, u32[]{:S(2)}, u32[]{:S(2)}) collective-permute-start(f32[80,128]{1,0:T(8,128)S(1)} %get-tuple-element.30), channel_id=1, source_target_pairs={{1,2},{3,4},{5,6},{7,8},{9,10},{11,12},{13,14},{15,0},{2,1},{4,3},... | collective-permute-start | bytes 122888 | tf_op jit(solution)/shard_map/ppermute | solution.py:18

commit v4 on v3

--- a/solution.py
+++ b/solution.py
@@ -8,6 +8,8 @@
 F32 = jnp.float32
 BF16 = jnp.bfloat16
 HALO = 4
+EDGE_GROUPS = [(1, 8), (9, 13)]
+AHEAD = 2
 POLAR = 3
 PLACES = 16
 
@@ -273,7 +275,7 @@
     return jnp.dot(jnp.concatenate(pieces, axis=1), weights[...], preferred_element_type=F32)
 
 
-def layers(at, chunks, moved, x0, y0, y1, y2, yc, yo, yu, w1, w2, wd, wc, wu):
+def layers(at, groups, moved, x0, y0, y1, y2, yc, yo, yu, w1, w2, wd, wc, wu):
     step, top, bottom, pole = at.step, at.top, at.bottom, at.pole
     x0[at(top), :] = pltpu.roll(x0[at(pole + 1), :], 32, 1)
     x0[at(pole), :] = pltpu.roll(x0[at(1), :], 32, 1)
@@ -281,59 +283,103 @@
         x = x0[at(row), :]
         side = jnp.where(at.mask(1, 16), moved("x0", row, 1, x, -1), moved("x0", row, 1, x, 1))
         y0[at(row), :] = jnp.where(at.mask(1, 64), x, side)
-
-    def store_fine(y, name, row, count, values, shift):
-        shifted = moved(name, row, count, values, shift).astype(BF16)
-        values = values.astype(BF16)
-        for p in range(2):
-            lanes = slice(p * 128, (p + 1) * 128)
-            y[at(row, count), p * 256 : p * 256 + 128] = values[:, lanes]
-            y[at(row, count), p * 256 + 128 : p * 256 + 256] = shifted[:, lanes]
-
-    def edges_fine(y, polar_rows):
-        y[at(top), 256:512] = y[at(pole + 1), 0:256]
-        y[at(pole), 256:512] = y[at(1), 0:256]
-        y[at(bottom), 0:256] = jnp.zeros((step, 256), BF16)
-        y[at(pole + 1 + polar_rows), 0:256] = jnp.zeros((step, 256), BF16)
-
-    for row, count in chunks(POLAR):
+    for y, polar_rows in ((y1, POLAR), (y2, POLAR - 1), (yc, POLAR - 1), (yo, POLAR - 2), (yu, POLAR - 2)):
+        for row in (bottom, pole + 1 + polar_rows):
+            y[at(row), :] = jnp.zeros((step, y.shape[1]), BF16)
+
+    def layer(name, polar_rows, inputs, weights, store, edge, clear):
+        def task(row, count):
+            def finish(found):
+                store(name, row, count, silu(found))
+                if row < bottom < row + count:
+                    clear()
+                if row <= pole + 1 < row + count:
+                    edge(top, pole + 1)
+                if row == 1 or row < pole < row + count:
+                    edge(pole, 1)
+
+            return lambda: product(inputs(row, count), weights), finish
+
+        return [task(row, polar_rows if row == pole + 1 else count) for row, count in groups]
+
+    def fine(y, shift):
+        def store(name, row, count, values):
+            shifted = moved(name, row, count, values, shift).astype(BF16)
+            values = values.astype(BF16)
+            for p in range(2):
+                lanes = slice(p * 128, (p + 1) * 128)
+                y[at(row, count), p * 256 : p * 256 + 128] = values[:, lanes]
+                y[at(row, count), p * 256 + 128 : p * 256 + 256] = shifted[:, lanes]
+
+        def edge(target, source):
+            y[at(target), 256:512] = y[at(source), 0:256]
+
+        def clear():
+            y[at(bottom), 0:256] = jnp.zeros((step, 256), BF16)
+
+        return store, edge, clear
+
+    def first_inputs(row, count):
         vertical = jnp.where(at.mask(count, 32), y0[at(row + 1, count), :], y0[at(row - 1, count), :])
-        pieces = [y0[at(row, count), :].astype(BF16), vertical.astype(BF16)]
-        store_fine(y1, "y1", row, count, silu(product(pieces, w1)), 1)
-    edges_fine(y1, POLAR)
-
-    for row, count in chunks(POLAR - 1):
-        pieces = [y1[at(row - 1, count), 256:512], y1[at(row, count), :], y1[at(row + 1, count), 0:256]]
-        store_fine(y2, "y2", row, count, silu(product(pieces, w2)), -1)
-    edges_fine(y2, POLAR - 1)
-
-    for row, count in chunks(POLAR - 1):
-        values = silu(product([y2[at(row - 1, count), 256:512], y2[at(row, count), :]], wd))
-        yc[at(row, count), 0:128] = moved("yc", row, count, values, 1).astype(BF16)
+        return [y0[at(row, count), :].astype(BF16), vertical.astype(BF16)]
+
+    def second_inputs(row, count):
+        return [y1[at(row - 1, count), 256:512], y1[at(row, count), :], y1[at(row + 1, count), 0:256]]
+
+    def down_inputs(row, count):
+        return [y2[at(row - 1, count), 256:512], y2[at(row, count), :]]
+
+    def coarse_inputs(row, count):
+        return [yc[at(row + a, count), :] for a in (-1, 0, 1)]
+
+    def up_inputs(row, count):
+        return [yo[at(row, count), :], yo[at(row + 1, count), :]]
+
+    def store_coarse_in(name, row, count, values):
+        yc[at(row, count), 0:128] = moved(name, row, count, values, 1).astype(BF16)
         yc[at(row, count), 128:256] = values.astype(BF16)
-        yc[at(row, count), 256:384] = moved("yc", row, count, values, -1).astype(BF16)
-    yc[at(top), :] = yc[at(pole + 1), :]
-    yc[at(pole), :] = yc[at(1), :]
-    yc[at(bottom), :] = jnp.zeros((step, 384), BF16)
-
-    for row, count in chunks(POLAR - 2):
-        values = silu(product([yc[at(row + a, count), :] for a in (-1, 0, 1)], wc))
-        yo[at(row, count), 0:128] = moved("yo", row, count, values, 1).astype(BF16)
+        yc[at(row, count), 256:384] = moved(name, row, count, values, -1).astype(BF16)
+
+    def edge_coarse_in(target, source):
+        yc[at(target), :] = yc[at(source), :]
+
+    def clear_coarse_in():
+        yc[at(bottom), :] = jnp.zeros((step, 384), BF16)
+
+    def clear_coarse_out():
+        yo[at(bottom), :] = jnp.zeros((step, 256), BF16)
+
+    def store_coarse_out(name, row, count, values):
+        yo[at(row, count), 0:128] = moved(name, row, count, values, 1).astype(BF16)
         yo[at(row, count), 128:256] = values.astype(BF16)
-    yo[at(bottom), :] = jnp.zeros((step, 256), BF16)
-    yo[at(pole + 2), :] = jnp.zeros((step, 256), BF16)
-
-    for row, count in chunks(POLAR - 2):
-        values = silu(product([yo[at(row, count), :], yo[at(row + 1, count), :]], wu))
-        store_fine(yu, "yu", row, count, values, -1)
-    edges_fine(yu, POLAR - 2)
-
-
-def merge(at, row, count, y2, yu, wm, wp):
+
+    return [
+        layer("y1", POLAR, first_inputs, w1, *fine(y1, 1)),
+        layer("y2", POLAR - 1, second_inputs, w2, *fine(y2, -1)),
+        layer("yc", POLAR - 1, down_inputs, wd, store_coarse_in, edge_coarse_in, clear_coarse_in),
+        layer("yo", POLAR - 2, coarse_inputs, wc, store_coarse_out, lambda target, source: None, clear_coarse_out),
+        layer("yu", POLAR - 2, up_inputs, wu, *fine(yu, -1)),
+    ]
+
+
+def run(tasks, ahead):
+    found = {}
+    for n in range(len(tasks) + ahead):
+        if n < len(tasks):
+            found[n] = tasks[n][0]()
+        if n >= ahead:
+            tasks[n - ahead][1](found.pop(n - ahead))
+
+
+def merge(at, row, count, y2, yu, wm):
     pieces = []
     for y in (y2, yu):
         pieces += [y[at(row - 1, count), 256:512], y[at(row, count), :], y[at(row + 1, count), 0:256]]
-    merged = silu(product(pieces, wm)).astype(BF16)
+    return product(pieces, wm)
+
+
+def project(found, wp):
+    merged = silu(found).astype(BF16)
     return lax.dot_general(wp[...], merged, (((1,), (1,)), ((), ())), preferred_element_type=F32)
 
 
@@ -348,8 +394,8 @@
     at = Rows(half, blocks)
     group = 4
 
-    def chunks(polar_rows):
-        return [(1 + i, group) for i in range(0, blocks, group)] + [(at.pole + 1, polar_rows)]
+    groups = [(1 + i, group) for i in range(0, blocks, group)]
+    polar = [(at.pole + 1, POLAR)]
 
     def moved(name, row, count, values, shift):
         for (key, _, way), ref in zip(SHARED_KEYS, shared):
@@ -364,7 +410,7 @@
         x0[at(row), :] = jnp.zeros((half, 128), F32)
     for i in range(blocks + POLAR):
         x0[at(at.of(i)), :] = cells[i * half : (i + 1) * half, :].astype(F32)
-    layers(at, chunks, moved, *scratch, w1, w2, wd, wc, wu)
+    tasks = sum(layers(at, polar + groups, moved, *scratch, w1, w2, wd, wc, wu), [])
 
     y2, yu = scratch[3], scratch[6]
     lane = lax.broadcasted_iota(jnp.int32, (8, 2 * half), 1)
@@ -376,17 +422,22 @@
         odds = jnp.take_along_axis(values[p * 16 + 8 : p * 16 + 16], spread, axis=1)
         return jnp.where(even, evens, odds)
 
-    for row in range(1, 1 + blocks, group):
-        found = merge(at, row, group, y2, yu, wm, wp)
-        for n in range(group // 2):
-            pair = (row - 1) // 2 + n
-            own = found[:, n * 2 * half : (n + 1) * 2 * half]
-            base = skip[pair * 32 : (pair + 1) * 32, :]
-            for i in range(2):
-                for p in range(2):
-                    line = (4 * pair + 2 * i + p) * 8
-                    update[line : line + 8, :] = weave(own, i, p)
-                    rest[line : line + 8, :] = weave(base, i, p)
+    def last(row, count):
+        def finish(found):
+            found = project(found, wp)
+            for n in range(count // 2):
+                pair = (row - 1) // 2 + n
+                own = found[:, n * 2 * half : (n + 1) * 2 * half]
+                base = skip[pair * 32 : (pair + 1) * 32, :]
+                for i in range(2):
+                    for p in range(2):
+                        line = (4 * pair + 2 * i + p) * 8
+                        update[line : line + 8, :] = weave(own, i, p)
+                        rest[line : line + 8, :] = weave(base, i, p)
+
+        return lambda: merge(at, row, count, y2, yu, wm), finish
+
+    run(tasks + [last(row, count) for row, count in groups], AHEAD)
 
 
 def edges_kernel(cells, inner, outer, w1, w2, wd, wc, wu, wm, wp, update, rest, *refs):
@@ -435,11 +486,11 @@
             lines.append(line)
         return lines[0] if count == 1 else jnp.concatenate(lines, axis=0)
 
-    def chunks(polar_rows):
-        return [(1, at.pole + polar_rows)]
-
-    layers(at, chunks, moved, *scratch, w1, w2, wd, wc, wu)
-    found = merge(at, 1, blocks, scratch[3], scratch[6], wm, wp)
+    for tasks in layers(at, EDGE_GROUPS, moved, *scratch, w1, w2, wd, wc, wu):
+        run(tasks, 1)
+    parts = []
+    run([(lambda row=row: merge(at, row, 8, scratch[3], scratch[6], wm), lambda v: parts.append(project(v, wp))) for row in (1, 9)], 1)
+    found = jnp.concatenate(parts, axis=1)
 
     columns = 2 * half
     lane = lax.broadcasted_iota(jnp.int32, (8, columns), 1)

time: 33.4 us -> 30.9 us (0.925)
  Pallas kernels: 14.9 us -> 12.5 us
    pallas_call x1, Pallas kernels: 6.1 us -> 4.28 us  [inside(): pl.pallas_call(inside_kernel, out_shape=[jax.ShapeDtypeStruct((blocks * 1...]
    pallas_call x1, Pallas kernels: 3.46 us -> 2.84 us  [edges(): pl.pallas_call(edges_kernel, out_shape=jax.ShapeDtypeStruct(out_shape, F3...]
  transfers between devices with their start and end apart: 3 -> 3, of which waited for: 1 -> 1; matrix products, arithmetic and copies ran while one was open for 0% -> 0% of each run, Pallas kernels for 26% -> 22%
where the time goes in v4:
time: 30.9 us; the launch traced here: 30.7 us
  Pallas kernels  12.5 us (40%)
  starting transfers between devices  9.44 us (31%)
  waiting for transfers between devices  5.13 us (17%)
  local copies, waits for them, and re-layouts  3.55 us (11%)
    all_to_all x1, starting transfers between devices, shards(): lax.all_to_all(parcels, 'lon', split_axis=0, concat_axis=0, tiled=True)  7.4 us
    all_to_all x1, waiting for transfers between devices, shards(): lax.all_to_all(parcels, 'lon', split_axis=0, concat_axis=0, tiled=True)  5.13 us
    pallas_call x1, Pallas kernels, inside(): pl.pallas_call(inside_kernel, out_shape=[jax.ShapeDtypeStruct((blocks * 1...  4.28 us
    unnamed x20, local copies, waits for them, and re-layouts  3.55 us
    pallas_call x1, Pallas kernels, edges(): pl.pallas_call(edges_kernel, out_shape=jax.ShapeDtypeStruct(out_shape, F3...  2.84 us
    pallas_call x1, Pallas kernels, prepare(): pl.pallas_call(prepare_kernel, in_specs=[pl.BlockSpec(memory_space=pltpu....  2.42 us
    ppermute x2, starting transfers between devices, swap(): return lax.ppermute(block, axis, pairs + [(b, a) for a, b in pairs])  2.04 us
    pallas_call x1, Pallas kernels, pack(): pl.pallas_call(pack_kernel, in_specs=[pl.BlockSpec(memory_space=pltpu.HBM...  2 us
  transfers between devices with their start and end apart: 3, of which 1 were waited for; matrix products, arithmetic and copies ran while one was open for 0% of the time, Pallas kernels for 22%

profile of v4, /device:TPU:0, one launch (start us, length us, event | category | flops | bytes accessed | tf_op | source)
XLA Modules:
  0.0 30.7 jit_solution(4565393355528832252)
XLA Ops:
  0.0 2.0 %pack.1 = bf16[16,80,128]{2,1,0:T(8,128)(2,1)} custom-call(bf16[16,2,2048]{2,1,0:T(2,128)(2,1)} %fields_hbm.1, s32[2,32,128]{2,1,0:T(8,128)} %refs_0_.1), custom_call_target="tpu_custom_call" | custom-call | tf_op jit(solution)/shard_map/pack/pallas_call | solution.py:53
  2.0 7.4 %all-to-all-start = ((bf16[16,80,128]{2,1,0:T(8,128)(2,1)}), bf16[16,80,128]{2,1,0:T(8,128)(2,1)S(1)}, u32[]{:S(2)}, u32[]{:S(2)}) async-start(bf16[16,80,128]{2,1,0:T(8,128)(2,1)} %pack.1), calls=%async_computation | async-start | bytes 655360 | tf_op jit(solution)/shard_map/all_to_all | solution.py:560
  9.4 2.4 %prepare.1 = (bf16[2048,512]{1,0:T(8,128)(2,1)S(1)}, s32[32,128]{1,0:T(8,128)S(1)}, bf16[256,256]{1,0:T(8,128)(2,1)S(1)}, bf16[1024,256]{1,0:T(8,128)(2,1)S(1)},...) custom-call(s32[2,32,128]{2,1,0:T(8,128)} %refs_0_.1, ...), custom_call_target="tpu_custom_call" | custom-call | tf_op jit(solution)/shard_map/prepare/pallas_call | solution.py:165
  11.8 0.0 copy-start
  11.8 0.8 %copy-done = bf16[1024,256]{1,0:T(8,128)(2,1)} copy-done((bf16[1024,256]{1,0:T(8,128)(2,1)}, bf16[1024,256]{1,0:T(8,128)(2,1)S(1)}, u32[]{:S(2)}) %copy-start) | copy-done | bytes 524312
  12.6 0.0 copy-start.2
  12.6 0.7 %copy-done.2 = bf16[1152,128]{1,0:T(8,128)(2,1)} copy-done((bf16[1152,128]{1,0:T(8,128)(2,1)}, bf16[1152,128]{1,0:T(8,128)(2,1)S(1)}, u32[]{:S(2)}) %copy-start.2) | copy-done | bytes 294936
  13.3 0.7 %copy-done.4 = bf16[512,256]{1,0:T(8,128)(2,1)} copy-done((bf16[512,256]{1,0:T(8,128)(2,1)}, bf16[512,256]{1,0:T(8,128)(2,1)S(1)}, u32[]{:S(2)}) %copy-start.4) | copy-done | bytes 262168
  14.0 0.7 %copy-done.6 = bf16[768,128]{1,0:T(8,128)(2,1)} copy-done((bf16[768,128]{1,0:T(8,128)(2,1)}, bf16[768,128]{1,0:T(8,128)(2,1)S(1)}, u32[]{:S(2)}) %copy-start.6) | copy-done | bytes 196632
  14.7 0.7 %copy-done.8 = bf16[256,256]{1,0:T(8,128)(2,1)} copy-done((bf16[256,256]{1,0:T(8,128)(2,1)}, bf16[256,256]{1,0:T(8,128)(2,1)S(1)}, u32[]{:S(2)}) %copy-start.8) | copy-done | bytes 131096
  15.4 5.1 %all-to-all-done.block = bf16[16,80,128]{2,1,0:T(8,128)(2,1)S(1)} async-done(((bf16[16,80,128]{2,1,0:T(8,128)(2,1)}), bf16[16,80,128]{2,1,0:T(8,128)(2,1)S(1)}, u32[]{:S(2)}, u32[]{:S(2)}) %all-to-all-start) | async-done | bytes 327712 | tf_op jit(solution)/shard_map/all_to_all | solution.py:560
  20.5 0.0 copy-start.9
  20.5 1.0 %remap.1 = (bf16[1280,128]{1,0:T(8,128)(2,1)S(1)}, f32[80,128]{1,0:T(8,128)S(1)}, f32[80,128]{1,0:T(8,128)S(1)}, f32[256,128]{1,0:T(8,128)S(1)}) custom-call(bf16[16,80,128]{2,1,0:T(8,128)(2,1)S(1)} %all-to-all-done.block, bf16[2048,512]{1,0:T(8,128)(2,1)S(1)} %get-tuple-element.26.onehot, s32[32,128]{1,0:T(8,128)S(1)} %get-tuple-element.27.source), custom_call_target="tpu_custom_call" | custom-call | tf_op jit(solution)/shard_map/remap/pallas_call | solution.py:230
  21.5 0.2 collective-permute-start
  21.7 1.9 %collective-permute-start.1 = (f32[80,128]{1,0:T(8,128)S(1)}, f32[80,128]{1,0:T(8,128)S(1)}, u32[]{:S(2)}, u32[]{:S(2)}) collective-permute-start(f32[80,128]{1,0:T(8,128)S(1)} %get-tuple-element.30), channel_id=1, source_target_pairs={{1,2},{3,4},{5,6},{7,8},{9,10},{11,12},{13,14},{15,0},{2,1},{4,3},... | collective-permute-start | bytes 122888 | tf_op jit(solution)/shard_map/ppermute | solution.py:20
  23.5 0.0 copy-done.1
  23.5 0.0 copy-done.3
  23.5 0.0 copy-done.5
  23.5 0.0 copy-done.7
  23.5 0.0 copy-done.9
  23.6 4.3 %inside.1 = (f32[256,128]{1,0:T(8,128)S(1)}, f32[256,128]{1,0:T(8,128)S(1)}, f32[23,256]{1,0:T(8,128)S(1)}, f32[23,256]{1,0:T(8,128)S(1)}, f32[23,128]{1,0:T(8,1...) custom-call(bf16[1280,128]{1,0:T(8,128)(2,1)S(1)} %get-tuple-element.28.cells, ...), custom_call_target="tpu_custom_call" | custom-call | flops 4000000000 | bytes 4000000 | tf_op jit(solution)/shard_map/inside/pallas_call | solution.py:525
  27.8 0.0 collective-permute-done.inner
  27.9 0.0 collective-permute-done.1.outer
  27.9 2.8 %edges.1 = f32[8,32,128]{2,1,0:T(8,128)} custom-call(bf16[1280,128]{1,0:T(8,128)(2,1)S(1)} %get-tuple-element.28.cells, f32[80,128]{1,0:T(8,128)S(1)} %collective-permute-done.inner, f32[80,128]{1,0:T(8,128)S(1)} %collective-permute-done.1.outer, bf16[256,256]{1,0:T(8,128)(2,1)S(1)} %copy-done.9, bf16[1024,256]{1,0:T(8,128)(2,1)S(1)} %copy-done.1, ...), custom_call_target="tpu_custom_call" | custom-call | tf_op jit(solution)/shard_map/edges/pallas_call | solution.py:537
  (7 shorter events, 0.0 us)
Async XLA Ops:
  2.0 18.5 %all-to-all-start = ((bf16[16,80,128]{2,1,0:T(8,128)(2,1)}), bf16[16,80,128]{2,1,0:T(8,128)(2,1)S(1)}, u32[]{:S(2)}, u32[]{:S(2)}) async-start(bf16[16,80,128]{2,1,0:T(8,128)(2,1)} %pack.1), calls=%async_computation | async-start | bytes 655360 | tf_op jit(solution)/shard_map/all_to_all | solution.py:560
  11.8 0.8 %copy-start = (bf16[1024,256]{1,0:T(8,128)(2,1)}, bf16[1024,256]{1,0:T(8,128)(2,1)S(1)}, u32[]{:S(2)}) copy-start(bf16[1024,256]{1,0:T(8,128)(2,1)S(1)} %get-tuple-element.32.w2) | copy-start | bytes 1572868
  12.6 0.7 %copy-start.2 = (bf16[1152,128]{1,0:T(8,128)(2,1)}, bf16[1152,128]{1,0:T(8,128)(2,1)S(1)}, u32[]{:S(2)}) copy-start(bf16[1152,128]{1,0:T(8,128)(2,1)S(1)} %get-tuple-element.34.wc) | copy-start | bytes 884740
  13.3 0.7 %copy-start.4 = (bf16[512,256]{1,0:T(8,128)(2,1)}, bf16[512,256]{1,0:T(8,128)(2,1)S(1)}, u32[]{:S(2)}) copy-start(bf16[512,256]{1,0:T(8,128)(2,1)S(1)} %get-tuple-element.35.wu) | copy-start | bytes 786436
  14.0 0.7 %copy-start.6 = (bf16[768,128]{1,0:T(8,128)(2,1)}, bf16[768,128]{1,0:T(8,128)(2,1)S(1)}, u32[]{:S(2)}) copy-start(bf16[768,128]{1,0:T(8,128)(2,1)S(1)} %get-tuple-element.33.wd) | copy-start | bytes 589828
  14.7 0.7 %copy-start.8 = (bf16[256,256]{1,0:T(8,128)(2,1)}, bf16[256,256]{1,0:T(8,128)(2,1)S(1)}, u32[]{:S(2)}) copy-start(bf16[256,256]{1,0:T(8,128)(2,1)S(1)} %get-tuple-element.31.w1) | copy-start | bytes 393220
  20.5 3.0 %copy-start.1 = (bf16[1024,256]{1,0:T(8,128)(2,1)S(1)}, bf16[1024,256]{1,0:T(8,128)(2,1)}, u32[]{:S(2)}) copy-start(bf16[1024,256]{1,0:T(8,128)(2,1)} %copy-done) | copy-start | bytes 1572868
  20.5 3.0 %copy-start.3 = (bf16[1152,128]{1,0:T(8,128)(2,1)S(1)}, bf16[1152,128]{1,0:T(8,128)(2,1)}, u32[]{:S(2)}) copy-start(bf16[1152,128]{1,0:T(8,128)(2,1)} %copy-done.2) | copy-start | bytes 884740
  20.5 3.0 %copy-start.5 = (bf16[512,256]{1,0:T(8,128)(2,1)S(1)}, bf16[512,256]{1,0:T(8,128)(2,1)}, u32[]{:S(2)}) copy-start(bf16[512,256]{1,0:T(8,128)(2,1)} %copy-done.4) | copy-start | bytes 786436
  20.5 3.0 %copy-start.7 = (bf16[768,128]{1,0:T(8,128)(2,1)S(1)}, bf16[768,128]{1,0:T(8,128)(2,1)}, u32[]{:S(2)}) copy-start(bf16[768,128]{1,0:T(8,128)(2,1)} %copy-done.6) | copy-start | bytes 589828
  20.5 3.0 %copy-start.9 = (bf16[256,256]{1,0:T(8,128)(2,1)S(1)}, bf16[256,256]{1,0:T(8,128)(2,1)}, u32[]{:S(2)}) copy-start(bf16[256,256]{1,0:T(8,128)(2,1)} %copy-done.8) | copy-start | bytes 393220
  21.5 6.4 %collective-permute-start = (f32[80,128]{1,0:T(8,128)S(1)}, f32[80,128]{1,0:T(8,128)S(1)}, u32[]{:S(2)}, u32[]{:S(2)}) collective-permute-start(f32[80,128]{1,0:T(8,128)S(1)} %get-tuple-element.29), channel_id=1, source_target_pairs={{0,1},{2,3},{4,5},{6,7},{8,9},{10,11},{12,13},{14,15},{1,0},{3,2},... | collective-permute-start | bytes 122888 | tf_op jit(solution)/shard_map/ppermute | solution.py:20
  21.7 6.2 %collective-permute-start.1 = (f32[80,128]{1,0:T(8,128)S(1)}, f32[80,128]{1,0:T(8,128)S(1)}, u32[]{:S(2)}, u32[]{:S(2)}) collective-permute-start(f32[80,128]{1,0:T(8,128)S(1)} %get-tuple-element.30), channel_id=1, source_target_pairs={{1,2},{3,4},{5,6},{7,8},{9,10},{11,12},{13,14},{15,0},{2,1},{4,3},... | collective-permute-start | bytes 122888 | tf_op jit(solution)/shard_map/ppermute | solution.py:20

commit v5 on v4

--- a/solution.py
+++ b/solution.py
@@ -8,10 +8,10 @@
 F32 = jnp.float32
 BF16 = jnp.bfloat16
 HALO = 4
-EDGE_GROUPS = [(1, 8), (9, 13)]
+EDGE_ROWS = 9
 AHEAD = 2
 POLAR = 3
-PLACES = 16
+PARTS = 4
 
 
 def swap(block, axis, first):
@@ -20,44 +20,67 @@
     return lax.ppermute(block, axis, pairs + [(b, a) for a, b in pairs])
 
 
-def pack_kernel(fields_hbm, table_hbm, parcels, fields, table, sems):
+def opposite(block, axis):
+    devices = lax.axis_size(axis)
+    return lax.ppermute(block, axis, [(i, (i + devices // 2) % devices) for i in range(devices)])
+
+
+def pack_kernel(fields_hbm, parcels_hbm, fields, parcels, in_sems, out_sems):
     channels, rows, _ = fields.shape
     devices, depth, columns = parcels.shape
     depth = rows * channels
-    copies = [
-        pltpu.make_async_copy(fields_hbm, fields, sems.at[0]),
-        pltpu.make_async_copy(table_hbm, table, sems.at[1]),
+    parts = in_sems.shape[0]
+    span = devices // parts
+
+    def lanes(n):
+        return slice(n * span * columns, (n + 1) * span * columns)
+
+    loads = [
+        pltpu.make_async_copy(fields_hbm.at[:, :, lanes(n)], fields.at[:, :, lanes(n)], in_sems.at[n])
+        for n in range(parts)
     ]
-    for copy in copies:
-        copy.start()
-    copies[1].wait()
-    lines = [table[0, : 2 * POLAR, :], lax.rem(table[1, : 2 * POLAR, :], columns)]
-    lines.append(jnp.zeros((PLACES - 4 * POLAR, columns), jnp.int32))
-    lines = jnp.concatenate(lines, axis=0).astype(F32).astype(BF16)
-    for target in range(devices):
-        parcels[target, 2 * depth :, :] = lines
-    copies[0].wait()
-    values = fields[...].astype(F32)
-    for row in range(rows):
-        line = values[:, row, :].astype(BF16)
-        for target in range(devices):
-            piece = line[:, target * columns : (target + 1) * columns]
-            opposite = (target + devices // 2) % devices
-            parcels[target, row * channels : (row + 1) * channels, :] = piece
-            parcels[opposite, depth + row * channels : depth + (row + 1) * channels, :] = piece
-
-
-def pack(fields, table, devices):
+    for load in loads:
+        load.start()
+    stores = []
+
+    def send(targets, part):
+        at = parcels.at[targets, part, :], parcels_hbm.at[targets, part, :]
+        stores.append(pltpu.make_async_copy(*at, out_sems.at[len(stores)]))
+        stores[-1].start()
+
+    for n in range(parts):
+        loads[n].wait()
+        values = fields[:, :, lanes(n)].astype(F32)
+        first, other = n * span, (n * span + devices // 2) % devices
+        for row in range(rows):
+            line = values[:, row, :].astype(BF16)
+            for m in range(span):
+                piece = line[:, m * columns : (m + 1) * columns]
+                parcels[first + m, row * channels : (row + 1) * channels, :] = piece
+                parcels[other + m, depth + row * channels : depth + (row + 1) * channels, :] = piece
+        send(slice(first, first + span), slice(0, depth))
+        send(slice(other, other + span), slice(depth, 2 * depth))
+    for store in stores:
+        store.wait()
+
+
+def pack(fields, devices, columns):
     channels, rows, _ = fields.shape
-    args = (fields, table)
+    shape = (devices, 2 * rows * channels, columns)
     return pl.pallas_call(
         pack_kernel,
-        in_specs=[pl.BlockSpec(memory_space=pltpu.HBM)] * 2,
-        out_shape=jax.ShapeDtypeStruct((devices, 2 * rows * channels + PLACES, table.shape[2]), BF16),
-        scratch_shapes=[pltpu.VMEM(a.shape, a.dtype) for a in args] + [pltpu.SemaphoreType.DMA((2,))],
+        in_specs=[pl.BlockSpec(memory_space=pltpu.HBM)],
+        out_specs=pl.BlockSpec(memory_space=pltpu.HBM),
+        out_shape=pltpu.HBM(shape, BF16),
+        scratch_shapes=[
+            pltpu.VMEM(fields.shape, BF16),
+            pltpu.VMEM(shape, BF16),
+            pltpu.SemaphoreType.DMA((PARTS,)),
+            pltpu.SemaphoreType.DMA((2 * PARTS,)),
+        ],
         compiler_params=pltpu.CompilerParams(vmem_limit_bytes=16 * 2**20),
         name="pack",
-    )(*[pltpu.with_memory_space_constraint(a, pltpu.HBM) for a in args])
+    )(pltpu.with_memory_space_constraint(fields, pltpu.HBM))
 
 
 def tap(kernel_ref, row, col):
@@ -112,29 +135,24 @@
     wp[...] = jnp.concatenate(lines, axis=0).astype(BF16)
 
 
-def locate(rows, cols, onehot, source):
+def locate(rows, cols):
     grid_rows, columns = rows.shape
     half = columns // 2
     code = rows * columns + cols
     lane = lax.broadcasted_iota(jnp.int32, (grid_rows, columns), 1)
     odd = [jnp.take_along_axis(code, lax.rem(lane, half) * 2 + q, axis=1) for q in range(2)]
     left = lax.broadcasted_iota(jnp.int32, (1, columns), 1) < half
-    place = lax.broadcasted_iota(jnp.int32, (2 * columns, columns), 0)
+    lines = []
     for pair in range(grid_rows // 4):
         for p in range(2):
             for q in range(2):
-                n = p * 2 + q
                 above, below = 4 * pair + p, 4 * pair + 2 + p
-                line = jnp.where(left, odd[q][above : above + 1, :], odd[q][below : below + 1, :])
-                source[4 * pair + n : 4 * pair + n + 1, :] = lax.div(line, 2 * columns)
-                here = place == lax.rem(line, 2 * columns)
-                onehot[pair * 2 * columns : (pair + 1) * 2 * columns, n * columns : (n + 1) * columns] = jnp.where(
-                    here, 1.0, 0.0
-                ).astype(BF16)
+                lines.append(jnp.where(left, odd[q][above : above + 1, :], odd[q][below : below + 1, :]))
+    return jnp.concatenate(lines, axis=0)
 
 
 def prepare_kernel(*refs):
-    args, outs, scratch, sems = refs[:8], refs[8:17], refs[17:25], refs[25]
+    args, (places, *weights), scratch, sems = refs[:8], refs[8:16], refs[16:24], refs[24]
     copies = [
         pltpu.make_async_copy(source, target, sems.at[n]) for n, (source, target) in enumerate(zip(args, scratch))
     ]
@@ -142,16 +160,15 @@
         copy.start()
     copies[0].wait()
     table = scratch[0]
-    locate(table[0], lax.rem(table[1], table.shape[2]), *outs[:2])
+    places[...] = locate(table[0], lax.rem(table[1], table.shape[2]))
     for copy in copies[1:]:
         copy.wait()
-    arrange(*scratch[1:], *outs[2:])
+    arrange(*scratch[1:], *weights)
 
 
 def prepare(table, first, second, down, coarse, up, merge, projection):
     channels, wide = second.shape[3], coarse.shape[3]
     columns = table.shape[2]
-    pairs = table.shape[1] // 4
     shapes = (
         (16 * first.shape[3], 4 * channels),
         (16 * channels, 4 * channels),
@@ -165,28 +182,23 @@
     return pl.pallas_call(
         prepare_kernel,
         in_specs=[pl.BlockSpec(memory_space=pltpu.HBM)] * 8,
-        out_shape=[
-            jax.ShapeDtypeStruct((pairs * 2 * columns, 4 * columns), BF16),
-            jax.ShapeDtypeStruct((pairs * 4, columns), jnp.int32),
-        ]
-        + [jax.ShapeDtypeStruct(s, BF16) for s in shapes],
+        out_shape=[jax.ShapeDtypeStruct(table.shape[1:], jnp.int32)] + [jax.ShapeDtypeStruct(s, BF16) for s in shapes],
         scratch_shapes=[pltpu.VMEM(a.shape, a.dtype) for a in args] + [pltpu.SemaphoreType.DMA((8,))],
         compiler_params=pltpu.CompilerParams(vmem_limit_bytes=16 * 2**20),
         name="prepare",
     )(*[pltpu.with_memory_space_constraint(a, pltpu.HBM) for a in args])
 
 
-def remap_kernel(block, onehot, source, cells, inner, outer, skip, polar_onehot, polar_source):
+def remap_kernel(block, places, polar, cells, inner, outer, skip):
     even = lax.rem(lax.axis_index("lon"), 2) == 0
     devices, depth, columns = block.shape
-    depth = (depth - PLACES) // 2
+    depth = depth // 2
     channels = depth // 2
-    opposite = lax.rem(lax.axis_index("lon") + devices // 2, devices)
-    places = block[opposite, 2 * depth :, :].astype(F32).astype(jnp.int32)
-    blank = jnp.zeros((polar_source.shape[0] - 2 * POLAR, columns), jnp.int32)
-    rows = jnp.concatenate([places[: 2 * POLAR], blank], axis=0)
-    cols = jnp.concatenate([places[2 * POLAR : 4 * POLAR], blank], axis=0)
-    locate(rows, cols, polar_onehot, polar_source)
+    lines = [places[...], locate(polar[0], lax.rem(polar[1], columns))]
+    lines = jnp.concatenate(lines, axis=0)
+    sources = lax.div(lines, 2 * columns)
+    offsets = lax.rem(lines, 2 * columns).astype(F32)
+    line_at = lax.broadcasted_iota(jnp.int32, (2 * columns, columns), 0).astype(F32)
     half = columns // 2
     fields = []
     for side in range(2):
@@ -195,15 +207,18 @@
         lower = block[:, at + channels : at + depth, :].reshape(devices * channels, columns)
         fields.append(jnp.concatenate([upper, lower], axis=1))
     pairs = cells.shape[0] // columns
+    begins, finishes = [], []
     own_pairs = skip.shape[0] // 32
     for pair in range(pairs):
         own = pair < own_pairs
-        at = pair if own else pair - own_pairs
-        chosen = (onehot if own else polar_onehot)[at * 2 * columns : (at + 1) * 2 * columns, :]
-        found = jnp.dot(fields[0 if own else 1], chosen, preferred_element_type=F32)
+        chosen = []
+        for n in range(4):
+            here = line_at == jnp.broadcast_to(offsets[4 * pair + n : 4 * pair + n + 1, :], line_at.shape)
+            chosen.append(jnp.where(here, 1.0, 0.0).astype(BF16))
+        found = jnp.dot(fields[0 if own else 1], jnp.concatenate(chosen, axis=1), preferred_element_type=F32)
         lines = []
         for n in range(4):
-            line = (source if own else polar_source)[4 * at + n : 4 * at + n + 1, :]
+            line = sources[4 * pair + n : 4 * pair + n + 1, :]
             line = jnp.broadcast_to(line, (channels, columns))
             total = jnp.zeros((channels, columns), F32)
             for s in range(devices):
@@ -215,33 +230,28 @@
         turned = jnp.concatenate(lines + lines, axis=0).T
         cells[pair * columns : (pair + 1) * columns, :] = turned.astype(BF16)
         for i in range(2):
-            row = (pair * 2 + i) * HALO
-            begin = turned[i * half : i * half + HALO]
-            finish = turned[(i + 1) * half - HALO : (i + 1) * half]
-            inner[row : row + HALO, :] = jnp.where(even, finish, begin)
-            outer[row : row + HALO, :] = jnp.where(even, begin, finish)
-
-
-def remap(block, onehot, source):
+            begins.append(turned[i * half : i * half + HALO])
+            finishes.append(turned[(i + 1) * half - HALO : (i + 1) * half])
+    begins, finishes = jnp.concatenate(begins, axis=0), jnp.concatenate(finishes, axis=0)
+    inner[...] = jnp.where(even, finishes, begins).astype(BF16)
+    outer[...] = jnp.where(even, begins, finishes).astype(BF16)
+
+
+def remap(block, places, polar):
     columns = block.shape[2]
-    own_rows = source.shape[0]
-    polar_rows = 4 * ((POLAR + 1) // 2)
-    count = (own_rows + polar_rows) // 4
+    grid_rows = places.shape[0]
+    count = (grid_rows + polar.shape[1]) // 4
     return pl.pallas_call(
         remap_kernel,
         out_shape=[
             jax.ShapeDtypeStruct((count * columns, columns), BF16),
-            jax.ShapeDtypeStruct((count * 2 * HALO, columns), F32),
-            jax.ShapeDtypeStruct((count * 2 * HALO, columns), F32),
-            jax.ShapeDtypeStruct((own_rows * 8, columns), F32),
-        ],
-        scratch_shapes=[
-            pltpu.VMEM((polar_rows // 4 * 2 * columns, 4 * columns), BF16),
-            pltpu.VMEM((polar_rows, columns), jnp.int32),
+            jax.ShapeDtypeStruct((count * 2 * HALO, columns), BF16),
+            jax.ShapeDtypeStruct((count * 2 * HALO, columns), BF16),
+            jax.ShapeDtypeStruct((grid_rows * 8, columns), F32),
         ],
         compiler_params=pltpu.CompilerParams(vmem_limit_bytes=16 * 2**20),
         name="remap",
-    )(block, onehot, source)
+    )(block, places, polar)
 
 
 def silu(values):
@@ -272,35 +282,59 @@
 
 
 def product(pieces, weights):
-    return jnp.dot(jnp.concatenate(pieces, axis=1), weights[...], preferred_element_type=F32)
-
-
-def layers(at, groups, moved, x0, y0, y1, y2, yc, yo, yu, w1, w2, wd, wc, wu):
+    values = pieces[0] if len(pieces) == 1 else jnp.concatenate(pieces, axis=0)
+    return jnp.dot(values, weights[...], preferred_element_type=F32)
+
+
+def layers(at, groups, pairs, moved, x0, y0, y1, y2, yc, yo, yu, w1, w2, wd, wc, wu):
     step, top, bottom, pole = at.step, at.top, at.bottom, at.pole
     x0[at(top), :] = pltpu.roll(x0[at(pole + 1), :], 32, 1)
     x0[at(pole), :] = pltpu.roll(x0[at(1), :], 32, 1)
-    for row in range(at.count):
-        x = x0[at(row), :]
-        side = jnp.where(at.mask(1, 16), moved("x0", row, 1, x, -1), moved("x0", row, 1, x, 1))
-        y0[at(row), :] = jnp.where(at.mask(1, 64), x, side)
+    ready = set()
+
+    def widen(row):
+        if row not in ready:
+            ready.add(row)
+            x = x0[at(row), :]
+            side = jnp.where(at.mask(1, 16), moved("x0", row, 1, x, -1), moved("x0", row, 1, x, 1))
+            y0[at(row), :] = jnp.where(at.mask(1, 64), x, side)
+
     for y, polar_rows in ((y1, POLAR), (y2, POLAR - 1), (yc, POLAR - 1), (yo, POLAR - 2), (yu, POLAR - 2)):
         for row in (bottom, pole + 1 + polar_rows):
             y[at(row), :] = jnp.zeros((step, y.shape[1]), BF16)
 
-    def layer(name, polar_rows, inputs, weights, store, edge, clear):
-        def task(row, count):
+    def layer(name, polar_rows, inputs, weights, store, edge, paired=False):
+        def task(ranges):
+            ranges = [(row, polar_rows if row == pole + 1 else count) for row, count in ranges]
+
+            def begin():
+                pieces = [jnp.concatenate(inputs(row, count), axis=1) for row, count in ranges]
+                return product(pieces, weights)
+
             def finish(found):
-                store(name, row, count, silu(found))
-                if row < bottom < row + count:
-                    clear()
-                if row <= pole + 1 < row + count:
-                    edge(top, pole + 1)
-                if row == 1 or row < pole < row + count:
-                    edge(pole, 1)
-
-            return lambda: product(inputs(row, count), weights), finish
-
-        return [task(row, polar_rows if row == pole + 1 else count) for row, count in groups]
+                found = silu(found)
+                start = 0
+                for row, count in ranges:
+                    if paired:
+                        lanes = found.shape[1] // 2
+                        rows = []
+                        for n in range(count):
+                            line = slice(start + n // 2 * step, start + (n // 2 + 1) * step)
+                            rows.append(found[line, n % 2 * lanes : (n % 2 + 1) * lanes])
+                        values = rows[0] if count == 1 else jnp.concatenate(rows, axis=0)
+                        start += (count + 1) // 2 * step
+                    else:
+                        values = found[start : start + count * step]
+                        start += count * step
+                    store(name, row, count, values)
+                    if row == pole + 1:
+                        edge(top, pole + 1)
+                    if row == 1:
+                        edge(pole, 1)
+
+            return begin, finish, ranges
+
+        return [task(ranges) for ranges in (pairs if paired else groups)]
 
     def fine(y, shift):
         def store(name, row, count, values):
@@ -314,12 +348,11 @@
         def edge(target, source):
             y[at(target), 256:512] = y[at(source), 0:256]
 
-        def clear():
-            y[at(bottom), 0:256] = jnp.zeros((step, 256), BF16)
-
-        return store, edge, clear
+        return store, edge
 
     def first_inputs(row, count):
+        for n in range(row - 1, row + count + 1):
+            widen(n)
         vertical = jnp.where(at.mask(count, 32), y0[at(row + 1, count), :], y0[at(row - 1, count), :])
         return [y0[at(row, count), :].astype(BF16), vertical.astype(BF16)]
 
@@ -343,12 +376,6 @@
     def edge_coarse_in(target, source):
         yc[at(target), :] = yc[at(source), :]
 
-    def clear_coarse_in():
-        yc[at(bottom), :] = jnp.zeros((step, 384), BF16)
-
-    def clear_coarse_out():
-        yo[at(bottom), :] = jnp.zeros((step, 256), BF16)
-
     def store_coarse_out(name, row, count, values):
         yo[at(row, count), 0:128] = moved(name, row, count, values, 1).astype(BF16)
         yo[at(row, count), 128:256] = values.astype(BF16)
@@ -356,26 +383,38 @@
     return [
         layer("y1", POLAR, first_inputs, w1, *fine(y1, 1)),
         layer("y2", POLAR - 1, second_inputs, w2, *fine(y2, -1)),
-        layer("yc", POLAR - 1, down_inputs, wd, store_coarse_in, edge_coarse_in, clear_coarse_in),
-        layer("yo", POLAR - 2, coarse_inputs, wc, store_coarse_out, lambda target, source: None, clear_coarse_out),
+        layer("yc", POLAR - 1, down_inputs, wd, store_coarse_in, edge_coarse_in),
+        layer("yo", POLAR - 2, coarse_inputs, wc, store_coarse_out, lambda target, source: None),
         layer("yu", POLAR - 2, up_inputs, wu, *fine(yu, -1)),
     ]
 
 
-def run(tasks, ahead):
-    found = {}
-    for n in range(len(tasks) + ahead):
-        if n < len(tasks):
-            found[n] = tasks[n][0]()
-        if n >= ahead:
-            tasks[n - ahead][1](found.pop(n - ahead))
+def run(at, stages, ahead):
+    tasks, owner = [], {}
+    for stage in stages:
+        rows = {}
+        for begin, finish, ranges in stage:
+            reads = set()
+            for row, count in ranges:
+                reads.update(range(row - 1, row + count + 2))
+            reads.update({at.pole + 1} if at.top in reads else (), {1} if at.pole in reads else ())
+            tasks.append((begin, finish, {owner[row] for row in reads if row in owner}))
+            for row, count in ranges:
+                rows.update({n: len(tasks) - 1 for n in range(row, row + count)})
+        owner = rows
+    found, issued = {}, 0
+    for turn in range(len(tasks)):
+        while issued < len(tasks) and issued <= turn + ahead and all(n < turn for n in tasks[issued][2]):
+            found[issued] = tasks[issued][0]()
+            issued += 1
+        tasks[turn][1](found.pop(turn))
 
 
 def merge(at, row, count, y2, yu, wm):
     pieces = []
     for y in (y2, yu):
         pieces += [y[at(row - 1, count), 256:512], y[at(row, count), :], y[at(row + 1, count), 0:256]]
-    return product(pieces, wm)
+    return product([jnp.concatenate(pieces, axis=1)], wm)
 
 
 def project(found, wp):
@@ -387,15 +426,17 @@
 SHARED_KEYS = [(name, lanes, shift) for name, lanes, shifts in SHARED for shift in shifts]
 
 
-def inside_kernel(cells, skip, w1, w2, wd, wc, wu, wm, wp, update, rest, *refs):
+def inside_kernel(cells, skip, w1, w2, wd, wc, wu, wm, wp, update, *refs):
     shared, scratch = refs[: len(SHARED_KEYS)], refs[len(SHARED_KEYS) :]
     half = update.shape[1] // 2
     blocks = update.shape[0] // 16
     at = Rows(half, blocks)
     group = 4
 
-    groups = [(1 + i, group) for i in range(0, blocks, group)]
-    polar = [(at.pole + 1, POLAR)]
+    groups = [[(1 + i, group)] for i in range(0, blocks, group)]
+    pairs = [[(1 + i, 2 * group)] for i in range(0, blocks, 2 * group)]
+    for first in (groups[0], pairs[0]):
+        first.insert(0, (at.pole + 1, POLAR))
 
     def moved(name, row, count, values, shift):
         for (key, _, way), ref in zip(SHARED_KEYS, shared):
@@ -410,11 +451,12 @@
         x0[at(row), :] = jnp.zeros((half, 128), F32)
     for i in range(blocks + POLAR):
         x0[at(at.of(i)), :] = cells[i * half : (i + 1) * half, :].astype(F32)
-    tasks = sum(layers(at, polar + groups, moved, *scratch, w1, w2, wd, wc, wu), [])
+    stages = layers(at, groups, pairs, moved, *scratch, w1, w2, wd, wc, wu)
 
     y2, yu = scratch[3], scratch[6]
     lane = lax.broadcasted_iota(jnp.int32, (8, 2 * half), 1)
     even = lax.rem(lane, 2) == 0
+    edge = (lane < 2 * HALO) | (lane >= 2 * half - 2 * HALO)
 
     def weave(values, i, p):
         spread = lax.div(lane, 2) + i * half
@@ -432,15 +474,15 @@
                 for i in range(2):
                     for p in range(2):
                         line = (4 * pair + 2 * i + p) * 8
-                        update[line : line + 8, :] = weave(own, i, p)
-                        rest[line : line + 8, :] = weave(base, i, p)
-
-        return lambda: merge(at, row, count, y2, yu, wm), finish
-
-    run(tasks + [last(row, count) for row, count in groups], AHEAD)
-
-
-def edges_kernel(cells, inner, outer, w1, w2, wd, wc, wu, wm, wp, update, rest, *refs):
+                        inner = jnp.where(edge, 0.0, weave(own, i, p))
+                        update[line : line + 8, :] = inner + weave(base, i, p)
+
+        return lambda: merge(at, row, count, y2, yu, wm), finish, [(row, count)]
+
+    run(at, stages + [[last(*ranges[-1]) for ranges in groups]], AHEAD)
+
+
+def edges_kernel(cells, inner, outer, w1, w2, wd, wc, wu, wm, wp, update, *refs):
     shared, out, scratch = refs[: len(SHARED_KEYS)], refs[len(SHARED_KEYS)], refs[len(SHARED_KEYS) + 1 :]
     even = lax.rem(lax.axis_index("lon"), 2) == 0
     half = out.shape[2] // 2
@@ -449,6 +491,8 @@
     at = Rows(step, blocks)
     place = lax.broadcasted_iota(jnp.int32, (step, 128), 0)
     x0 = scratch[0]
+    near, far = inner[...].astype(F32), outer[...].astype(F32)
+    left, right = jnp.where(even, far, near), jnp.where(even, near, far)
     beside = {}
     for row in (at.top, at.bottom, at.pole, at.count - 1):
         x0[at(row), :] = jnp.zeros((step, 128), F32)
@@ -456,13 +500,11 @@
         row = at.of(i)
         begin = cells[i * half : i * half + 16, :].astype(F32)
         finish = cells[(i + 1) * half - 16 : (i + 1) * half, :].astype(F32)
-        near = inner[i * HALO : (i + 1) * HALO, :]
-        far = outer[i * HALO : (i + 1) * HALO, :]
         base = row * step
-        x0[base : base + HALO, :] = jnp.where(even, far, near)
+        x0[base : base + HALO, :] = left[i * HALO : (i + 1) * HALO]
         x0[base + HALO : base + 2 * HALO, :] = begin[:HALO]
         x0[base + 2 * HALO : base + 3 * HALO, :] = finish[16 - HALO :]
-        x0[base + 3 * HALO : base + 4 * HALO, :] = jnp.where(even, near, far)
+        x0[base + 3 * HALO : base + 4 * HALO, :] = right[i * HALO : (i + 1) * HALO]
         beside[row] = {-1: begin[HALO : HALO + 1], 1: finish[15 - HALO : 16 - HALO]}
     beside[at.top] = {way: pltpu.roll(line, 32, 1) for way, line in beside[at.pole + 1].items()}
     beside[at.pole] = {way: pltpu.roll(line, 32, 1) for way, line in beside[1].items()}
@@ -486,10 +528,19 @@
             lines.append(line)
         return lines[0] if count == 1 else jnp.concatenate(lines, axis=0)
 
-    for tasks in layers(at, EDGE_GROUPS, moved, *scratch, w1, w2, wd, wc, wu):
-        run(tasks, 1)
+    cut = EDGE_ROWS
+    groups = [[(1, cut)], [(1 + cut, blocks - cut), (at.pole + 1, POLAR)]]
+    pairs = [[(1, blocks), (at.pole + 1, POLAR)]]
     parts = []
-    run([(lambda row=row: merge(at, row, 8, scratch[3], scratch[6], wm), lambda v: parts.append(project(v, wp))) for row in (1, 9)], 1)
+
+    def last(row, count):
+        def finish(found):
+            parts.append(project(found, wp))
+
+        return lambda: merge(at, row, count, scratch[3], scratch[6], wm), finish, [(row, count)]
+
+    stages = layers(at, groups, pairs, moved, *scratch, w1, w2, wd, wc, wu)
+    run(at, stages + [[last(1, blocks // 2), last(1 + blocks // 2, blocks // 2)]], 1)
     found = jnp.concatenate(parts, axis=1)
 
     columns = 2 * half
@@ -508,8 +559,7 @@
             odds = jnp.take_along_axis(found[p * 16 + 8 : p * 16 + 16, lanes], spread, axis=1)
             h = 2 * i + p
             line = slice(h * 8, (h + 1) * 8)
-            value = jnp.where(edge, jnp.where(odd, odds, evens), update[line, :])
-            out[:, h, :] = value + rest[line, :]
+            out[:, h, :] = jnp.where(edge, jnp.where(odd, odds, evens), 0.0) + update[line, :]
 
 
 def buffers(step, blocks):
@@ -524,7 +574,7 @@
     rows = Rows(columns // 2, blocks).count
     return pl.pallas_call(
         inside_kernel,
-        out_shape=[jax.ShapeDtypeStruct((blocks * 16, columns), F32)] * 2
+        out_shape=[jax.ShapeDtypeStruct((blocks * 16, columns), F32)]
         + [jax.ShapeDtypeStruct((rows, lanes), F32) for _, lanes, _ in SHARED_KEYS],
         scratch_shapes=buffers(columns // 2, blocks),
         compiler_params=pltpu.CompilerParams(vmem_limit_bytes=20 * 2**20),
@@ -556,12 +606,13 @@
 ):
     _, grid_rows, columns = remap_table.shape
     count = lax.axis_size("lon")
-    parcels = pack(latlon_fields, remap_table, count)
+    polar = opposite(remap_table[:, : 4 * ((POLAR + 1) // 2), :], "lon")
+    parcels = pack(latlon_fields, count, columns)
     block = lax.all_to_all(parcels, "lon", split_axis=0, concat_axis=0, tiled=True)
-    onehot, source, *weights = prepare(
+    places, *weights = prepare(
         remap_table, kernel_first, kernel_second, kernel_down, kernel_coarse, kernel_up, kernel_merge, projection
     )
-    cells, inner, outer, skip = remap(block, onehot, source)
+    cells, inner, outer, skip = remap(block, places, polar)
     outer = swap(outer, "lon", 1)
     inner = swap(inner, "lon", 0)
     found = inside(cells, skip, weights)

time: 30.9 us -> 30.1 us (0.974)
  starting transfers between devices: 9.44 us -> 12.6 us
  local copies, waits for them, and re-layouts: 3.55 us -> 0.7 us
  Pallas kernels: 12.5 us -> 11.8 us
  waiting for transfers between devices: 5.13 us -> 4.59 us
    all_to_all x1, waiting for transfers between devices: 5.13 us -> 0.14 us  [shards(): lax.all_to_all(parcels, 'lon', split_axis=0, concat_axis=0, tiled=True)]
    ppermute x0 -> x1, waiting for transfers between devices: none -> 4.45 us  [opposite(): lax.ppermute(block, axis, [(i, (i + devices // 2) % devices) for i in ran...]
    unnamed x20 -> x0, local copies, waits for them, and re-layouts: 3.55 us -> none
    ppermute x0 -> x1, starting transfers between devices: none -> 2.83 us  [opposite(): lax.ppermute(block, axis, [(i, (i + devices // 2) % devices) for i in ran...]
    slice x0 -> x1, local copies, waits for them, and re-layouts: none -> 0.7 us  [shards(): polar = opposite(remap_table[:, :4 * ((POLAR + 1) // 2), :], 'lon')]
    pallas_call x1, Pallas kernels: 2.42 us -> 2.01 us  [prepare(): pl.pallas_call(prepare_kernel, in_specs=[pl.BlockSpec(memory_space=pltpu....]
    ppermute x2, starting transfers between devices: 2.04 us -> 2.4 us  [swap(): return lax.ppermute(block, axis, pairs + [(b, a) for a, b in pairs])]
  transfers between devices with their start and end apart: 3 -> 4, of which waited for: 1 -> 2; matrix products, arithmetic and copies ran while one was open for 0% -> 2% of each run, Pallas kernels for 22% -> 21%
where the time goes in v5:
time: 30.1 us; the launch traced here: 29.8 us
  starting transfers between devices  12.6 us (42%)
  Pallas kernels  11.8 us (39%)
  waiting for transfers between devices  4.59 us (15%)
  local copies, waits for them, and re-layouts  0.7 us (2%)
    all_to_all x1, starting transfers between devices, shards(): lax.all_to_all(parcels, 'lon', split_axis=0, concat_axis=0, tiled=True)  7.4 us
    ppermute x1, waiting for transfers between devices, opposite(): lax.ppermute(block, axis, [(i, (i + devices // 2) % devices) for i in ran...  4.45 us
    pallas_call x1, Pallas kernels, inside(): pl.pallas_call(inside_kernel, out_shape=[jax.ShapeDtypeStruct((blocks * 1...  4.29 us
    ppermute x1, starting transfers between devices, opposite(): lax.ppermute(block, axis, [(i, (i + devices // 2) % devices) for i in ran...  2.83 us
    pallas_call x1, Pallas kernels, edges(): pl.pallas_call(edges_kernel, out_shape=jax.ShapeDtypeStruct(out_shape, F3...  2.63 us
    ppermute x2, starting transfers between devices, swap(): return lax.ppermute(block, axis, pairs + [(b, a) for a, b in pairs])  2.4 us
    pallas_call x1, Pallas kernels, prepare(): pl.pallas_call(prepare_kernel, in_specs=[pl.BlockSpec(memory_space=pltpu....  2.01 us
    pallas_call x1, Pallas kernels, pack(): pl.pallas_call(pack_kernel, in_specs=[pl.BlockSpec(memory_space=pltpu.HBM...  1.88 us
  transfers between devices with their start and end apart: 4, of which 2 were waited for; matrix products, arithmetic and copies ran while one was open for 2% of the time, Pallas kernels for 21%

profile of v5, /device:TPU:0, one launch (start us, length us, event | category | flops | bytes accessed | tf_op | source)
XLA Modules:
  0.0 29.8 jit_solution(10363806335311232753)
XLA Ops:
  0.0 1.9 %pack.1 = bf16[16,64,128]{2,1,0:T(8,128)(2,1)} custom-call(bf16[16,2,2048]{2,1,0:T(2,128)(2,1)} %fields_hbm.1), custom_call_target="tpu_custom_call" | custom-call | tf_op jit(solution)/shard_map/pack/pallas_call | solution.py:70
  1.9 7.4 %all-to-all-start = ((bf16[16,64,128]{2,1,0:T(8,128)(2,1)}), bf16[16,64,128]{2,1,0:T(8,128)(2,1)S(1)}, u32[]{:S(2)}, u32[]{:S(2)}) async-start(bf16[16,64,128]{2,1,0:T(8,128)(2,1)} %pack.1), calls=%async_computation | async-start | bytes 524288 | tf_op jit(solution)/shard_map/all_to_all | solution.py:611
  9.3 0.7 %slice.3 = s32[2,8,128]{2,1,0:T(8,128)S(1)} slice(s32[2,32,128]{2,1,0:T(8,128)} %refs_0_.1), slice={[0:2], [0:8], [0:128]} | slice | bytes 16384 | tf_op jit(solution)/shard_map/slice | solution.py:609
  10.0 2.8 %collective-permute-start = (s32[2,8,128]{2,1,0:T(8,128)S(1)}, s32[2,8,128]{2,1,0:T(8,128)S(1)}, u32[]{:S(2)}, u32[]{:S(2)}) collective-permute-start(s32[2,8,128]{2,1,0:T(8,128)S(1)} %slice.3), channel_id=1, source_target_pairs={{0,8},{1,9},{2,10},{3,11},{4,12},{5,13},{6,14},{7,15},{8,0},{9,1},... | collective-permute-start | bytes 24584 | tf_op jit(solution)/shard_map/ppermute | solution.py:25
  12.8 2.0 %prepare.1 = (s32[32,128]{1,0:T(8,128)S(1)}, bf16[256,256]{1,0:T(8,128)(2,1)S(1)}, bf16[1024,256]{1,0:T(8,128)(2,1)S(1)}, bf16[768,128]{1,0:T(8,128)(2,1)S(1)}, ...) custom-call(s32[2,32,128]{2,1,0:T(8,128)} %refs_0_.1, ...), custom_call_target="tpu_custom_call" | custom-call | tf_op jit(solution)/shard_map/prepare/pallas_call | solution.py:182
  14.8 4.5 %collective-permute-done.polar = s32[2,8,128]{2,1,0:T(8,128)S(1)} collective-permute-done((s32[2,8,128]{2,1,0:T(8,128)S(1)}, s32[2,8,128]{2,1,0:T(8,128)S(1)}, u32[]{:S(2)}, u32[]{:S(2)}) %collective-permute-start) | collective-permute-done | bytes 8224 | tf_op jit(solution)/shard_map/ppermute | solution.py:25
  19.3 0.1 all-to-all-done.block
  19.4 1.0 %remap.1 = (bf16[1280,128]{1,0:T(8,128)(2,1)S(1)}, bf16[80,128]{1,0:T(8,128)(2,1)S(1)}, bf16[80,128]{1,0:T(8,128)(2,1)S(1)}, f32[256,128]{1,0:T(8,128)S(1)}) custom-call(bf16[16,64,128]{2,1,0:T(8,128)(2,1)S(1)} %all-to-all-done.block, s32[32,128]{1,0:T(8,128)S(1)} %get-tuple-element.24.places, s32[2,8,128]{2,1,0:T(8,128)S(1)} %collective-permute-done.polar), custom_call_target="tpu_custom_call" | custom-call | tf_op jit(solution)/shard_map/remap/pallas_call | solution.py:244
  20.4 0.1 collective-permute-start.1
  20.5 2.3 %collective-permute-start.2 = (bf16[80,128]{1,0:T(8,128)(2,1)S(1)}, bf16[80,128]{1,0:T(8,128)(2,1)S(1)}, u32[]{:S(2)}, u32[]{:S(2)}) collective-permute-start(bf16[80,128]{1,0:T(8,128)(2,1)S(1)} %get-tuple-element.27), channel_id=1, source_target_pairs={{1,2},{3,4},{5,6},{7,8},{9,10},{11,12},{13,14},{15,0},{2,1},{4,3},... | collective-permute-start | bytes 61448 | tf_op jit(solution)/shard_map/ppermute | solution.py:20
  22.8 4.3 %inside.1 = (f32[256,128]{1,0:T(8,128)S(1)}, f32[23,256]{1,0:T(8,128)S(1)}, f32[23,256]{1,0:T(8,128)S(1)}, f32[23,128]{1,0:T(8,128)S(1)}, f32[23,128]{1,0:T(8,12...) custom-call(bf16[1280,128]{1,0:T(8,128)(2,1)S(1)} %get-tuple-element.25.cells, ...), custom_call_target="tpu_custom_call" | custom-call | flops 4000000000 | bytes 4000000 | tf_op jit(solution)/shard_map/inside/pallas_call | solution.py:575
  27.1 0.0 collective-permute-done.1.inner
  27.1 0.0 collective-permute-done.2.outer
  27.1 2.6 %edges.1 = f32[8,32,128]{2,1,0:T(8,128)} custom-call(bf16[1280,128]{1,0:T(8,128)(2,1)S(1)} %get-tuple-element.25.cells, bf16[80,128]{1,0:T(8,128)(2,1)S(1)} %collective-permute-done.1.inner, bf16[80,128]{1,0:T(8,128)(2,1)S(1)} %collective-permute-done.2.outer, bf16[256,256]{1,0:T(8,128)(2,1)S(1)} %get-tuple-element.28.w1, ...), custom_call_target="tpu_custom_call" | custom-call | tf_op jit(solution)/shard_map/edges/pallas_call | solution.py:587
Async XLA Ops:
  1.9 17.5 %all-to-all-start = ((bf16[16,64,128]{2,1,0:T(8,128)(2,1)}), bf16[16,64,128]{2,1,0:T(8,128)(2,1)S(1)}, u32[]{:S(2)}, u32[]{:S(2)}) async-start(bf16[16,64,128]{2,1,0:T(8,128)(2,1)} %pack.1), calls=%async_computation | async-start | bytes 524288 | tf_op jit(solution)/shard_map/all_to_all | solution.py:611
  10.0 9.3 %collective-permute-start = (s32[2,8,128]{2,1,0:T(8,128)S(1)}, s32[2,8,128]{2,1,0:T(8,128)S(1)}, u32[]{:S(2)}, u32[]{:S(2)}) collective-permute-start(s32[2,8,128]{2,1,0:T(8,128)S(1)} %slice.3), channel_id=1, source_target_pairs={{0,8},{1,9},{2,10},{3,11},{4,12},{5,13},{6,14},{7,15},{8,0},{9,1},... | collective-permute-start | bytes 24584 | tf_op jit(solution)/shard_map/ppermute | solution.py:25
  20.4 6.7 %collective-permute-start.1 = (bf16[80,128]{1,0:T(8,128)(2,1)S(1)}, bf16[80,128]{1,0:T(8,128)(2,1)S(1)}, u32[]{:S(2)}, u32[]{:S(2)}) collective-permute-start(bf16[80,128]{1,0:T(8,128)(2,1)S(1)} %get-tuple-element.26), channel_id=1, source_target_pairs={{0,1},{2,3},{4,5},{6,7},{8,9},{10,11},{12,13},{14,15},{1,0},{3,2},... | collective-permute-start | bytes 61448 | tf_op jit(solution)/shard_map/ppermute | solution.py:20
  20.5 6.6 %collective-permute-start.2 = (bf16[80,128]{1,0:T(8,128)(2,1)S(1)}, bf16[80,128]{1,0:T(8,128)(2,1)S(1)}, u32[]{:S(2)}, u32[]{:S(2)}) collective-permute-start(bf16[80,128]{1,0:T(8,128)(2,1)S(1)} %get-tuple-element.27), channel_id=1, source_target_pairs={{1,2},{3,4},{5,6},{7,8},{9,10},{11,12},{13,14},{15,0},{2,1},{4,3},... | collective-permute-start | bytes 61448 | tf_op jit(solution)/shard_map/ppermute | solution.py:20

commit v6 on v5

--- a/solution.py
+++ b/solution.py
@@ -10,8 +10,8 @@
 HALO = 4
 EDGE_ROWS = 9
 AHEAD = 2
+PARTS = 4
 POLAR = 3
-PARTS = 4
 
 
 def swap(block, axis, first):
@@ -25,62 +25,43 @@
     return lax.ppermute(block, axis, [(i, (i + devices // 2) % devices) for i in range(devices)])
 
 
-def pack_kernel(fields_hbm, parcels_hbm, fields, parcels, in_sems, out_sems):
-    channels, rows, _ = fields.shape
-    devices, depth, columns = parcels.shape
-    depth = rows * channels
-    parts = in_sems.shape[0]
-    span = devices // parts
-
-    def lanes(n):
-        return slice(n * span * columns, (n + 1) * span * columns)
-
-    loads = [
-        pltpu.make_async_copy(fields_hbm.at[:, :, lanes(n)], fields.at[:, :, lanes(n)], in_sems.at[n])
-        for n in range(parts)
-    ]
-    for load in loads:
-        load.start()
-    stores = []
-
-    def send(targets, part):
-        at = parcels.at[targets, part, :], parcels_hbm.at[targets, part, :]
-        stores.append(pltpu.make_async_copy(*at, out_sems.at[len(stores)]))
-        stores[-1].start()
-
-    for n in range(parts):
-        loads[n].wait()
-        values = fields[:, :, lanes(n)].astype(F32)
+def pack_kernel(fields_hbm, parcels, fields, load_sems, sems):
+    devices, channels, _, columns = fields.shape
+    span = devices // PARTS
+    loads = []
+    for target in range(devices):
+        lanes = slice(target * columns, (target + 1) * columns)
+        loads.append(pltpu.make_async_copy(fields_hbm.at[:, :, lanes], fields.at[target], load_sems.at[target]))
+        loads[-1].start()
+    copies = []
+    for n in range(PARTS):
+        for load in loads[n * span : (n + 1) * span]:
+            load.wait()
         first, other = n * span, (n * span + devices // 2) % devices
-        for row in range(rows):
-            line = values[:, row, :].astype(BF16)
-            for m in range(span):
-                piece = line[:, m * columns : (m + 1) * columns]
-                parcels[first + m, row * channels : (row + 1) * channels, :] = piece
-                parcels[other + m, depth + row * channels : depth + (row + 1) * channels, :] = piece
-        send(slice(first, first + span), slice(0, depth))
-        send(slice(other, other + span), slice(depth, 2 * depth))
-    for store in stores:
-        store.wait()
+        places = parcels.at[first : first + span, :channels], parcels.at[other : other + span, channels:]
+        for place in places:
+            copies.append(pltpu.make_async_copy(fields.at[first : first + span], place, sems.at[len(copies)]))
+            copies[-1].start()
+    for copy in copies:
+        copy.wait()
 
 
 def pack(fields, devices, columns):
     channels, rows, _ = fields.shape
-    shape = (devices, 2 * rows * channels, columns)
-    return pl.pallas_call(
+    parcels = pl.pallas_call(
         pack_kernel,
         in_specs=[pl.BlockSpec(memory_space=pltpu.HBM)],
         out_specs=pl.BlockSpec(memory_space=pltpu.HBM),
-        out_shape=pltpu.HBM(shape, BF16),
+        out_shape=pltpu.HBM((devices, 2 * channels, rows, columns), BF16),
         scratch_shapes=[
-            pltpu.VMEM(fields.shape, BF16),
-            pltpu.VMEM(shape, BF16),
-            pltpu.SemaphoreType.DMA((PARTS,)),
+            pltpu.VMEM((devices, channels, rows, columns), BF16),
+            pltpu.SemaphoreType.DMA((devices,)),
             pltpu.SemaphoreType.DMA((2 * PARTS,)),
         ],
         compiler_params=pltpu.CompilerParams(vmem_limit_bytes=16 * 2**20),
         name="pack",
     )(pltpu.with_memory_space_constraint(fields, pltpu.HBM))
+    return parcels.reshape(devices, 2 * channels * rows, columns)
 
 
 def tap(kernel_ref, row, col):
@@ -189,7 +170,7 @@
     )(*[pltpu.with_memory_space_constraint(a, pltpu.HBM) for a in args])
 
 
-def remap_kernel(block, places, polar, cells, inner, outer, skip):
+def remap_kernel(block, places, polar, cells, inner, outer, skip, wide):
     even = lax.rem(lax.axis_index("lon"), 2) == 0
     devices, depth, columns = block.shape
     depth = depth // 2
@@ -200,12 +181,15 @@
     offsets = lax.rem(lines, 2 * columns).astype(F32)
     line_at = lax.broadcasted_iota(jnp.int32, (2 * columns, columns), 0).astype(F32)
     half = columns // 2
+    wide[...] = block[...].astype(F32).reshape(wide.shape)
     fields = []
     for side in range(2):
-        at = side * depth
-        upper = block[:, at : at + channels, :].reshape(devices * channels, columns)
-        lower = block[:, at + channels : at + depth, :].reshape(devices * channels, columns)
-        fields.append(jnp.concatenate([upper, lower], axis=1))
+        parts = []
+        for row in range(2):
+            places_of = [s * 2 * depth + side * depth + row for s in range(devices)]
+            lines = [wide[pl.ds(at, channels, stride=2), :] for at in places_of]
+            parts.append(jnp.concatenate(lines, axis=0).astype(BF16))
+        fields.append(jnp.concatenate(parts, axis=1))
     pairs = cells.shape[0] // columns
     begins, finishes = [], []
     own_pairs = skip.shape[0] // 32
@@ -249,6 +233,7 @@
             jax.ShapeDtypeStruct((count * 2 * HALO, columns), BF16),
             jax.ShapeDtypeStruct((grid_rows * 8, columns), F32),
         ],
+        scratch_shapes=[pltpu.VMEM((block.shape[0] * block.shape[1], columns), F32)],
         compiler_params=pltpu.CompilerParams(vmem_limit_bytes=16 * 2**20),
         name="remap",
     )(block, places, polar)

time: 30.1 us -> 29.9 us (level)
  no operation moved by 1% of the time
where the time goes in v6:
time: 29.9 us; the launch traced here: 29.6 us
  starting transfers between devices  12.6 us (42%)
  Pallas kernels  11.6 us (39%)
  waiting for transfers between devices  4.59 us (15%)
  local copies, waits for them, and re-layouts  0.7 us (2%)
    all_to_all x1, starting transfers between devices, shards(): lax.all_to_all(parcels, 'lon', split_axis=0, concat_axis=0, tiled=True)  7.4 us
    ppermute x1, waiting for transfers between devices, opposite(): lax.ppermute(block, axis, [(i, (i + devices // 2) % devices) for i in ran...  4.45 us
    pallas_call x1, Pallas kernels, inside(): pl.pallas_call(inside_kernel, out_shape=[jax.ShapeDtypeStruct((blocks * 1...  4.29 us
    ppermute x1, starting transfers between devices, opposite(): lax.ppermute(block, axis, [(i, (i + devices // 2) % devices) for i in ran...  2.83 us
    pallas_call x1, Pallas kernels, edges(): pl.pallas_call(edges_kernel, out_shape=jax.ShapeDtypeStruct(out_shape, F3...  2.63 us
    ppermute x2, starting transfers between devices, swap(): return lax.ppermute(block, axis, pairs + [(b, a) for a, b in pairs])  2.4 us
    pallas_call x1, Pallas kernels, prepare(): pl.pallas_call(prepare_kernel, in_specs=[pl.BlockSpec(memory_space=pltpu....  2.01 us
    pallas_call x1, Pallas kernels, pack(): pl.pallas_call(pack_kernel, in_specs=[pl.BlockSpec(memory_space=pltpu.HBM...  1.73 us
  transfers between devices with their start and end apart: 4, of which 2 were waited for; matrix products, arithmetic and copies ran while one was open for 2% of the time, Pallas kernels for 21%

profile of v6, /device:TPU:0, one launch (start us, length us, event | category | flops | bytes accessed | tf_op | source)
XLA Modules:
  0.0 29.6 jit_solution(4384331172321579417)
XLA Ops:
  0.0 1.7 %pack.1 = bf16[16,32,2,128]{3,2,1,0:T(2,128)(2,1)} custom-call(bf16[16,2,2048]{2,1,0:T(2,128)(2,1)} %fields_hbm.1), custom_call_target="tpu_custom_call" | custom-call | tf_op jit(solution)/shard_map/pack/pallas_call | solution.py:51
  1.7 7.4 %all-to-all-start = ((bf16[16,64,128]{2,1,0:T(8,128)(2,1)}), bf16[16,64,128]{2,1,0:T(8,128)(2,1)S(1)}, u32[]{:S(2)}, u32[]{:S(2)}) async-start(bf16[16,64,128]{2,1,0:T(8,128)(2,1)} %bitcast.3), calls=%async_computation | async-start | bytes 524288 | tf_op jit(solution)/shard_map/all_to_all | solution.py:596
  9.1 0.7 %slice.3 = s32[2,8,128]{2,1,0:T(8,128)S(1)} slice(s32[2,32,128]{2,1,0:T(8,128)} %refs_0_.1), slice={[0:2], [0:8], [0:128]} | slice | bytes 16384 | tf_op jit(solution)/shard_map/slice | solution.py:594
  9.8 2.8 %collective-permute-start = (s32[2,8,128]{2,1,0:T(8,128)S(1)}, s32[2,8,128]{2,1,0:T(8,128)S(1)}, u32[]{:S(2)}, u32[]{:S(2)}) collective-permute-start(s32[2,8,128]{2,1,0:T(8,128)S(1)} %slice.3), channel_id=1, source_target_pairs={{0,8},{1,9},{2,10},{3,11},{4,12},{5,13},{6,14},{7,15},{8,0},{9,1},... | collective-permute-start | bytes 24584 | tf_op jit(solution)/shard_map/ppermute | solution.py:25
  12.7 2.0 %prepare.1 = (s32[32,128]{1,0:T(8,128)S(1)}, bf16[256,256]{1,0:T(8,128)(2,1)S(1)}, bf16[1024,256]{1,0:T(8,128)(2,1)S(1)}, bf16[768,128]{1,0:T(8,128)(2,1)S(1)}, ...) custom-call(s32[2,32,128]{2,1,0:T(8,128)} %refs_0_.1, ...), custom_call_target="tpu_custom_call" | custom-call | tf_op jit(solution)/shard_map/prepare/pallas_call | solution.py:163
  14.7 4.5 %collective-permute-done.polar = s32[2,8,128]{2,1,0:T(8,128)S(1)} collective-permute-done((s32[2,8,128]{2,1,0:T(8,128)S(1)}, s32[2,8,128]{2,1,0:T(8,128)S(1)}, u32[]{:S(2)}, u32[]{:S(2)}) %collective-permute-start) | collective-permute-done | bytes 8224 | tf_op jit(solution)/shard_map/ppermute | solution.py:25
  19.1 0.1 all-to-all-done.block
  19.3 1.0 %remap.1 = (bf16[1280,128]{1,0:T(8,128)(2,1)S(1)}, bf16[80,128]{1,0:T(8,128)(2,1)S(1)}, bf16[80,128]{1,0:T(8,128)(2,1)S(1)}, f32[256,128]{1,0:T(8,128)S(1)}) custom-call(bf16[16,64,128]{2,1,0:T(8,128)(2,1)S(1)} %all-to-all-done.block, s32[32,128]{1,0:T(8,128)S(1)} %get-tuple-element.24.places, s32[2,8,128]{2,1,0:T(8,128)S(1)} %collective-permute-done.polar), custom_call_target="tpu_custom_call" | custom-call | tf_op jit(solution)/shard_map/remap/pallas_call | solution.py:228
  20.2 0.1 collective-permute-start.1
  20.3 2.3 %collective-permute-start.2 = (bf16[80,128]{1,0:T(8,128)(2,1)S(1)}, bf16[80,128]{1,0:T(8,128)(2,1)S(1)}, u32[]{:S(2)}, u32[]{:S(2)}) collective-permute-start(bf16[80,128]{1,0:T(8,128)(2,1)S(1)} %get-tuple-element.27), channel_id=1, source_target_pairs={{1,2},{3,4},{5,6},{7,8},{9,10},{11,12},{13,14},{15,0},{2,1},{4,3},... | collective-permute-start | bytes 61448 | tf_op jit(solution)/shard_map/ppermute | solution.py:20
  22.7 4.3 %inside.1 = (f32[256,128]{1,0:T(8,128)S(1)}, f32[23,256]{1,0:T(8,128)S(1)}, f32[23,256]{1,0:T(8,128)S(1)}, f32[23,128]{1,0:T(8,128)S(1)}, f32[23,128]{1,0:T(8,12...) custom-call(bf16[1280,128]{1,0:T(8,128)(2,1)S(1)} %get-tuple-element.25.cells, ...), custom_call_target="tpu_custom_call" | custom-call | flops 4000000000 | bytes 4000000 | tf_op jit(solution)/shard_map/inside/pallas_call | solution.py:560
  27.0 0.0 collective-permute-done.1.inner
  27.0 0.0 collective-permute-done.2.outer
  27.0 2.6 %edges.1 = f32[8,32,128]{2,1,0:T(8,128)} custom-call(bf16[1280,128]{1,0:T(8,128)(2,1)S(1)} %get-tuple-element.25.cells, bf16[80,128]{1,0:T(8,128)(2,1)S(1)} %collective-permute-done.1.inner, bf16[80,128]{1,0:T(8,128)(2,1)S(1)} %collective-permute-done.2.outer, bf16[256,256]{1,0:T(8,128)(2,1)S(1)} %get-tuple-element.28.w1, ...), custom_call_target="tpu_custom_call" | custom-call | tf_op jit(solution)/shard_map/edges/pallas_call | solution.py:572
Async XLA Ops:
  1.7 17.5 %all-to-all-start = ((bf16[16,64,128]{2,1,0:T(8,128)(2,1)}), bf16[16,64,128]{2,1,0:T(8,128)(2,1)S(1)}, u32[]{:S(2)}, u32[]{:S(2)}) async-start(bf16[16,64,128]{2,1,0:T(8,128)(2,1)} %bitcast.3), calls=%async_computation | async-start | bytes 524288 | tf_op jit(solution)/shard_map/all_to_all | solution.py:596
  9.8 9.3 %collective-permute-start = (s32[2,8,128]{2,1,0:T(8,128)S(1)}, s32[2,8,128]{2,1,0:T(8,128)S(1)}, u32[]{:S(2)}, u32[]{:S(2)}) collective-permute-start(s32[2,8,128]{2,1,0:T(8,128)S(1)} %slice.3), channel_id=1, source_target_pairs={{0,8},{1,9},{2,10},{3,11},{4,12},{5,13},{6,14},{7,15},{8,0},{9,1},... | collective-permute-start | bytes 24584 | tf_op jit(solution)/shard_map/ppermute | solution.py:25
  20.2 6.7 %collective-permute-start.1 = (bf16[80,128]{1,0:T(8,128)(2,1)S(1)}, bf16[80,128]{1,0:T(8,128)(2,1)S(1)}, u32[]{:S(2)}, u32[]{:S(2)}) collective-permute-start(bf16[80,128]{1,0:T(8,128)(2,1)S(1)} %get-tuple-element.26), channel_id=1, source_target_pairs={{0,1},{2,3},{4,5},{6,7},{8,9},{10,11},{12,13},{14,15},{1,0},{3,2},... | collective-permute-start | bytes 61448 | tf_op jit(solution)/shard_map/ppermute | solution.py:20
  20.3 6.6 %collective-permute-start.2 = (bf16[80,128]{1,0:T(8,128)(2,1)S(1)}, bf16[80,128]{1,0:T(8,128)(2,1)S(1)}, u32[]{:S(2)}, u32[]{:S(2)}) collective-permute-start(bf16[80,128]{1,0:T(8,128)(2,1)S(1)} %get-tuple-element.27), channel_id=1, source_target_pairs={{1,2},{3,4},{5,6},{7,8},{9,10},{11,12},{13,14},{15,0},{2,1},{4,3},... | collective-permute-start | bytes 61448 | tf_op jit(solution)/shard_map/ppermute | solution.py:20

commit v7 on v6

--- a/solution.py
+++ b/solution.py
@@ -170,73 +170,101 @@
     )(*[pltpu.with_memory_space_constraint(a, pltpu.HBM) for a in args])
 
 
-def remap_kernel(block, places, polar, cells, inner, outer, skip, wide):
-    even = lax.rem(lax.axis_index("lon"), 2) == 0
+def collect(block, side, places, wide):
     devices, depth, columns = block.shape
     depth = depth // 2
     channels = depth // 2
-    lines = [places[...], locate(polar[0], lax.rem(polar[1], columns))]
-    lines = jnp.concatenate(lines, axis=0)
-    sources = lax.div(lines, 2 * columns)
-    offsets = lax.rem(lines, 2 * columns).astype(F32)
+    wide[...] = block[:, side * depth : (side + 1) * depth, :].astype(F32).reshape(wide.shape)
+    parts = []
+    for row in range(2):
+        lines = [wide[pl.ds(s * depth + row, channels, stride=2), :] for s in range(devices)]
+        parts.append(jnp.concatenate(lines, axis=0).astype(BF16))
+    fields = jnp.concatenate(parts, axis=1)
+    sources = lax.div(places, 2 * columns)
+    offsets = lax.rem(places, 2 * columns).astype(F32)
     line_at = lax.broadcasted_iota(jnp.int32, (2 * columns, columns), 0).astype(F32)
-    half = columns // 2
-    wide[...] = block[...].astype(F32).reshape(wide.shape)
-    fields = []
-    for side in range(2):
-        parts = []
-        for row in range(2):
-            places_of = [s * 2 * depth + side * depth + row for s in range(devices)]
-            lines = [wide[pl.ds(at, channels, stride=2), :] for at in places_of]
-            parts.append(jnp.concatenate(lines, axis=0).astype(BF16))
-        fields.append(jnp.concatenate(parts, axis=1))
-    pairs = cells.shape[0] // columns
-    begins, finishes = [], []
-    own_pairs = skip.shape[0] // 32
-    for pair in range(pairs):
-        own = pair < own_pairs
+    for pair in range(places.shape[0] // 4):
         chosen = []
         for n in range(4):
             here = line_at == jnp.broadcast_to(offsets[4 * pair + n : 4 * pair + n + 1, :], line_at.shape)
             chosen.append(jnp.where(here, 1.0, 0.0).astype(BF16))
-        found = jnp.dot(fields[0 if own else 1], jnp.concatenate(chosen, axis=1), preferred_element_type=F32)
+        found = jnp.dot(fields, jnp.concatenate(chosen, axis=1), preferred_element_type=F32)
         lines = []
         for n in range(4):
-            line = sources[4 * pair + n : 4 * pair + n + 1, :]
-            line = jnp.broadcast_to(line, (channels, columns))
+            line = jnp.broadcast_to(sources[4 * pair + n : 4 * pair + n + 1, :], (channels, columns))
             total = jnp.zeros((channels, columns), F32)
             for s in range(devices):
                 value = found[s * channels : (s + 1) * channels, n * columns : (n + 1) * columns]
                 total = jnp.where(line == s, value, total)
             lines.append(total)
-            if own:
-                skip[(pair * 4 + n) * 8 : (pair * 4 + n + 1) * 8, :] = total[:8]
-        turned = jnp.concatenate(lines + lines, axis=0).T
-        cells[pair * columns : (pair + 1) * columns, :] = turned.astype(BF16)
-        for i in range(2):
-            begins.append(turned[i * half : i * half + HALO])
-            finishes.append(turned[(i + 1) * half - HALO : (i + 1) * half])
+        yield pair, lines
+
+
+def cells_of(lines, pair, cells):
+    turned = jnp.concatenate(lines + lines, axis=0).T
+    columns = turned.shape[0]
+    half = columns // 2
+    cells[pair * columns : (pair + 1) * columns, :] = turned.astype(BF16)
+    begin = [turned[i * half : i * half + HALO] for i in range(2)]
+    finish = [turned[(i + 1) * half - HALO : (i + 1) * half] for i in range(2)]
+    return jnp.concatenate(begin, axis=0), jnp.concatenate(finish, axis=0)
+
+
+def own_kernel(block, places, cells, begin, finish, skip, wide):
+    for pair, lines in collect(block, 0, places[...], wide):
+        for n in range(4):
+            skip[(pair * 4 + n) * 8 : (pair * 4 + n + 1) * 8, :] = lines[n][:8]
+        rows = slice(pair * 2 * HALO, (pair + 1) * 2 * HALO)
+        begin[rows, :], finish[rows, :] = cells_of(lines, pair, cells)
+
+
+def remap_own(block, places):
+    devices, depth, columns = block.shape
+    grid_rows = places.shape[0]
+    count = grid_rows // 4
+    return pl.pallas_call(
+        own_kernel,
+        out_shape=[
+            jax.ShapeDtypeStruct((count * columns, columns), BF16),
+            jax.ShapeDtypeStruct((count * 2 * HALO, columns), F32),
+            jax.ShapeDtypeStruct((count * 2 * HALO, columns), F32),
+            jax.ShapeDtypeStruct((grid_rows * 8, columns), F32),
+        ],
+        scratch_shapes=[pltpu.VMEM((devices * depth // 2, columns), F32)],
+        compiler_params=pltpu.CompilerParams(vmem_limit_bytes=16 * 2**20),
+        name="remap_own",
+    )(block, places)
+
+
+def polar_kernel(block, polar, begin, finish, cells, inner, outer, wide):
+    columns = block.shape[2]
+    places = locate(polar[0], lax.rem(polar[1], columns))
+    begins, finishes = [begin[...]], [finish[...]]
+    for pair, lines in collect(block, 1, places, wide):
+        first, last = cells_of(lines, pair, cells)
+        begins.append(first)
+        finishes.append(last)
+    even = lax.rem(lax.axis_index("lon"), 2) == 0
     begins, finishes = jnp.concatenate(begins, axis=0), jnp.concatenate(finishes, axis=0)
     inner[...] = jnp.where(even, finishes, begins).astype(BF16)
     outer[...] = jnp.where(even, begins, finishes).astype(BF16)
 
 
-def remap(block, places, polar):
-    columns = block.shape[2]
-    grid_rows = places.shape[0]
-    count = (grid_rows + polar.shape[1]) // 4
+def remap_polar(block, polar, begin, finish):
+    devices, depth, columns = block.shape
+    count = polar.shape[1] // 4
+    rows = begin.shape[0] + count * 2 * HALO
     return pl.pallas_call(
-        remap_kernel,
+        polar_kernel,
         out_shape=[
             jax.ShapeDtypeStruct((count * columns, columns), BF16),
-            jax.ShapeDtypeStruct((count * 2 * HALO, columns), BF16),
-            jax.ShapeDtypeStruct((count * 2 * HALO, columns), BF16),
-            jax.ShapeDtypeStruct((grid_rows * 8, columns), F32),
+            jax.ShapeDtypeStruct((rows, columns), BF16),
+            jax.ShapeDtypeStruct((rows, columns), BF16),
         ],
-        scratch_shapes=[pltpu.VMEM((block.shape[0] * block.shape[1], columns), F32)],
+        scratch_shapes=[pltpu.VMEM((devices * depth // 2, columns), F32)],
         compiler_params=pltpu.CompilerParams(vmem_limit_bytes=16 * 2**20),
-        name="remap",
-    )(block, places, polar)
+        name="remap_polar",
+    )(block, polar, begin, finish)
 
 
 def silu(values):
@@ -411,7 +439,7 @@
 SHARED_KEYS = [(name, lanes, shift) for name, lanes, shifts in SHARED for shift in shifts]
 
 
-def inside_kernel(cells, skip, w1, w2, wd, wc, wu, wm, wp, update, *refs):
+def inside_kernel(cells, polar_cells, skip, w1, w2, wd, wc, wu, wm, wp, update, *refs):
     shared, scratch = refs[: len(SHARED_KEYS)], refs[len(SHARED_KEYS) :]
     half = update.shape[1] // 2
     blocks = update.shape[0] // 16
@@ -435,7 +463,8 @@
     for row in (at.top, at.bottom, at.pole, at.count - 1):
         x0[at(row), :] = jnp.zeros((half, 128), F32)
     for i in range(blocks + POLAR):
-        x0[at(at.of(i)), :] = cells[i * half : (i + 1) * half, :].astype(F32)
+        own, n = (cells, i) if i < blocks else (polar_cells, i - blocks)
+        x0[at(at.of(i)), :] = own[n * half : (n + 1) * half, :].astype(F32)
     stages = layers(at, groups, pairs, moved, *scratch, w1, w2, wd, wc, wu)
 
     y2, yu = scratch[3], scratch[6]
@@ -467,7 +496,7 @@
     run(at, stages + [[last(*ranges[-1]) for ranges in groups]], AHEAD)
 
 
-def edges_kernel(cells, inner, outer, w1, w2, wd, wc, wu, wm, wp, update, *refs):
+def edges_kernel(cells, polar_cells, inner, outer, w1, w2, wd, wc, wu, wm, wp, update, *refs):
     shared, out, scratch = refs[: len(SHARED_KEYS)], refs[len(SHARED_KEYS)], refs[len(SHARED_KEYS) + 1 :]
     even = lax.rem(lax.axis_index("lon"), 2) == 0
     half = out.shape[2] // 2
@@ -483,8 +512,9 @@
         x0[at(row), :] = jnp.zeros((step, 128), F32)
     for i in range(blocks + POLAR):
         row = at.of(i)
-        begin = cells[i * half : i * half + 16, :].astype(F32)
-        finish = cells[(i + 1) * half - 16 : (i + 1) * half, :].astype(F32)
+        own, n = (cells, i) if i < blocks else (polar_cells, i - blocks)
+        begin = own[n * half : n * half + 16, :].astype(F32)
+        finish = own[(n + 1) * half - 16 : (n + 1) * half, :].astype(F32)
         base = row * step
         x0[base : base + HALO, :] = left[i * HALO : (i + 1) * HALO]
         x0[base + HALO : base + 2 * HALO, :] = begin[:HALO]
@@ -553,7 +583,7 @@
     return [pltpu.VMEM((rows, lanes), dtype) for lanes, dtype in shapes]
 
 
-def inside(cells, skip, weights):
+def inside(cells, polar_cells, skip, weights):
     columns = skip.shape[1]
     blocks = skip.shape[0] // 16
     rows = Rows(columns // 2, blocks).count
@@ -565,17 +595,17 @@
         compiler_params=pltpu.CompilerParams(vmem_limit_bytes=20 * 2**20),
         cost_estimate=pl.CostEstimate(flops=4 * 10**9, bytes_accessed=4 * 10**6, transcendentals=0),
         name="inside",
-    )(cells, skip, *weights)
-
-
-def edges(out_shape, cells, inner, outer, weights, found):
+    )(cells, polar_cells, skip, *weights)
+
+
+def edges(out_shape, cells, polar_cells, inner, outer, weights, found):
     return pl.pallas_call(
         edges_kernel,
         out_shape=jax.ShapeDtypeStruct(out_shape, F32),
         scratch_shapes=buffers(4 * HALO, out_shape[1] // 2),
         compiler_params=pltpu.CompilerParams(vmem_limit_bytes=20 * 2**20),
         name="edges",
-    )(cells, inner, outer, *weights, *found)
+    )(cells, polar_cells, inner, outer, *weights, *found)
 
 
 def shards(
@@ -597,11 +627,12 @@
     places, *weights = prepare(
         remap_table, kernel_first, kernel_second, kernel_down, kernel_coarse, kernel_up, kernel_merge, projection
     )
-    cells, inner, outer, skip = remap(block, places, polar)
+    cells, begin, finish, skip = remap_own(block, places)
+    polar_cells, inner, outer = remap_polar(block, polar, begin, finish)
     outer = swap(outer, "lon", 1)
     inner = swap(inner, "lon", 0)
-    found = inside(cells, skip, weights)
-    return edges((projection.shape[0], grid_rows, columns), cells, inner, outer, weights, found)
+    found = inside(cells, polar_cells, skip, weights)
+    return edges((projection.shape[0], grid_rows, columns), cells, polar_cells, inner, outer, weights, found)
 
 
 def solution(mesh):

time: 29.9 us -> 29.7 us (level)
  starting transfers between devices: 12.6 us -> 12.1 us
  Pallas kernels: 11.6 us -> 12 us
    all_to_all x1, waiting for transfers between devices: 0.14 us -> 4.59 us  [shards(): lax.all_to_all(parcels, 'lon', split_axis=0, concat_axis=0, tiled=True)]
    ppermute x1, waiting for transfers between devices: 4.45 us -> 0.01 us  [opposite(): lax.ppermute(block, axis, [(i, (i + devices // 2) % devices) for i in ran...]
    ppermute x2, starting transfers between devices: 2.4 us -> 1.86 us  [swap(): return lax.ppermute(block, axis, pairs + [(b, a) for a, b in pairs])]
    pallas_call x1 -> x2, Pallas kernels: 0.96 us -> 1.31 us  [the longest x1 0.82 us: remap_own(): pl.pallas_call(own_kernel, out_shape=[jax.ShapeDtypeStruct((count * colum...]
  transfers between devices with their start and end apart: 4 -> 4, of which waited for: 2 -> 1; matrix products, arithmetic and copies ran while one was open for 2% -> 2% of each run, Pallas kernels for 21% -> 24%
where the time goes in v7:
time: 29.7 us; the launch traced here: 29.4 us
  starting transfers between devices  12.1 us (41%)
  Pallas kernels  12 us (40%)
  waiting for transfers between devices  4.59 us (15%)
  local copies, waits for them, and re-layouts  0.7 us (2%)
    all_to_all x1, starting transfers between devices, shards(): lax.all_to_all(parcels, 'lon', split_axis=0, concat_axis=0, tiled=True)  7.4 us
    all_to_all x1, waiting for transfers between devices, shards(): lax.all_to_all(parcels, 'lon', split_axis=0, concat_axis=0, tiled=True)  4.59 us
    pallas_call x1, Pallas kernels, inside(): pl.pallas_call(inside_kernel, out_shape=[jax.ShapeDtypeStruct((blocks * 1...  4.3 us
    ppermute x1, starting transfers between devices, opposite(): lax.ppermute(block, axis, [(i, (i + devices // 2) % devices) for i in ran...  2.83 us
    pallas_call x1, Pallas kernels, edges(): pl.pallas_call(edges_kernel, out_shape=jax.ShapeDtypeStruct(out_shape, F3...  2.63 us
    pallas_call x1, Pallas kernels, prepare(): pl.pallas_call(prepare_kernel, in_specs=[pl.BlockSpec(memory_space=pltpu....  2.01 us
    ppermute x2, starting transfers between devices, swap(): return lax.ppermute(block, axis, pairs + [(b, a) for a, b in pairs])  1.86 us
    pallas_call x1, Pallas kernels, pack(): pl.pallas_call(pack_kernel, in_specs=[pl.BlockSpec(memory_space=pltpu.HBM...  1.73 us
  transfers between devices with their start and end apart: 4, of which 1 were waited for; matrix products, arithmetic and copies ran while one was open for 2% of the time, Pallas kernels for 24%

profile of v7, /device:TPU:0, one launch (start us, length us, event | category | flops | bytes accessed | tf_op | source)
XLA Modules:
  0.0 29.4 jit_solution(14745074786192828779)
XLA Ops:
  0.0 1.7 %pack.1 = bf16[16,32,2,128]{3,2,1,0:T(2,128)(2,1)} custom-call(bf16[16,2,2048]{2,1,0:T(2,128)(2,1)} %fields_hbm.1), custom_call_target="tpu_custom_call" | custom-call | tf_op jit(solution)/shard_map/pack/pallas_call | solution.py:51
  1.7 7.4 %all-to-all-start = ((bf16[16,64,128]{2,1,0:T(8,128)(2,1)}), bf16[16,64,128]{2,1,0:T(8,128)(2,1)S(1)}, u32[]{:S(2)}, u32[]{:S(2)}) async-start(bf16[16,64,128]{2,1,0:T(8,128)(2,1)} %bitcast.3), calls=%async_computation | async-start | bytes 524288 | tf_op jit(solution)/shard_map/all_to_all | solution.py:626
  9.1 0.7 %slice.3 = s32[2,8,128]{2,1,0:T(8,128)S(1)} slice(s32[2,32,128]{2,1,0:T(8,128)} %refs_0_.1), slice={[0:2], [0:8], [0:128]} | slice | bytes 16384 | tf_op jit(solution)/shard_map/slice | solution.py:624
  9.8 2.8 %collective-permute-start = (s32[2,8,128]{2,1,0:T(8,128)S(1)}, s32[2,8,128]{2,1,0:T(8,128)S(1)}, u32[]{:S(2)}, u32[]{:S(2)}) collective-permute-start(s32[2,8,128]{2,1,0:T(8,128)S(1)} %slice.3), channel_id=1, source_target_pairs={{0,8},{1,9},{2,10},{3,11},{4,12},{5,13},{6,14},{7,15},{8,0},{9,1},... | collective-permute-start | bytes 24584 | tf_op jit(solution)/shard_map/ppermute | solution.py:25
  12.7 2.0 %prepare.1 = (s32[32,128]{1,0:T(8,128)S(1)}, bf16[256,256]{1,0:T(8,128)(2,1)S(1)}, bf16[1024,256]{1,0:T(8,128)(2,1)S(1)}, bf16[768,128]{1,0:T(8,128)(2,1)S(1)}, ...) custom-call(s32[2,32,128]{2,1,0:T(8,128)} %refs_0_.1, ...), custom_call_target="tpu_custom_call" | custom-call | tf_op jit(solution)/shard_map/prepare/pallas_call | solution.py:163
  14.7 4.6 %all-to-all-done.block = bf16[16,64,128]{2,1,0:T(8,128)(2,1)S(1)} async-done(((bf16[16,64,128]{2,1,0:T(8,128)(2,1)}), bf16[16,64,128]{2,1,0:T(8,128)(2,1)S(1)}, u32[]{:S(2)}, u32[]{:S(2)}) %all-to-all-start) | async-done | bytes 262176 | tf_op jit(solution)/shard_map/all_to_all | solution.py:626
  19.3 0.8 %remap_own.1 = (bf16[1024,128]{1,0:T(8,128)(2,1)S(1)}, f32[64,128]{1,0:T(8,128)S(1)}, f32[64,128]{1,0:T(8,128)S(1)}, f32[256,128]{1,0:T(8,128)S(1)}) custom-call(bf16[16,64,128]{2,1,0:T(8,128)(2,1)S(1)} %all-to-all-done.block, s32[32,128]{1,0:T(8,128)S(1)} %get-tuple-element.27.places), custom_call_target="tpu_custom_call" | custom-call | tf_op jit(solution)/shard_map/remap_own/pallas_call | solution.py:225
  20.1 0.0 collective-permute-done.polar
  20.1 0.5 %remap_polar.1 = (bf16[256,128]{1,0:T(8,128)(2,1)S(1)}, bf16[80,128]{1,0:T(8,128)(2,1)S(1)}, bf16[80,128]{1,0:T(8,128)(2,1)S(1)}) custom-call(bf16[16,64,128]{2,1,0:T(8,128)(2,1)S(1)} %all-to-all-done.block, s32[2,8,128]{2,1,0:T(8,128)S(1)} %collective-permute-done.polar, f32[64,128]{1,0:T(8,128)S(1)} %get-tuple-element.29.begin, ...), custom_call_target="tpu_custom_call" | custom-call | tf_op jit(solution)/shard_map/remap_polar/pallas_call | solution.py:257
  20.6 0.1 collective-permute-start.1
  20.7 1.8 %collective-permute-start.2 = (bf16[80,128]{1,0:T(8,128)(2,1)S(1)}, bf16[80,128]{1,0:T(8,128)(2,1)S(1)}, u32[]{:S(2)}, u32[]{:S(2)}) collective-permute-start(bf16[80,128]{1,0:T(8,128)(2,1)S(1)} %get-tuple-element.33), channel_id=1, source_target_pairs={{1,2},{3,4},{5,6},{7,8},{9,10},{11,12},{13,14},{15,0},{2,1},{4,3},... | collective-permute-start | bytes 61448 | tf_op jit(solution)/shard_map/ppermute | solution.py:20
  22.5 4.3 %inside.1 = (f32[256,128]{1,0:T(8,128)S(1)}, f32[23,256]{1,0:T(8,128)S(1)}, f32[23,256]{1,0:T(8,128)S(1)}, f32[23,128]{1,0:T(8,128)S(1)}, f32[23,128]{1,0:T(8,12...) custom-call(bf16[1024,128]{1,0:T(8,128)(2,1)S(1)} %get-tuple-element.28.cells, ...), custom_call_target="tpu_custom_call" | custom-call | flops 4000000000 | bytes 4000000 | tf_op jit(solution)/shard_map/inside/pallas_call | solution.py:590
  26.8 0.0 collective-permute-done.1.inner
  26.8 0.0 collective-permute-done.2.outer
  26.8 2.6 %edges.1 = f32[8,32,128]{2,1,0:T(8,128)} custom-call(bf16[1024,128]{1,0:T(8,128)(2,1)S(1)} %get-tuple-element.28.cells, bf16[256,128]{1,0:T(8,128)(2,1)S(1)} %get-tuple-element.31.polar_cells, bf16[80,128]{1,0:T(8,128)(2,1)S(1)} %collective-permute-done.1.inner, bf16[80,128]{1,0:T(8,128)(2,1)S(1)} %collective-permute-done.2.outer, ...), custom_call_target="tpu_custom_call" | custom-call | tf_op jit(solution)/shard_map/edges/pallas_call | solution.py:602
Async XLA Ops:
  1.7 17.5 %all-to-all-start = ((bf16[16,64,128]{2,1,0:T(8,128)(2,1)}), bf16[16,64,128]{2,1,0:T(8,128)(2,1)S(1)}, u32[]{:S(2)}, u32[]{:S(2)}) async-start(bf16[16,64,128]{2,1,0:T(8,128)(2,1)} %bitcast.3), calls=%async_computation | async-start | bytes 524288 | tf_op jit(solution)/shard_map/all_to_all | solution.py:626
  9.8 10.3 %collective-permute-start = (s32[2,8,128]{2,1,0:T(8,128)S(1)}, s32[2,8,128]{2,1,0:T(8,128)S(1)}, u32[]{:S(2)}, u32[]{:S(2)}) collective-permute-start(s32[2,8,128]{2,1,0:T(8,128)S(1)} %slice.3), channel_id=1, source_target_pairs={{0,8},{1,9},{2,10},{3,11},{4,12},{5,13},{6,14},{7,15},{8,0},{9,1},... | collective-permute-start | bytes 24584 | tf_op jit(solution)/shard_map/ppermute | solution.py:25
  20.6 6.2 %collective-permute-start.1 = (bf16[80,128]{1,0:T(8,128)(2,1)S(1)}, bf16[80,128]{1,0:T(8,128)(2,1)S(1)}, u32[]{:S(2)}, u32[]{:S(2)}) collective-permute-start(bf16[80,128]{1,0:T(8,128)(2,1)S(1)} %get-tuple-element.32), channel_id=1, source_target_pairs={{0,1},{2,3},{4,5},{6,7},{8,9},{10,11},{12,13},{14,15},{1,0},{3,2},... | collective-permute-start | bytes 61448 | tf_op jit(solution)/shard_map/ppermute | solution.py:20
  20.7 6.1 %collective-permute-start.2 = (bf16[80,128]{1,0:T(8,128)(2,1)S(1)}, bf16[80,128]{1,0:T(8,128)(2,1)S(1)}, u32[]{:S(2)}, u32[]{:S(2)}) collective-permute-start(bf16[80,128]{1,0:T(8,128)(2,1)S(1)} %get-tuple-element.33), channel_id=1, source_target_pairs={{1,2},{3,4},{5,6},{7,8},{9,10},{11,12},{13,14},{15,0},{2,1},{4,3},... | collective-permute-start | bytes 61448 | tf_op jit(solution)/shard_map/ppermute | solution.py:20

commit v8 on v7

--- a/solution.py
+++ b/solution.py
@@ -246,7 +246,7 @@
         finishes.append(last)
     even = lax.rem(lax.axis_index("lon"), 2) == 0
     begins, finishes = jnp.concatenate(begins, axis=0), jnp.concatenate(finishes, axis=0)
-    inner[...] = jnp.where(even, finishes, begins).astype(BF16)
+    inner[...] = jnp.where(even, finishes, begins)
     outer[...] = jnp.where(even, begins, finishes).astype(BF16)
 
 
@@ -258,7 +258,7 @@
         polar_kernel,
         out_shape=[
             jax.ShapeDtypeStruct((count * columns, columns), BF16),
-            jax.ShapeDtypeStruct((rows, columns), BF16),
+            jax.ShapeDtypeStruct((rows, columns), F32),
             jax.ShapeDtypeStruct((rows, columns), BF16),
         ],
         scratch_shapes=[pltpu.VMEM((devices * depth // 2, columns), F32)],
@@ -299,16 +299,21 @@
     return jnp.dot(values, weights[...], preferred_element_type=F32)
 
 
-def layers(at, groups, pairs, moved, x0, y0, y1, y2, yc, yo, yu, w1, w2, wd, wc, wu):
+def layers(at, groups, pairs, moved, cells_of_row, y0, y1, y2, yc, yo, yu, w1, w2, wd, wc, wu):
     step, top, bottom, pole = at.step, at.top, at.bottom, at.pole
-    x0[at(top), :] = pltpu.roll(x0[at(pole + 1), :], 32, 1)
-    x0[at(pole), :] = pltpu.roll(x0[at(1), :], 32, 1)
     ready = set()
 
     def widen(row):
         if row not in ready:
             ready.add(row)
-            x = x0[at(row), :]
+            if row == top:
+                x = pltpu.roll(cells_of_row(pole + 1), 32, 1)
+            elif row == pole:
+                x = pltpu.roll(cells_of_row(1), 32, 1)
+            elif row == bottom or row == at.count - 1:
+                x = jnp.zeros((step, 128), F32)
+            else:
+                x = cells_of_row(row)
             side = jnp.where(at.mask(1, 16), moved("x0", row, 1, x, -1), moved("x0", row, 1, x, 1))
             y0[at(row), :] = jnp.where(at.mask(1, 64), x, side)
 
@@ -459,13 +464,11 @@
                     ref[row + i : row + i + 1, :] = values[i * half + column : i * half + column + 1, :]
         return ring(values, half, shift)
 
-    x0 = scratch[0]
-    for row in (at.top, at.bottom, at.pole, at.count - 1):
-        x0[at(row), :] = jnp.zeros((half, 128), F32)
-    for i in range(blocks + POLAR):
-        own, n = (cells, i) if i < blocks else (polar_cells, i - blocks)
-        x0[at(at.of(i)), :] = own[n * half : (n + 1) * half, :].astype(F32)
-    stages = layers(at, groups, pairs, moved, *scratch, w1, w2, wd, wc, wu)
+    def cells_of_row(row):
+        own, n = (cells, row - 1) if row <= blocks else (polar_cells, row - at.pole - 1)
+        return own[n * half : (n + 1) * half, :].astype(F32)
+
+    stages = layers(at, groups, pairs, moved, cells_of_row, *scratch[1:], w1, w2, wd, wc, wu)
 
     y2, yu = scratch[3], scratch[6]
     lane = lax.broadcasted_iota(jnp.int32, (8, 2 * half), 1)
@@ -505,11 +508,9 @@
     at = Rows(step, blocks)
     place = lax.broadcasted_iota(jnp.int32, (step, 128), 0)
     x0 = scratch[0]
-    near, far = inner[...].astype(F32), outer[...].astype(F32)
+    near, far = inner[...], outer[...].astype(F32)
     left, right = jnp.where(even, far, near), jnp.where(even, near, far)
     beside = {}
-    for row in (at.top, at.bottom, at.pole, at.count - 1):
-        x0[at(row), :] = jnp.zeros((step, 128), F32)
     for i in range(blocks + POLAR):
         row = at.of(i)
         own, n = (cells, i) if i < blocks else (polar_cells, i - blocks)
@@ -554,7 +555,7 @@
 
         return lambda: merge(at, row, count, scratch[3], scratch[6], wm), finish, [(row, count)]
 
-    stages = layers(at, groups, pairs, moved, *scratch, w1, w2, wd, wc, wu)
+    stages = layers(at, groups, pairs, moved, lambda row: x0[at(row), :], *scratch[1:], w1, w2, wd, wc, wu)
     run(at, stages + [[last(1, blocks // 2), last(1 + blocks // 2, blocks // 2)]], 1)
     found = jnp.concatenate(parts, axis=1)
 

time: 29.7 us -> 29.6 us (level)
  starting transfers between devices: 12.1 us -> 11.8 us
where the time goes in v8:
time: 29.6 us; the launch traced here: 29.2 us
  Pallas kernels  12 us (41%)
  starting transfers between devices  11.8 us (40%)
  waiting for transfers between devices  4.64 us (16%)
  local copies, waits for them, and re-layouts  0.7 us (2%)
    all_to_all x1, starting transfers between devices, shards(): lax.all_to_all(parcels, 'lon', split_axis=0, concat_axis=0, tiled=True)  7.4 us
    all_to_all x1, waiting for transfers between devices, shards(): lax.all_to_all(parcels, 'lon', split_axis=0, concat_axis=0, tiled=True)  4.59 us
    pallas_call x1, Pallas kernels, inside(): pl.pallas_call(inside_kernel, out_shape=[jax.ShapeDtypeStruct((blocks * 1...  4.29 us
    ppermute x1, starting transfers between devices, opposite(): lax.ppermute(block, axis, [(i, (i + devices // 2) % devices) for i in ran...  2.83 us
    pallas_call x1, Pallas kernels, edges(): pl.pallas_call(edges_kernel, out_shape=jax.ShapeDtypeStruct(out_shape, F3...  2.64 us
    pallas_call x1, Pallas kernels, prepare(): pl.pallas_call(prepare_kernel, in_specs=[pl.BlockSpec(memory_space=pltpu....  2.01 us
    pallas_call x1, Pallas kernels, pack(): pl.pallas_call(pack_kernel, in_specs=[pl.BlockSpec(memory_space=pltpu.HBM...  1.73 us
    ppermute x2, starting transfers between devices, swap(): return lax.ppermute(block, axis, pairs + [(b, a) for a, b in pairs])  1.63 us
  transfers between devices with their start and end apart: 4, of which 1 were waited for; matrix products, arithmetic and copies ran while one was open for 2% of the time, Pallas kernels for 24%

profile of v8, /device:TPU:0, one launch (start us, length us, event | category | flops | bytes accessed | tf_op | source)
XLA Modules:
  0.0 29.2 jit_solution(227172659070235561)
XLA Ops:
  0.0 1.7 %pack.1 = bf16[16,32,2,128]{3,2,1,0:T(2,128)(2,1)} custom-call(bf16[16,2,2048]{2,1,0:T(2,128)(2,1)} %fields_hbm.1), custom_call_target="tpu_custom_call" | custom-call | tf_op jit(solution)/shard_map/pack/pallas_call | solution.py:51
  1.7 7.4 %all-to-all-start = ((bf16[16,64,128]{2,1,0:T(8,128)(2,1)}), bf16[16,64,128]{2,1,0:T(8,128)(2,1)S(1)}, u32[]{:S(2)}, u32[]{:S(2)}) async-start(bf16[16,64,128]{2,1,0:T(8,128)(2,1)} %bitcast.3), calls=%async_computation | async-start | bytes 524288 | tf_op jit(solution)/shard_map/all_to_all | solution.py:627
  9.1 0.7 %slice.3 = s32[2,8,128]{2,1,0:T(8,128)S(1)} slice(s32[2,32,128]{2,1,0:T(8,128)} %refs_0_.1), slice={[0:2], [0:8], [0:128]} | slice | bytes 16384 | tf_op jit(solution)/shard_map/slice | solution.py:625
  9.8 2.8 %collective-permute-start = (s32[2,8,128]{2,1,0:T(8,128)S(1)}, s32[2,8,128]{2,1,0:T(8,128)S(1)}, u32[]{:S(2)}, u32[]{:S(2)}) collective-permute-start(s32[2,8,128]{2,1,0:T(8,128)S(1)} %slice.3), channel_id=1, source_target_pairs={{0,8},{1,9},{2,10},{3,11},{4,12},{5,13},{6,14},{7,15},{8,0},{9,1},... | collective-permute-start | bytes 24584 | tf_op jit(solution)/shard_map/ppermute | solution.py:25
  12.7 2.0 %prepare.1 = (s32[32,128]{1,0:T(8,128)S(1)}, bf16[256,256]{1,0:T(8,128)(2,1)S(1)}, bf16[1024,256]{1,0:T(8,128)(2,1)S(1)}, bf16[768,128]{1,0:T(8,128)(2,1)S(1)}, ...) custom-call(s32[2,32,128]{2,1,0:T(8,128)} %refs_0_.1, ...), custom_call_target="tpu_custom_call" | custom-call | tf_op jit(solution)/shard_map/prepare/pallas_call | solution.py:163
  14.7 4.6 %all-to-all-done.block = bf16[16,64,128]{2,1,0:T(8,128)(2,1)S(1)} async-done(((bf16[16,64,128]{2,1,0:T(8,128)(2,1)}), bf16[16,64,128]{2,1,0:T(8,128)(2,1)S(1)}, u32[]{:S(2)}, u32[]{:S(2)}) %all-to-all-start) | async-done | bytes 262176 | tf_op jit(solution)/shard_map/all_to_all | solution.py:627
  19.3 0.8 %remap_own.1 = (bf16[1024,128]{1,0:T(8,128)(2,1)S(1)}, f32[64,128]{1,0:T(8,128)S(1)}, f32[64,128]{1,0:T(8,128)S(1)}, f32[256,128]{1,0:T(8,128)S(1)}) custom-call(bf16[16,64,128]{2,1,0:T(8,128)(2,1)S(1)} %all-to-all-done.block, s32[32,128]{1,0:T(8,128)S(1)} %get-tuple-element.27.places), custom_call_target="tpu_custom_call" | custom-call | tf_op jit(solution)/shard_map/remap_own/pallas_call | solution.py:225
  20.1 0.0 collective-permute-done.polar
  20.1 0.5 %remap_polar.1 = (bf16[256,128]{1,0:T(8,128)(2,1)S(1)}, f32[80,128]{1,0:T(8,128)S(1)}, bf16[80,128]{1,0:T(8,128)(2,1)S(1)}) custom-call(bf16[16,64,128]{2,1,0:T(8,128)(2,1)S(1)} %all-to-all-done.block, s32[2,8,128]{2,1,0:T(8,128)S(1)} %collective-permute-done.polar, f32[64,128]{1,0:T(8,128)S(1)} %get-tuple-element.29.begin, ...), custom_call_target="tpu_custom_call" | custom-call | tf_op jit(solution)/shard_map/remap_polar/pallas_call | solution.py:257
  20.6 1.6 %collective-permute-start.2 = (bf16[80,128]{1,0:T(8,128)(2,1)S(1)}, bf16[80,128]{1,0:T(8,128)(2,1)S(1)}, u32[]{:S(2)}, u32[]{:S(2)}) collective-permute-start(bf16[80,128]{1,0:T(8,128)(2,1)S(1)} %get-tuple-element.33), channel_id=1, source_target_pairs={{1,2},{3,4},{5,6},{7,8},{9,10},{11,12},{13,14},{15,0},{2,1},{4,3},... | collective-permute-start | bytes 61448 | tf_op jit(solution)/shard_map/ppermute | solution.py:20
  22.2 0.0 collective-permute-start.1
  22.2 4.3 %inside.1 = (f32[256,128]{1,0:T(8,128)S(1)}, f32[23,256]{1,0:T(8,128)S(1)}, f32[23,256]{1,0:T(8,128)S(1)}, f32[23,128]{1,0:T(8,128)S(1)}, f32[23,128]{1,0:T(8,12...) custom-call(bf16[1024,128]{1,0:T(8,128)(2,1)S(1)} %get-tuple-element.28.cells, ...), custom_call_target="tpu_custom_call" | custom-call | flops 4000000000 | bytes 4000000 | tf_op jit(solution)/shard_map/inside/pallas_call | solution.py:591
  26.5 0.0 collective-permute-done.2.outer
  26.6 0.0 collective-permute-done.1.inner
  26.6 2.6 %edges.1 = f32[8,32,128]{2,1,0:T(8,128)} custom-call(bf16[1024,128]{1,0:T(8,128)(2,1)S(1)} %get-tuple-element.28.cells, bf16[256,128]{1,0:T(8,128)(2,1)S(1)} %get-tuple-element.31.polar_cells, f32[80,128]{1,0:T(8,128)S(1)} %collective-permute-done.1.inner, bf16[80,128]{1,0:T(8,128)(2,1)S(1)} %collective-permute-done.2.outer, ...), custom_call_target="tpu_custom_call" | custom-call | tf_op jit(solution)/shard_map/edges/pallas_call | solution.py:603
Async XLA Ops:
  1.7 17.5 %all-to-all-start = ((bf16[16,64,128]{2,1,0:T(8,128)(2,1)}), bf16[16,64,128]{2,1,0:T(8,128)(2,1)S(1)}, u32[]{:S(2)}, u32[]{:S(2)}) async-start(bf16[16,64,128]{2,1,0:T(8,128)(2,1)} %bitcast.3), calls=%async_computation | async-start | bytes 524288 | tf_op jit(solution)/shard_map/all_to_all | solution.py:627
  9.8 10.3 %collective-permute-start = (s32[2,8,128]{2,1,0:T(8,128)S(1)}, s32[2,8,128]{2,1,0:T(8,128)S(1)}, u32[]{:S(2)}, u32[]{:S(2)}) collective-permute-start(s32[2,8,128]{2,1,0:T(8,128)S(1)} %slice.3), channel_id=1, source_target_pairs={{0,8},{1,9},{2,10},{3,11},{4,12},{5,13},{6,14},{7,15},{8,0},{9,1},... | collective-permute-start | bytes 24584 | tf_op jit(solution)/shard_map/ppermute | solution.py:25
  20.6 6.0 %collective-permute-start.2 = (bf16[80,128]{1,0:T(8,128)(2,1)S(1)}, bf16[80,128]{1,0:T(8,128)(2,1)S(1)}, u32[]{:S(2)}, u32[]{:S(2)}) collective-permute-start(bf16[80,128]{1,0:T(8,128)(2,1)S(1)} %get-tuple-element.33), channel_id=1, source_target_pairs={{1,2},{3,4},{5,6},{7,8},{9,10},{11,12},{13,14},{15,0},{2,1},{4,3},... | collective-permute-start | bytes 61448 | tf_op jit(solution)/shard_map/ppermute | solution.py:20
  22.2 4.3 %collective-permute-start.1 = (f32[80,128]{1,0:T(8,128)S(1)}, f32[80,128]{1,0:T(8,128)S(1)}, u32[]{:S(2)}, u32[]{:S(2)}) collective-permute-start(f32[80,128]{1,0:T(8,128)S(1)} %get-tuple-element.32), channel_id=1, source_target_pairs={{0,1},{2,3},{4,5},{6,7},{8,9},{10,11},{12,13},{14,15},{1,0},{3,2},... | collective-permute-start | bytes 122888 | tf_op jit(solution)/shard_map/ppermute | solution.py:20
